TPU v7x, 32 devices: a whole 2x2x4 slice. The times are simulated.
32 devices in a mesh: row: 8 (over z, x), blk: 4 (over y, core).
Axes of the slice: x: 2, y: 2, z: 4, core: 2. Of those that a mesh axis runs over, the one named last changes fastest.
Arguments:
- source_table: bfloat16 [2048, 512], P('blk'), may hold values from -6 to 6
- target_table: bfloat16 [16384, 512], P(('row', 'blk')), may hold values from -6 to 6
- message_weight: bfloat16 [512, 512], replicated, may hold values from -0.25 to 0.25
- self_weight: bfloat16 [512, 512], replicated, may hold values from -0.25 to 0.25
- tile_lists: int32 [32, 4], P(('row', 'blk')), may hold values from 0 to 3, each once within a row
- key_offsets: int32 [16384, 4], P(('row', 'blk')), may hold values from 0 to 511
- list_lengths: int32 [32], P(('row', 'blk')), may hold values from 1 to 4, 64 in all
- cotangent: bfloat16 [16384, 512], P(('row', 'blk')), may hold values from -6 to 6
Outputs:
- updated: bfloat16 [16384, 512], P(('row', 'blk'))
- target_gradient: bfloat16 [16384, 512], P(('row', 'blk'))
- source_gradient: bfloat16 [2048, 512], P(('blk', 'row'))
- self_gradient: float32 [512, 512], replicated
- message_gradient: float32 [512, 512], replicated
Inputs may be any that keep to these rules, and one draw needn't show every extreme that they name: Each row of tile_lists names every one of the 4 source tiles once. A target tile uses the first list_lengths entries of its row of tile_lists.
All inputs are finite; a program needn't handle non-finite values. No bound on the sum of `list_lengths` on one device may be relied on, other than what follows from the above.
Results may differ from a plain program's by a relative error of at most 0.0058.
Values may be sent and summed in bfloat16 or wider, within the bound.
No kernel may reach another device: no remote copies, remote signals or barrier semaphores. Data moves between devices by JAX's collectives and lax.ppermute only.
A program may use at most 64 MiB of HBM per device.

v0:
```python
import jax
import jax.numpy as jnp
from jax import lax
from jax.sharding import PartitionSpec as P


def slot_table(lists):
    slot_count = lists.shape[1]
    slot_ids = lax.iota(jnp.int32, slot_count)
    matches = lists[:, :, None] == slot_ids[None, None, :]
    return jnp.sum(jnp.where(matches, slot_ids[None, :, None], 0), axis=1)


def tile_patterns(offset_tiles, slot_column, lengths, tile_rows):
    slot_count = offset_tiles.shape[2]
    chosen_slot = lax.iota(jnp.int32, slot_count)[None, None, :] == slot_column[:, None, None]
    chosen = jnp.sum(jnp.where(chosen_slot, offset_tiles, 0), axis=2)
    used = slot_column < lengths
    positions = lax.iota(jnp.int32, tile_rows)
    pattern = (chosen[:, :, None] == positions[None, None, :]) & used[:, None, None]
    return pattern.astype(jnp.bfloat16)


def local(
    source_table,
    target_table,
    message_weight,
    self_weight,
    tile_lists,
    key_offsets,
    list_lengths,
    cotangent,
):
    tile_rows = target_table.shape[0] // tile_lists.shape[0]
    tiles_here = tile_lists.shape[0]
    slot_count = tile_lists.shape[1]
    width = target_table.shape[1]
    block_rows = source_table.shape[0]
    row_devices = lax.axis_size("row")
    share_rows = block_rows // row_devices
    own_rows = lax.dynamic_slice_in_dim(
        source_table, lax.axis_index("row") * share_rows, share_rows, 0
    )
    projected = jnp.dot(source_table, message_weight, preferred_element_type=jnp.float32).astype(
        jnp.bfloat16
    )
    inverse_tile = 1.0 / list_lengths.astype(jnp.float32)
    slot_of = slot_table(tile_lists)
    offset_tiles = key_offsets.reshape(tiles_here, tile_rows, slot_count)
    start_sum = jnp.zeros((target_table.shape[0], width), jnp.float32)
    pieces = lax.all_gather(projected, "blk", axis=0, tiled=True)
    piece_tiles = pieces.shape[0] // tile_rows

    def gather_visit(local_tile, running):
        source_tile = lax.dynamic_slice_in_dim(pieces, local_tile * tile_rows, tile_rows, 0)
        slot_column = lax.dynamic_index_in_dim(slot_of, local_tile, 1, keepdims=False)
        pattern = tile_patterns(offset_tiles, slot_column, list_lengths, tile_rows)
        added = jnp.einsum("trc,cw->trw", pattern, source_tile, preferred_element_type=jnp.float32)
        return running + added.reshape(running.shape)

    gathered = lax.fori_loop(0, piece_tiles, gather_visit, start_sum)
    inverse_row = jnp.repeat(inverse_tile, tile_rows)[:, None]
    preact = (
        jnp.dot(target_table, self_weight, preferred_element_type=jnp.float32)
        + gathered * inverse_row
    )
    sigmoid_pre = jax.nn.sigmoid(preact)
    updated = (target_table.astype(jnp.float32) + preact * sigmoid_pre).astype(jnp.bfloat16)
    upstream = cotangent.astype(jnp.float32)
    grad_pre = (upstream * sigmoid_pre * (1.0 + preact * (1.0 - sigmoid_pre))).astype(jnp.bfloat16)
    target_gradient = (
        upstream + jnp.dot(grad_pre, self_weight.T, preferred_element_type=jnp.float32)
    ).astype(jnp.bfloat16)
    grad_tiles = grad_pre.reshape(tiles_here, tile_rows, width)

    def tile_terms(slot_column, offsets, lengths, inverses, grads):
        pattern = tile_patterns(offsets, slot_column, lengths, tile_rows)
        terms = jnp.einsum("trc,trw->tcw", pattern, grads, preferred_element_type=jnp.float32)
        return jnp.sum(terms * inverses[:, None, None], axis=0)

    def partial_visit(local_tile, running):
        slot_column = lax.dynamic_index_in_dim(slot_of, local_tile, 1, keepdims=False)
        term = tile_terms(slot_column, offset_tiles, list_lengths, inverse_tile, grad_tiles)
        return lax.dynamic_update_slice_in_dim(running, term, local_tile * tile_rows, 0)

    block_sum = lax.psum_scatter(
        lax.fori_loop(
            0,
            block_rows * lax.axis_size("blk") // tile_rows,
            partial_visit,
            jnp.zeros((block_rows * lax.axis_size("blk"), width), jnp.float32),
        ),
        "blk",
        scatter_dimension=0,
        tiled=True,
    )
    source_sum = lax.psum_scatter(block_sum, "row", scatter_dimension=0, tiled=True)
    source_grad_rounded = source_sum.astype(jnp.bfloat16)
    source_gradient = jnp.dot(
        source_grad_rounded, message_weight.T, preferred_element_type=jnp.float32
    ).astype(jnp.bfloat16)
    self_partial = jnp.dot(target_table.T, grad_pre, preferred_element_type=jnp.float32)
    message_partial = jnp.dot(own_rows.T, source_grad_rounded, preferred_element_type=jnp.float32)
    self_total, message_total = lax.psum((self_partial, message_partial), ("row", "blk"))
    target_total = target_table.shape[0] * row_devices * lax.axis_size("blk")
    source_total = block_rows * lax.axis_size("blk")
    self_gradient = self_total * target_total ** (-0.5)
    message_gradient = message_total * source_total ** (-0.5)
    return (updated, target_gradient, source_gradient, self_gradient, message_gradient)


def solution(mesh):
    placed = (
        P("blk", None),
        P(("row", "blk"), None),
        P(),
        P(),
        P(("row", "blk"), None),
        P(("row", "blk"), None),
        P(("row", "blk")),
        P(("row", "blk"), None),
    )
    return jax.shard_map(
        local,
        mesh=mesh,
        in_specs=placed,
        out_specs=(
            P(("row", "blk"), None),
            P(("row", "blk"), None),
            P(("blk", "row"), None),
            P(),
            P(),
        ),
        check_vma=False,
    )
```

profile of v0, /device:TPU:0, one launch (start us, length us, event | category | flops | bytes accessed | tf_op | source)
XLA Modules:
  0.0 337.7 jit_solution(10654011447682155521)
XLA Ops:
  7.2 2.5 convolution_convert_fusion
  10.5 0.7 select_reduce_fusion.2
  11.2 24.3 %all-gather.2.cloned.1.call-done = bf16[2048,512]{1,0:T(8,128)(2,1)} async-done(((bf16[512,512]{1,0:T(8,128)(2,1)}), bf16[2048,512]{1,0:T(8,128)(2,1)}) %all-gather.2.cloned.1.call-update) | async-done | bytes 2097168 | tf_op jit(solution)/shard_map/all_gather | solution.py:51
  35.5 19.9 %while.28 = (s32[]{:T(128)}, f32[512,512]{1,0:T(8,128)S(1)}, s32[1,4]{1,0:T(1,128)S(1)}, s32[1,512,4]{1,2,0:T(4,128)}, s32[1]{0:T(128)}, /*index=5*/bf16[2048,51...) while((s32[]{:T(128)}, f32[512,512]{1,0:T(8,128)S(1)}, s32[1,4]{1,0:T(1,128)S(1)}, ...), condition=%wide.region_3.4_spmd.clone, body=%wide.region_1.3_spmd.clone.sunk | while | flops 269487616 | bytes 2634434 | solution.py:61
  36.1 0.6 iota_compare_fusion.8
  36.7 0.8 select_reduce_fusion.6
  38.8 1.6 convolution_add_fusion.4
  41.7 0.8 select_reduce_fusion.6
  43.8 1.6 convolution_add_fusion.4
  46.0 0.6 iota_compare_fusion.8
  46.7 0.8 select_reduce_fusion.6
  48.8 1.6 convolution_add_fusion.4
  51.7 0.8 select_reduce_fusion.6
  53.7 1.6 convolution_add_fusion.4
  55.4 1.7 fusion.15
  57.1 2.5 broadcast_in_dim.94
  59.6 16.8 %while.27 = (s32[]{:T(128)}, f32[2048,512]{1,0:T(8,128)}, s32[1,4]{1,0:T(1,128)S(1)}, s32[1,512,4]{1,2,0:T(4,128)S(1)}, s32[1]{0:T(128)}, /*index=5*/bf16[1,512,...) while((s32[]{:T(128)}, f32[2048,512]{1,0:T(8,128)}, ...), condition=%wide.region_6.7_spmd, body=%wide.region_4.6_spmd.sunk | while | flops 269225472 | bytes 1586368 | solution.py:87
  62.2 1.5 fusion.37
  66.4 1.6 fusion.37
  68.6 0.6 iota_compare_fusion.7
  70.6 1.6 fusion.37
  74.8 1.6 fusion.37
  76.5 44.6 %reduce-scatter.3.cloned.1.call-done = f32[512,512]{1,0:T(8,128)} async-done(((f32[2048,512]{1,0:T(8,128)}), f32[512,512]{1,0:T(8,128)}) %reduce-scatter.3.cloned.1.call-update) | async-done | bytes 1048592 | tf_op jit(solution)/shard_map/reduce_scatter | solution.py:86
  121.2 1.4 convolution_bitcast_fusion
  122.6 65.7 %reduce-scatter.5.cloned.1.call-done = f32[64,512]{1,0:T(8,128)} async-done(((f32[512,512]{1,0:T(8,128)}), f32[64,512]{1,0:T(8,128)}) %reduce-scatter.5.cloned.1.call-update) | async-done | bytes 131088 | tf_op jit(solution)/shard_map/reduce_scatter | solution.py:97
  188.3 2.3 fusion.16
  190.6 1.3 fusion.13
  191.8 0.9 convolution_convert_fusion.1
  192.8 134.6 %all-reduce.3.cloned.1.call-done = (f32[512,512]{0,1:T(8,128)}, f32[512,512]{1,0:T(8,128)}) async-done(((f32[512,512]{0,1:T(8,128)}, f32[512,512]{1,0:T(8,128)}), (f32[512,512]{0,1:T(8,128)}, f32[512,512]{1,0:T(8,128)})) %all-reduce.3.cloned.1.call-update) | async-done | bytes 2097168 | tf_op jit(solution)/shard_map/psum | solution.py:104
  327.3 1.4 broadcast_multiply_fusion.1
  328.7 1.3 copy.15
  330.0 1.1 broadcast_multiply_fusion
  (40 shorter events, 8.5 us)
Async XLA Ops:
  7.2 48.2 %copy-start = (bf16[512,512]{1,0:T(8,128)(2,1)S(1)}, bf16[512,512]{1,0:T(8,128)(2,1)}, u32[]{:S(2)}) copy-start(bf16[512,512]{1,0:T(8,128)(2,1)} %param.15) | copy-start | bytes 1572868
  7.2 28.3 %all-gather.2.cloned.1.call-start = ((), (), s32[]{:S(2)}) async-start(), calls=%async_computation.2 | async-start | bytes 2621440 | tf_op jit(solution)/shard_map/all_gather | solution.py:51
  9.7 111.3 %reduce-scatter.3.cloned.1.call-start = ((), (), s32[]{:S(2)}) async-start(), calls=%async_computation.3 | async-start | bytes 5242880 | tf_op jit(solution)/shard_map/reduce_scatter | solution.py:86
  35.5 19.9 %copy-start.5 = (bf16[512,512]{1,0:T(8,128)(2,1)S(1)}, bf16[512,512]{1,0:T(8,128)(2,1)}, u32[]{:S(2)}) copy-start(bf16[512,512]{1,0:T(8,128)(2,1)} %param.13) | copy-start | bytes 1572868
  35.5 19.9 %copy-start.6 = (bf16[512,512]{1,0:T(8,128)(2,1)S(1)}, bf16[512,512]{1,0:T(8,128)(2,1)}, u32[]{:S(2)}) copy-start(bf16[512,512]{1,0:T(8,128)(2,1)} %param.19) | copy-start | bytes 1572868
  55.4 4.2 %copy-start.3 = (s32[1,512,4]{1,2,0:T(4,128)S(1)}, s32[1,512,4]{1,2,0:T(4,128)}, u32[]{:S(2)}) copy-start(s32[1,512,4]{1,2,0:T(4,128)} %get-tuple-element.471) | copy-start | bytes 24580
  76.4 111.9 %reduce-scatter.5.cloned.1.call-start = ((), (), s32[]{:S(2)}) async-start(), calls=%async_computation.4 | async-start | bytes 1179648 | tf_op jit(solution)/shard_map/reduce_scatter | solution.py:97
  121.1 70.8 %copy-start.1 = (bf16[512,512]{1,0:T(8,128)(2,1)S(1)}, bf16[512,512]{1,0:T(8,128)(2,1)}, u32[]{:S(2)}) copy-start(bf16[512,512]{1,0:T(8,128)(2,1)} %param.14) | copy-start | bytes 1572868
  121.1 206.2 %all-reduce.3.cloned.1.call-start = ((), (), s32[]{:S(2)}) async-start(), calls=%async_computation.5 | async-start | bytes 4194304 | tf_op jit(solution)/shard_map/psum | solution.py:104
  188.3 3.6 %copy-start.4 = (f32[64,512]{1,0:T(8,128)S(1)}, f32[64,512]{1,0:T(8,128)}, u32[]{:S(2)}) copy-start(f32[64,512]{1,0:T(8,128)} %reduce-scatter.5.cloned.1.call-done) | copy-start | bytes 393220
  327.3 2.7 copy-start.2
Sparse Core Ops, SparseCore 0:
  10.1 25.2 all-gather.1
  76.5 44.4 reduce-scatter.2
  124.9 63.3 reduce-scatter.4
  194.2 133.0 all-reduce.2
where the time goes:
time: 338 us
  waiting for transfers between devices  269 us (80%)
  matrix products  22.8 us (7%)
  between operations  14.5 us (4%)
  other arithmetic  11.9 us (4%)
  loops' own time  10.6 us (3%)
  local copies, waits for them, and re-layouts  8.48 us (3%)
    psum x1, waiting for transfers between devices, local(): lax.psum((self_partial, message_partial), ('row', 'blk'))  135 us
    reduce_scatter x1, waiting for transfers between devices, local(): lax.psum_scatter(block_sum, 'row', scatter_dimension=0, tiled=True)  65.7 us
    reduce_scatter x1, waiting for transfers between devices, local(): lax.psum_scatter(lax.fori_loop(0, block_rows * lax.axis_size('blk') // ti...  44.6 us
    all_gather x1, waiting for transfers between devices, local(): pieces = lax.all_gather(projected, 'blk', axis=0, tiled=True)  24.3 us
  transfers between devices with their start and end apart: 4, of which 4 were waited for; matrix products, arithmetic and copies ran while one was open for 1% of the time, Pallas kernels for 0%

commit v1 on v0

v1 whole, which is shorter than its diff:
```python
import functools

import jax
import jax.numpy as jnp
from jax import lax
from jax.experimental import pallas as pl
from jax.experimental.pallas import tpu as pltpu
from jax.sharding import PartitionSpec as P

AXES = ("row", "blk")
BF16 = jnp.bfloat16
F32 = jnp.float32
SMEM = pl.BlockSpec(memory_space=pltpu.SMEM)
VMEM = pl.BlockSpec(memory_space=pltpu.VMEM)
VMEM_BYTES = 48 * 1024 * 1024


def swap(value, mask, devices):
    return lax.ppermute(value, AXES, [(i, i ^ mask) for i in range(devices)])


def call(body, name, out_shape, scratch=(), flops=0, moved=0):
    return pl.pallas_call(
        body,
        name=name,
        out_shape=out_shape,
        scratch_shapes=scratch,
        compiler_params=pltpu.CompilerParams(vmem_limit_bytes=VMEM_BYTES),
        cost_estimate=pl.CostEstimate(flops=flops, bytes_accessed=moved, transcendentals=0),
    )


def shaped(shape, dtype):
    return jax.ShapeDtypeStruct(shape, dtype)


def mm(a, b, dims=((1,), (0,))):
    return lax.dot_general(a, b, (dims, ((), ())), preferred_element_type=F32)


def gather_first(links_ref, s0_ref, s1_ref, t_ref, ws_ref, own_ref, h_ref):
    own_ref[...] = mm(t_ref[...], ws_ref[...])
    links = links_ref[...].T
    rows = t_ref.shape[0]
    lanes = lax.broadcasted_iota(jnp.int32, (rows, rows), 1)
    total = None
    for m, s_ref in enumerate((s0_ref, s1_ref)):
        pattern = (links[:, m : m + 1] == lanes).astype(F32).astype(BF16)
        added = mm(pattern, s_ref[...])
        total = added if total is None else total + added
    h_ref[...] = total


def gather_rest(links_ref, h0_ref, *refs):
    s_refs, hb_ref = refs[:-1], refs[-1]
    links = links_ref[...].T
    rows = h0_ref.shape[0]
    lanes = lax.broadcasted_iota(jnp.int32, (rows, rows), 1)
    total = h0_ref[...]
    for m, s_ref in enumerate(s_refs):
        pattern = (links[:, m + 2 : m + 3] == lanes).astype(F32).astype(BF16)
        total = total + mm(pattern, s_ref[...])
    hb_ref[...] = total.astype(BF16)


def activate(length_ref, hb_ref, own_ref, wm_ref, t_ref, cot_ref, updated_ref, grad_ref):
    inverse = 1.0 / jnp.full((1, hb_ref.shape[1]), length_ref[0], jnp.int32).astype(F32)
    preact = own_ref[...] + mm(hb_ref[...], wm_ref[...]) * inverse
    sig = jax.nn.sigmoid(preact)
    updated_ref[...] = (t_ref[...].astype(F32) + preact * sig).astype(BF16)
    grad_ref[...] = (cot_ref[...].astype(F32) * sig * (1.0 + preact * (1.0 - sig))).astype(BF16)


def weight_terms(place_ref, lengths_ref, x0_ref, x1_ref, g0_ref, g1_ref, *refs):
    own_ref, sent_refs, total_ref = refs[0], refs[1:-1], refs[-1]
    core = place_ref[0]
    quad = place_ref[1]
    rows = own_ref.shape[0]
    width = own_ref.shape[1]

    def factor(i):
        length = jnp.where(core == 0, 1, lengths_ref[i])
        return 1.0 / jnp.full((1, width), length, jnp.int32).astype(F32)

    dims = ((0,), (0,))
    total_ref[...] = mm(x0_ref[...], g0_ref[...], dims) * factor(0) + mm(x1_ref[...], g1_ref[...], dims) * factor(1)
    own_ref[...] = total_ref[pl.ds(pl.multiple_of(quad * rows, rows), rows), :]
    for m, ref in enumerate(sent_refs, 1):
        ref[...] = total_ref[pl.ds(pl.multiple_of((quad ^ m) * rows, rows), rows), :].astype(BF16)


def source_terms(share, sides, place_ref, lengths_ref, l0_ref, l1_ref, g0_ref, g1_ref, *refs):
    core = place_ref[0]
    quad = place_ref[1]
    rows, width = refs[0].shape
    targets = g0_ref.shape[0]
    position = lax.broadcasted_iota(jnp.int32, (rows, targets), 0)
    inside = (position // share) * (2 * share) + position % share
    inverses = [1.0 / jnp.full((1, width), lengths_ref[i], jnp.int32).astype(F32) for i in range(2)]
    for m, ref in enumerate(refs):
        to = quad ^ m
        block = (to % sides) * 2 + core
        row_at = inside + (to // sides) * share
        total = None
        for i, (l_ref, g_ref) in enumerate(((l0_ref, g0_ref), (l1_ref, g1_ref))):
            pattern = (l_ref[pl.ds(block, 1), :] == row_at).astype(F32).astype(BF16)
            added = mm(pattern, g_ref[...]) * inverses[i]
            total = added if total is None else total + added
        ref[...] = total.astype(ref.dtype)


def add_up(own_ref, *refs):
    out_ref = refs[-1]
    total = own_ref[...]
    for ref in refs[:-1]:
        total = total + ref[...].astype(F32)
    out_ref[...] = total.astype(BF16)


def add_tree(*refs):
    values = [ref[...].astype(F32) for ref in refs[:-1]]
    while len(values) > 1:
        values = [values[i] + values[i + 1] for i in range(0, len(values), 2)]
    refs[-1][...] = values[0].astype(BF16)


def split_sum(peers, place_ref, own_ref, *refs):
    received, outs, total_ref = refs[:peers], refs[peers:-1], refs[-1]
    layer = place_ref[2]
    rows = outs[0].shape[0]
    total = own_ref[...]
    for ref in received:
        total = total + ref[...].astype(F32)
    total_ref[...] = total
    for m, ref in enumerate(outs):
        at = pl.multiple_of((layer ^ m) * rows, rows)
        ref[...] = total_ref[pl.ds(at, rows), :].astype(ref.dtype)


def finish_source(wm_ref, own_ref, *refs):
    total = own_ref[...]
    for ref in refs[:-1]:
        total = total + ref[...].astype(F32)
    refs[-1][...] = mm(total.astype(BF16), wm_ref[...], ((1,), (1,))).astype(BF16)


def finish_weights(quads, scales, place_ref, *refs):
    mine, theirs, outs = refs[:quads], refs[quads : 2 * quads], refs[2 * quads :]
    core = place_ref[0]
    quad = place_ref[1]
    rows = mine[0].shape[0]

    def write(out_ref, pieces, scale):
        for m, ref in enumerate(pieces):
            at = pl.multiple_of((quad ^ m) * rows, rows)
            out_ref[pl.ds(at, rows), :] = ref[...].astype(F32) * scale

    @pl.when(core == 0)
    def _():
        write(outs[0], mine, scales[0])
        write(outs[1], theirs, scales[1])

    @pl.when(core != 0)
    def _():
        write(outs[0], theirs, scales[0])
        write(outs[1], mine, scales[1])


def local(row_devices, blk_devices, source_table, target_table, message_weight, self_weight, tile_lists, key_offsets, list_lengths, cotangent):
    devices = row_devices * blk_devices
    targets, width = target_table.shape
    block_rows = source_table.shape[0]
    slots = tile_lists.shape[1]
    assert tile_lists.shape[0] == 1 and block_rows == targets and slots == blk_devices
    sides = blk_devices // 2
    quads = blk_devices
    layers = row_devices // 2
    share = block_rows // row_devices

    row_at = lax.axis_index("row")
    blk_at = lax.axis_index("blk")
    core = blk_at % 2
    quad = (row_at % 2) * sides + blk_at // 2
    layer = row_at // 2
    place = jnp.stack([core, quad, layer]).astype(jnp.int32)

    blocks = lax.iota(jnp.int32, blk_devices)
    used = (tile_lists[0][None, :] == blocks[:, None]) & (lax.iota(jnp.int32, slots)[None, :] < list_lengths[0])
    links = jnp.max(jnp.where(used[:, :, None], key_offsets.T[None, :, :], -1), axis=1)
    near = jnp.max(jnp.where((blocks[:, None] ^ blk_at) == blocks[None, :], 1, 0)[:, :, None] * (links[None, :, :] + 1), axis=1) - 1
    near = jnp.pad(near, ((0, -slots % 8), (0, 0)), constant_values=-1)
    links = jnp.pad(links, ((0, -slots % 8), (0, 0)), constant_values=-1)

    held = {0: source_table, 1: swap(source_table, 1, devices)}
    for m in range(2, blk_devices, 2):
        held[m] = swap(source_table, m, devices)
        held[m + 1] = swap(held[m], 1, devices)
    packed = jnp.concatenate([links, jnp.broadcast_to(list_lengths[:, None], (8, targets))], axis=0)
    packed = swap(packed, 1, devices)
    their_links = packed[: links.shape[0]]
    lengths = jnp.stack([list_lengths[0], packed[links.shape[0], 0]])

    square = 2 * targets * width * width
    own_term, gathered = call(
        gather_first, "gather_first", (shaped((targets, width), F32),) * 2, flops=3 * square, moved=5 << 20
    )(near, held[0], held[1], target_table, self_weight)
    gathered = call(gather_rest, "gather_rest", shaped((targets, width), BF16), flops=2 * square, moved=3 << 20)(
        near, gathered, *[held[m] for m in range(2, blk_devices)]
    )
    mine = jnp.where(core == 0, target_table, gathered)
    other = jnp.where(core == 0, gathered, target_table)
    other = swap(other, 1, devices)
    updated, grad_pre = pl.pallas_call(
        activate,
        name="activate",
        in_specs=[SMEM] + [VMEM] * 5,
        out_shape=(shaped((targets, width), BF16),) * 2,
        compiler_params=pltpu.CompilerParams(vmem_limit_bytes=VMEM_BYTES),
        cost_estimate=pl.CostEstimate(flops=square, bytes_accessed=4 << 20, transcendentals=targets * width),
    )(list_lengths, gathered, own_term, message_weight, target_table, cotangent)
    their_grad = swap(grad_pre, 1, devices)

    piece = width // quads
    terms = pl.pallas_call(
        weight_terms,
        name="weight_terms",
        in_specs=[SMEM] * 2 + [VMEM] * 4,
        out_shape=[shaped((piece, width), F32)] + [shaped((piece, width), BF16)] * (quads - 1),
        scratch_shapes=[pltpu.VMEM((width, width), F32)],
        compiler_params=pltpu.CompilerParams(vmem_limit_bytes=VMEM_BYTES),
        cost_estimate=pl.CostEstimate(flops=2 * square, bytes_accessed=3 << 20, transcendentals=0),
    )(place, lengths, mine, other, grad_pre, their_grad)
    received = [swap(terms[m], 2 * m, devices) for m in range(1, quads)]
    part = call(add_up, "weight_sum_square", shaped((piece, width), BF16), moved=1 << 20)(terms[0], *received)

    rows_out = layers * share
    sources = pl.pallas_call(
        functools.partial(source_terms, share, sides),
        name="source_terms",
        in_specs=[SMEM] * 2 + [VMEM] * 4,
        out_shape=[shaped((rows_out, width), F32)] + [shaped((rows_out, width), BF16)] * (quads - 1),
        compiler_params=pltpu.CompilerParams(vmem_limit_bytes=VMEM_BYTES),
        cost_estimate=pl.CostEstimate(flops=4 * square, bytes_accessed=3 << 20, transcendentals=0),
    )(place, lengths, links, their_links, grad_pre, their_grad)
    source_received = [swap(sources[m], 2 * m, devices) for m in range(1, quads)]

    layer_parts = [part] + [swap(part, 2 * quads * m, devices) for m in range(1, layers)]
    total = call(add_tree, "weight_sum_layers", shaped((piece, width), BF16), moved=1 << 20)(*layer_parts)

    source_parts = pl.pallas_call(
        functools.partial(split_sum, quads - 1),
        name="source_sum_square",
        in_specs=[SMEM] + [VMEM] * quads,
        out_shape=[shaped((share, width), F32)] + [shaped((share, width), BF16)] * (layers - 1),
        scratch_shapes=[pltpu.VMEM((rows_out, width), F32)],
        compiler_params=pltpu.CompilerParams(vmem_limit_bytes=VMEM_BYTES),
        cost_estimate=pl.CostEstimate(flops=0, bytes_accessed=2 << 20, transcendentals=0),
    )(place, sources[0], *source_received)
    source_last = [swap(source_parts[m], 2 * quads * m, devices) for m in range(1, layers)]
    source_gradient = call(finish_source, "finish_source", shaped((share, width), BF16), moved=1 << 20)(
        message_weight, source_parts[0], *source_last
    )

    pieces = [total] + [swap(total, 2 * m, devices) for m in range(1, quads)]
    their_pieces = [swap(value, 1, devices) for value in pieces]
    target_total = targets * devices
    source_total = block_rows * blk_devices
    self_gradient, message_gradient = pl.pallas_call(
        functools.partial(finish_weights, quads, (target_total ** (-0.5), source_total ** (-0.5))),
        name="finish_weights",
        in_specs=[SMEM] + [VMEM] * (2 * quads),
        out_shape=(shaped((width, width), F32),) * 2,
        compiler_params=pltpu.CompilerParams(vmem_limit_bytes=VMEM_BYTES),
        cost_estimate=pl.CostEstimate(flops=0, bytes_accessed=3 << 20, transcendentals=0),
    )(place, *pieces, *their_pieces)

    target_gradient = (
        cotangent.astype(F32) + jnp.dot(grad_pre, self_weight.T, preferred_element_type=F32)
    ).astype(BF16)
    return (updated, target_gradient, source_gradient, self_gradient, message_gradient)


def solution(mesh):
    split = P(AXES, None)
    return jax.shard_map(
        functools.partial(local, mesh.shape["row"], mesh.shape["blk"]),
        mesh=mesh,
        in_specs=(P("blk", None), split, P(), P(), split, split, P(AXES), split),
        out_specs=(split, split, P(("blk", "row"), None), P(), P()),
        check_vma=False,
    )
```

time: 338 us -> 76.4 us (0.23)
  waiting for transfers between devices: 269 us -> 29.2 us
  starting transfers between devices: 0.16 us -> 26.9 us
  matrix products: 22.8 us -> 1.27 us
  between operations: 14.5 us -> 1.48 us
  Pallas kernels: 0 us -> 10.6 us
  loops' own time: 10.6 us -> 0 us
  other arithmetic: 11.9 us -> 1.98 us
  local copies, waits for them, and re-layouts: 8.48 us -> 4.65 us
    psum x1 -> x0, waiting for transfers between devices: 135 us -> none  [local(): lax.psum((self_partial, message_partial), ('row', 'blk'))]
    reduce_scatter x2 -> x0, waiting for transfers between devices: 110 us -> none  [the longest x1 65.7 us: local(): lax.psum_scatter(block_sum, 'row', scatter_dimension=0, tiled=True)]
    ppermute x0 -> x25, waiting for transfers between devices: none -> 29.2 us  [swap(): return lax.ppermute(value, AXES, [(i, i ^ mask) for i in range(devices)])]
    ppermute x0 -> x25, starting transfers between devices: none -> 26.9 us  [swap(): return lax.ppermute(value, AXES, [(i, i ^ mask) for i in range(devices)])]
    all_gather x1 -> x0, waiting for transfers between devices: 24.3 us -> none  [local(): pieces = lax.all_gather(projected, 'blk', axis=0, tiled=True)]
    dot_general x14 -> x1, matrix products: 22.8 us -> 1.27 us  [local(): jnp.dot(grad_pre, self_weight.T, preferred_element_type=F32)]
    another operation x2 -> x0, loops' own time: 10.6 us -> none  [the longest x1 5.34 us: local(): gathered = lax.fori_loop(0, piece_tiles, gather_visit, start_sum)]
    pallas_call x0 -> x10, Pallas kernels: none -> 10.6 us  [the longest x1 2.01 us: local(): pl.pallas_call(functools.partial(finish_weights, quads, (target_total **...]
  transfers between devices with their start and end apart: 4 -> 25, of which waited for: 4 -> 8; matrix products, arithmetic and copies ran while one was open for 1% -> 5% of each run, Pallas kernels for 0% -> 6%
where the time goes in v1:
time: 76.4 us; the launch traced here: 76 us
  waiting for transfers between devices  29.2 us (38%)
  starting transfers between devices  26.9 us (35%)
  Pallas kernels  10.6 us (14%)
  local copies, waits for them, and re-layouts  4.65 us (6%)
  other arithmetic  1.98 us (3%)
  between operations  1.48 us (2%)
  matrix products  1.27 us (2%)
    ppermute x25, waiting for transfers between devices, swap(): return lax.ppermute(value, AXES, [(i, i ^ mask) for i in range(devices)])  29.2 us
    ppermute x25, starting transfers between devices, swap(): return lax.ppermute(value, AXES, [(i, i ^ mask) for i in range(devices)])  26.9 us
    unnamed x18, local copies, waits for them, and re-layouts  4.12 us
    pallas_call x1, Pallas kernels, local(): pl.pallas_call(functools.partial(finish_weights, quads, (target_total **...  2.01 us
    pallas_call x1, Pallas kernels, local(): pl.pallas_call(functools.partial(source_terms, share, sides), name='sourc...  1.81 us
    pallas_call x1, Pallas kernels, local(): pl.pallas_call(activate, name='activate', in_specs=[SMEM] + [VMEM] * 5, o...  1.59 us
  transfers between devices with their start and end apart: 25, of which 8 were waited for; matrix products, arithmetic and copies ran while one was open for 5% of the time, Pallas kernels for 6%

profile of v1, /device:TPU:0, one launch (start us, length us, event | category | flops | bytes accessed | tf_op | source)
XLA Modules:
  0.0 76.0 jit_solution(16801418360262707141)
XLA Ops:
  1.1 2.6 %collective-permute-start.1 = (bf16[512,512]{1,0:T(8,128)(2,1)}, bf16[512,512]{1,0:T(8,128)(2,1)S(1)}, u32[]{:S(2)}, u32[]{:S(2)}) collective-permute-start(bf16[512,512]{1,0:T(8,128)(2,1)} %s0_ref.1), channel_id=1, source_target_pairs={{0,2},{1,3},{2,0},{3,1},{4,6},{5,7},{6,4},{7,5},{8,10},{9,11},{10,... | collective-permute-start | bytes 1572872 | tf_op jit(solution)/shard_map/ppermute | solution.py:19
  5.2 11.2 %collective-permute-done.1.refs_0_ = bf16[512,512]{1,0:T(8,128)(2,1)S(1)} collective-permute-done((bf16[512,512]{1,0:T(8,128)(2,1)}, bf16[512,512]{1,0:T(8,128)(2,1)S(1)}, u32[]{:S(2)}, u32[]{:S(2)}) %collective-permute-start.1) | collective-permute-done | bytes 524320 | tf_op jit(solution)/shard_map/ppermute | solution.py:19
  16.7 1.0 %copy-done = bf16[512,512]{1,0:T(8,128)(2,1)S(1)} copy-done((bf16[512,512]{1,0:T(8,128)(2,1)S(1)}, bf16[512,512]{1,0:T(8,128)(2,1)}, u32[]{:S(2)}) %copy-start) | copy-done | bytes 524312
  17.7 1.0 %copy-done.4 = bf16[512,512]{1,0:T(8,128)(2,1)S(1)} copy-done((bf16[512,512]{1,0:T(8,128)(2,1)S(1)}, bf16[512,512]{1,0:T(8,128)(2,1)}, u32[]{:S(2)}) %copy-start.4) | copy-done | bytes 524312
  18.8 1.0 %copy-done.6 = bf16[512,512]{1,0:T(8,128)(2,1)S(1)} copy-done((bf16[512,512]{1,0:T(8,128)(2,1)S(1)}, bf16[512,512]{1,0:T(8,128)(2,1)}, u32[]{:S(2)}) %copy-start.6) | copy-done | bytes 524312
  19.8 1.0 %gather_first.1 = (f32[512,512]{1,0:T(8,128)S(1)}, f32[512,512]{1,0:T(8,128)S(1)}) custom-call(s32[8,512]{1,0:T(8,128)S(1)} %pad.8.links_ref, bf16[512,512]{1,0:T(8,128)(2,1)S(1)} %copy-done.6, bf16[512,512]{1,0:T(8,128)(2,1)S(1)} %collective-permute-done.s1_ref, bf16[512,512]{1,0:T(8,128)(2,1)S(1)} %copy-done, bf16[512,512]{1,0:T(8,128)(2,1)S(1)} %copy-done.4), custom_call_target="tpu_custom_call" | custom-call | flops 805306368 | bytes 5242880 | tf_op jit(solution)/shard_map/gather_first/pallas_call | solution.py:204
  20.9 1.0 %gather_rest.1.hb_ref = bf16[512,512]{1,0:T(8,128)(2,1)S(1)} custom-call(s32[8,512]{1,0:T(8,128)S(1)} %pad.8.links_ref, f32[512,512]{1,0:T(8,128)S(1)} %get-tuple-element.23.h0_ref, bf16[512,512]{1,0:T(8,128)(2,1)S(1)} %collective-permute-done.1.refs_0_, bf16[512,512]{1,0:T(8,128)(2,1)S(1)} %collective-permute-done.2.refs_1_), custom_call_target="tpu_custom_call" | custom-call | flops 536870912 | bytes 3145728 | tf_op jit(solution)/shard_map/gather_rest/pallas_call | solution.py:207
  22.2 1.6 %activate.1 = (bf16[512,512]{1,0:T(8,128)(2,1)}, bf16[512,512]{1,0:T(8,128)(2,1)S(1)}) custom-call(s32[1]{0:T(128)} %copy.13.length_ref, bf16[512,512]{1,0:T(8,128)(2,1)S(1)} %gather_rest.1.hb_ref, f32[512,512]{1,0:T(8,128)S(1)} %get-tuple-element.24.own_ref, bf16[512,512]{1,0:T(8,128)(2,1)S(1)} %copy-done.2, bf16[512,512]{1,0:T(8,128)(2,1)S(1)} %copy-done.1, ...), custom_call_target="tpu_custom_call" | custom-call | flops 268435456 | bytes 4194304 | tf_op jit(solution)/shard_map/activate/pallas_call | solution.py:213
  24.3 0.9 %broadcast_select_fusion = (bf16[512,512]{1,0:T(8,128)(2,1)}, bf16[512,512]{1,0:T(8,128)(2,1)S(1)}) fusion(bf16[512,512]{1,0:T(8,128)(2,1)S(1)} %gather_rest.1.hb_ref, bf16[512,512]{1,0:T(8,128)(2,1)S(1)} %copy-done.1, pred[]{:T(512)S(6)} %eq.50), kind=kLoop, calls=%fused_computation.2 | loop fusion | flops 524288 | bytes 2097153 | tf_op jit(solution)/shard_map/jit(_where)/select_n | solution.py:211
  25.9 1.3 %collective-permute-done.3 = s32[16,512]{1,0:T(8,128)S(1)} collective-permute-done((s32[16,512]{1,0:T(8,128)S(1)}, s32[16,512]{1,0:T(8,128)S(1)}, u32[]{:S(2)}, u32[]{:S(2)}) %collective-permute-start.3) | collective-permute-done | bytes 32800 | tf_op jit(solution)/shard_map/ppermute | solution.py:19
  28.4 1.3 %weight_terms.1 = (f32[128,512]{1,0:T(8,128)S(1)}, bf16[128,512]{1,0:T(8,128)(2,1)S(1)}, bf16[128,512]{1,0:T(8,128)(2,1)S(1)}, bf16[128,512]{1,0:T(8,128)(2,1)S(1)}) custom-call(s32[3]{0:T(128)S(1)} %pad_add_fusion.place_ref, s32[2]{0:T(128)S(1)} %pad_add_fusion.1.lengths_ref, bf16[512,512]{1,0:T(8,128)(2,1)S(1)} %get-tuple-element.42.x0_ref, ...), custom_call_target="tpu_custom_call" | custom-call | flops 536870912 | bytes 3145728 | tf_op jit(solution)/shard_map/weight_terms/pallas_call | solution.py:224
  29.7 1.8 %collective-permute-start.12 = (bf16[128,512]{1,0:T(8,128)(2,1)S(1)}, bf16[128,512]{1,0:T(8,128)(2,1)S(1)}, u32[]{:S(2)}, u32[]{:S(2)}) collective-permute-start(bf16[128,512]{1,0:T(8,128)(2,1)S(1)} %get-tuple-element.36), channel_id=1, source_target_pairs={{0,2},{1,3},{2,0},{3,1},{4,6},{5,7},{6,4},{7,5},{8,10},{9,11},{10,... | collective-permute-start | bytes 393224 | tf_op jit(solution)/shard_map/ppermute | solution.py:19
  31.6 1.5 %collective-permute-start.13 = (bf16[128,512]{1,0:T(8,128)(2,1)S(1)}, bf16[128,512]{1,0:T(8,128)(2,1)S(1)}, u32[]{:S(2)}, u32[]{:S(2)}) collective-permute-start(bf16[128,512]{1,0:T(8,128)(2,1)S(1)} %get-tuple-element.37), channel_id=1, source_target_pairs={{0,4},{1,5},{2,6},{3,7},{4,0},{5,1},{6,2},{7,3},{8,12},{9,13},{10,... | collective-permute-start | bytes 393224 | tf_op jit(solution)/shard_map/ppermute | solution.py:19
  33.3 2.1 %collective-permute-done.12.refs_0_ = bf16[128,512]{1,0:T(8,128)(2,1)S(1)} collective-permute-done((bf16[128,512]{1,0:T(8,128)(2,1)S(1)}, bf16[128,512]{1,0:T(8,128)(2,1)S(1)}, u32[]{:S(2)}, u32[]{:S(2)}) %collective-permute-start.12) | collective-permute-done | bytes 131104 | tf_op jit(solution)/shard_map/ppermute | solution.py:19
  35.4 2.6 %collective-permute-done.13.refs_1_ = bf16[128,512]{1,0:T(8,128)(2,1)S(1)} collective-permute-done((bf16[128,512]{1,0:T(8,128)(2,1)S(1)}, bf16[128,512]{1,0:T(8,128)(2,1)S(1)}, u32[]{:S(2)}, u32[]{:S(2)}) %collective-permute-start.13) | collective-permute-done | bytes 131104 | tf_op jit(solution)/shard_map/ppermute | solution.py:19
  37.9 1.5 %collective-permute-done.14.refs_2_ = bf16[128,512]{1,0:T(8,128)(2,1)S(1)} collective-permute-done((bf16[128,512]{1,0:T(8,128)(2,1)S(1)}, bf16[128,512]{1,0:T(8,128)(2,1)S(1)}, u32[]{:S(2)}, u32[]{:S(2)}) %collective-permute-start.14) | collective-permute-done | bytes 131104 | tf_op jit(solution)/shard_map/ppermute | solution.py:19
  39.5 1.8 %collective-permute-start.15 = (bf16[128,512]{1,0:T(8,128)(2,1)S(1)}, bf16[128,512]{1,0:T(8,128)(2,1)S(1)}, u32[]{:S(2)}, u32[]{:S(2)}) collective-permute-start(bf16[128,512]{1,0:T(8,128)(2,1)S(1)} %weight_sum_square.1.refs_0_), channel_id=1, source_target_pairs={{0,8},{1,9},{2,10},{3,11},{4,12},{5,13},{6,14},{7,15},{8,0},{9,1},... | collective-permute-start | bytes 393224 | tf_op jit(solution)/shard_map/ppermute | solution.py:19
  41.3 1.8 %source_terms.1 = (f32[256,512]{1,0:T(8,128)S(1)}, bf16[256,512]{1,0:T(8,128)(2,1)S(1)}, bf16[256,512]{1,0:T(8,128)(2,1)S(1)}, bf16[256,512]{1,0:T(8,128)(2,1)S(1)}) custom-call(s32[3]{0:T(128)S(1)} %pad_add_fusion.place_ref, s32[2]{0:T(128)S(1)} %pad_add_fusion.1.lengths_ref, s32[8,512]{1,0:T(8,128)S(1)} %pad.9.l0_ref, s32[8,512]{1,0:T(8,128)S(1)} %slice.9.l1_ref, ...), custom_call_target="tpu_custom_call" | custom-call | flops 1073741824 | bytes 3145728 | tf_op jit(solution)/shard_map/source_terms/pallas_call | solution.py:237
  43.1 1.6 %collective-permute-start.5 = (bf16[256,512]{1,0:T(8,128)(2,1)S(1)}, bf16[256,512]{1,0:T(8,128)(2,1)S(1)}, u32[]{:S(2)}, u32[]{:S(2)}) collective-permute-start(bf16[256,512]{1,0:T(8,128)(2,1)S(1)} %get-tuple-element.28), channel_id=1, source_target_pairs={{0,2},{1,3},{2,0},{3,1},{4,6},{5,7},{6,4},{7,5},{8,10},{9,11},{10,... | collective-permute-start | bytes 786440 | tf_op jit(solution)/shard_map/ppermute | solution.py:19
  44.7 1.5 %collective-permute-start.6 = (bf16[256,512]{1,0:T(8,128)(2,1)S(1)}, bf16[256,512]{1,0:T(8,128)(2,1)S(1)}, u32[]{:S(2)}, u32[]{:S(2)}) collective-permute-start(bf16[256,512]{1,0:T(8,128)(2,1)S(1)} %get-tuple-element.29), channel_id=1, source_target_pairs={{0,4},{1,5},{2,6},{3,7},{4,0},{5,1},{6,2},{7,3},{8,12},{9,13},{10,... | collective-permute-start | bytes 786440 | tf_op jit(solution)/shard_map/ppermute | solution.py:19
  46.6 2.6 %collective-permute-start.16 = (bf16[128,512]{1,0:T(8,128)(2,1)S(1)}, bf16[128,512]{1,0:T(8,128)(2,1)S(1)}, u32[]{:S(2)}, u32[]{:S(2)}) collective-permute-start(bf16[128,512]{1,0:T(8,128)(2,1)S(1)} %weight_sum_square.1.refs_0_), channel_id=1, source_target_pairs={{0,16},{1,17},{2,18},{3,19},{4,20},{5,21},{6,22},{7,23},{8,24},{9,... | collective-permute-start | bytes 393224 | tf_op jit(solution)/shard_map/ppermute | solution.py:19
  49.3 8.7 %collective-permute-done.16.refs_2_ = bf16[128,512]{1,0:T(8,128)(2,1)S(1)} collective-permute-done((bf16[128,512]{1,0:T(8,128)(2,1)S(1)}, bf16[128,512]{1,0:T(8,128)(2,1)S(1)}, u32[]{:S(2)}, u32[]{:S(2)}) %collective-permute-start.16) | collective-permute-done | bytes 131104 | tf_op jit(solution)/shard_map/ppermute | solution.py:19
  58.1 1.3 %collective-permute-start.18 = (bf16[128,512]{1,0:T(8,128)(2,1)S(1)}, bf16[128,512]{1,0:T(8,128)(2,1)S(1)}, u32[]{:S(2)}, u32[]{:S(2)}) collective-permute-start(bf16[128,512]{1,0:T(8,128)(2,1)S(1)} %weight_sum_layers.1.refs_0_), channel_id=1, source_target_pairs={{0,2},{1,3},{2,0},{3,1},{4,6},{5,7},{6,4},{7,5},{8,10},{9,11},{10,... | collective-permute-start | bytes 393224 | tf_op jit(solution)/shard_map/ppermute | solution.py:19
  59.4 1.5 %collective-permute-start.19 = (bf16[128,512]{1,0:T(8,128)(2,1)S(1)}, bf16[128,512]{1,0:T(8,128)(2,1)S(1)}, u32[]{:S(2)}, u32[]{:S(2)}) collective-permute-start(bf16[128,512]{1,0:T(8,128)(2,1)S(1)} %weight_sum_layers.1.refs_0_), channel_id=1, source_target_pairs={{0,4},{1,5},{2,6},{3,7},{4,0},{5,1},{6,2},{7,3},{8,12},{9,13},{10,... | collective-permute-start | bytes 393224 | tf_op jit(solution)/shard_map/ppermute | solution.py:19
  62.4 2.0 %collective-permute-start.8 = (bf16[64,512]{1,0:T(8,128)(2,1)S(1)}, bf16[64,512]{1,0:T(8,128)(2,1)S(1)}, u32[]{:S(2)}, u32[]{:S(2)}) collective-permute-start(bf16[64,512]{1,0:T(8,128)(2,1)S(1)} %get-tuple-element.32), channel_id=1, source_target_pairs={{0,8},{1,9},{2,10},{3,11},{4,12},{5,13},{6,14},{7,15},{8,0},{9,1},... | collective-permute-start | bytes 196616 | tf_op jit(solution)/shard_map/ppermute | solution.py:19
  64.4 1.3 %collective-permute-start.9 = (bf16[64,512]{1,0:T(8,128)(2,1)S(1)}, bf16[64,512]{1,0:T(8,128)(2,1)S(1)}, u32[]{:S(2)}, u32[]{:S(2)}) collective-permute-start(bf16[64,512]{1,0:T(8,128)(2,1)S(1)} %get-tuple-element.33), channel_id=1, source_target_pairs={{0,16},{1,17},{2,18},{3,19},{4,20},{5,21},{6,22},{7,23},{8,24},{9,... | collective-permute-start | bytes 196616 | tf_op jit(solution)/shard_map/ppermute | solution.py:19
  65.7 1.0 %collective-permute-done.8.refs_0_ = bf16[64,512]{1,0:T(8,128)(2,1)S(1)} collective-permute-done((bf16[64,512]{1,0:T(8,128)(2,1)S(1)}, bf16[64,512]{1,0:T(8,128)(2,1)S(1)}, u32[]{:S(2)}, u32[]{:S(2)}) %collective-permute-start.8) | collective-permute-done | bytes 65568 | tf_op jit(solution)/shard_map/ppermute | solution.py:19
  66.7 3.3 %collective-permute-start.10 = (bf16[64,512]{1,0:T(8,128)(2,1)S(1)}, bf16[64,512]{1,0:T(8,128)(2,1)S(1)}, u32[]{:S(2)}, u32[]{:S(2)}) collective-permute-start(bf16[64,512]{1,0:T(8,128)(2,1)S(1)} %get-tuple-element.34), channel_id=1, source_target_pairs={{0,24},{1,25},{2,26},{3,27},{4,28},{5,29},{6,30},{7,31},{8,16},{9,... | collective-permute-start | bytes 196616 | tf_op jit(solution)/shard_map/ppermute | solution.py:19
  70.0 0.8 %collective-permute-done.9.refs_1_ = bf16[64,512]{1,0:T(8,128)(2,1)S(1)} collective-permute-done((bf16[64,512]{1,0:T(8,128)(2,1)S(1)}, bf16[64,512]{1,0:T(8,128)(2,1)S(1)}, u32[]{:S(2)}, u32[]{:S(2)}) %collective-permute-start.9) | collective-permute-done | bytes 65568 | tf_op jit(solution)/shard_map/ppermute | solution.py:19
  71.8 1.3 %fusion = bf16[512,512]{1,0:T(8,128)(2,1)} fusion(bf16[512,512]{1,0:T(8,128)(2,1)S(1)} %get-tuple-element.26.g0_ref, bf16[512,512]{1,0:T(8,128)(2,1)S(1)} %copy-done.5, bf16[512,512]{1,0:T(8,128)(2,1)S(1)} %copy-done.3), kind=kOutput, calls=%fused_computation.1 | convolution fusion | flops 269221888 | bytes 2097152 | tf_op jit(solution)/shard_map/dot_general | solution.py:278
  73.1 0.9 %finish_source.1 = bf16[64,512]{1,0:T(8,128)(2,1)} custom-call(bf16[512,512]{1,0:T(8,128)(2,1)S(1)} %copy-done.2, f32[64,512]{1,0:T(8,128)S(1)} %get-tuple-element.31.own_ref, bf16[64,512]{1,0:T(8,128)(2,1)S(1)} %collective-permute-done.8.refs_0_, bf16[64,512]{1,0:T(8,128)(2,1)S(1)} %collective-permute-done.9.refs_1_, ...), custom_call_target="tpu_custom_call" | custom-call | bytes 1048576 | tf_op jit(solution)/shard_map/finish_source/pallas_call | solution.py:260
  74.0 2.0 %finish_weights.1 = (f32[512,512]{1,0:T(8,128)}, f32[512,512]{1,0:T(8,128)}) custom-call(s32[3]{0:T(128)S(1)} %pad_add_fusion.place_ref, bf16[128,512]{1,0:T(8,128)(2,1)S(1)} %weight_sum_layers.1.refs_0_, bf16[128,512]{1,0:T(8,128)(2,1)S(1)} %collective-permute-done.18.refs_1_, bf16[128,512]{1,0:T(8,128)(2,1)S(1)} %collective-permute-done.19.refs_2_, ...), custom_call_target="tpu_custom_call" | custom-call | bytes 3145728 | tf_op jit(solution)/shard_map/finish_weights/pallas_call | solution.py:268
  (63 shorter events, 7.7 us)
Async XLA Ops:
  0.6 16.1 %collective-permute-start = (bf16[512,512]{1,0:T(8,128)(2,1)}, bf16[512,512]{1,0:T(8,128)(2,1)S(1)}, u32[]{:S(2)}, u32[]{:S(2)}) collective-permute-start(bf16[512,512]{1,0:T(8,128)(2,1)} %s0_ref.1), channel_id=1, source_target_pairs={{0,1},{1,0},{2,3},{3,2},{4,5},{5,4},{6,7},{7,6},{8,9},{9,8},{10,11... | collective-permute-start | bytes 1572872 | tf_op jit(solution)/shard_map/ppermute | solution.py:19
  1.1 15.3 %collective-permute-start.1 = (bf16[512,512]{1,0:T(8,128)(2,1)}, bf16[512,512]{1,0:T(8,128)(2,1)S(1)}, u32[]{:S(2)}, u32[]{:S(2)}) collective-permute-start(bf16[512,512]{1,0:T(8,128)(2,1)} %s0_ref.1), channel_id=1, source_target_pairs={{0,2},{1,3},{2,0},{3,1},{4,6},{5,7},{6,4},{7,5},{8,10},{9,11},{10,... | collective-permute-start | bytes 1572872 | tf_op jit(solution)/shard_map/ppermute | solution.py:19
  16.5 4.4 %collective-permute-start.2 = (bf16[512,512]{1,0:T(8,128)(2,1)S(1)}, bf16[512,512]{1,0:T(8,128)(2,1)S(1)}, u32[]{:S(2)}, u32[]{:S(2)}) collective-permute-start(bf16[512,512]{1,0:T(8,128)(2,1)S(1)} %collective-permute-done.1.refs_0_), channel_id=1, source_target_pairs={{0,1},{1,0},{2,3},{3,2},{4,5},{5,4},{6,7},{7,6},{8,9},{9,8},{10,11... | collective-permute-start | bytes 1572872 | tf_op jit(solution)/shard_map/ppermute | solution.py:19
  16.7 1.0 %copy-start = (bf16[512,512]{1,0:T(8,128)(2,1)S(1)}, bf16[512,512]{1,0:T(8,128)(2,1)}, u32[]{:S(2)}) copy-start(bf16[512,512]{1,0:T(8,128)(2,1)} %t_ref.3) | copy-start | bytes 1572868
  17.7 1.0 %copy-start.4 = (bf16[512,512]{1,0:T(8,128)(2,1)S(1)}, bf16[512,512]{1,0:T(8,128)(2,1)}, u32[]{:S(2)}) copy-start(bf16[512,512]{1,0:T(8,128)(2,1)} %ws_ref.1) | copy-start | bytes 1572868
  18.8 1.0 %copy-start.6 = (bf16[512,512]{1,0:T(8,128)(2,1)S(1)}, bf16[512,512]{1,0:T(8,128)(2,1)}, u32[]{:S(2)}) copy-start(bf16[512,512]{1,0:T(8,128)(2,1)} %s0_ref.1) | copy-start | bytes 1572868
  20.9 1.0 %copy-start.1 = (bf16[512,512]{1,0:T(8,128)(2,1)S(1)}, bf16[512,512]{1,0:T(8,128)(2,1)}, u32[]{:S(2)}) copy-start(bf16[512,512]{1,0:T(8,128)(2,1)} %t_ref.3) | copy-start | bytes 1572868
  20.9 1.2 %copy-start.2 = (bf16[512,512]{1,0:T(8,128)(2,1)S(1)}, bf16[512,512]{1,0:T(8,128)(2,1)}, u32[]{:S(2)}) copy-start(bf16[512,512]{1,0:T(8,128)(2,1)} %wm_ref.3) | copy-start | bytes 1572868
  20.9 1.3 %copy-start.3 = (bf16[512,512]{1,0:T(8,128)(2,1)S(1)}, bf16[512,512]{1,0:T(8,128)(2,1)}, u32[]{:S(2)}) copy-start(bf16[512,512]{1,0:T(8,128)(2,1)} %cot_ref.1) | copy-start | bytes 1572868
  23.8 4.6 %collective-permute-start.4 = (bf16[512,512]{1,0:T(8,128)(2,1)S(1)}, bf16[512,512]{1,0:T(8,128)(2,1)S(1)}, u32[]{:S(2)}, u32[]{:S(2)}) collective-permute-start(bf16[512,512]{1,0:T(8,128)(2,1)S(1)} %get-tuple-element.26.g0_ref), channel_id=1, source_target_pairs={{0,1},{1,0},{2,3},{3,2},{4,5},{5,4},{6,7},{7,6},{8,9},{9,8},{10,11... | collective-permute-start | bytes 1572872 | tf_op jit(solution)/shard_map/ppermute | solution.py:19
  25.2 3.2 %collective-permute-start.11 = (bf16[512,512]{1,0:T(8,128)(2,1)}, bf16[512,512]{1,0:T(8,128)(2,1)S(1)}, u32[]{:S(2)}, u32[]{:S(2)}) collective-permute-start(bf16[512,512]{1,0:T(8,128)(2,1)} %get-tuple-element.41), channel_id=1, source_target_pairs={{0,1},{1,0},{2,3},{3,2},{4,5},{5,4},{6,7},{7,6},{8,9},{9,8},{10,11... | collective-permute-start | bytes 1572872 | tf_op jit(solution)/shard_map/ppermute | solution.py:19
  25.2 1.9 %collective-permute-start.3 = (s32[16,512]{1,0:T(8,128)S(1)}, s32[16,512]{1,0:T(8,128)S(1)}, u32[]{:S(2)}, u32[]{:S(2)}) collective-permute-start(s32[16,512]{1,0:T(8,128)S(1)} %concatenate.3), channel_id=1, source_target_pairs={{0,1},{1,0},{2,3},{3,2},{4,5},{5,4},{6,7},{7,6},{8,9},{9,8},{10,11... | collective-permute-start | bytes 98312 | tf_op jit(solution)/shard_map/ppermute | solution.py:19
  29.7 5.6 %collective-permute-start.12 = (bf16[128,512]{1,0:T(8,128)(2,1)S(1)}, bf16[128,512]{1,0:T(8,128)(2,1)S(1)}, u32[]{:S(2)}, u32[]{:S(2)}) collective-permute-start(bf16[128,512]{1,0:T(8,128)(2,1)S(1)} %get-tuple-element.36), channel_id=1, source_target_pairs={{0,2},{1,3},{2,0},{3,1},{4,6},{5,7},{6,4},{7,5},{8,10},{9,11},{10,... | collective-permute-start | bytes 393224 | tf_op jit(solution)/shard_map/ppermute | solution.py:19
  31.6 6.4 %collective-permute-start.13 = (bf16[128,512]{1,0:T(8,128)(2,1)S(1)}, bf16[128,512]{1,0:T(8,128)(2,1)S(1)}, u32[]{:S(2)}, u32[]{:S(2)}) collective-permute-start(bf16[128,512]{1,0:T(8,128)(2,1)S(1)} %get-tuple-element.37), channel_id=1, source_target_pairs={{0,4},{1,5},{2,6},{3,7},{4,0},{5,1},{6,2},{7,3},{8,12},{9,13},{10,... | collective-permute-start | bytes 393224 | tf_op jit(solution)/shard_map/ppermute | solution.py:19
  33.0 6.4 %collective-permute-start.14 = (bf16[128,512]{1,0:T(8,128)(2,1)S(1)}, bf16[128,512]{1,0:T(8,128)(2,1)S(1)}, u32[]{:S(2)}, u32[]{:S(2)}) collective-permute-start(bf16[128,512]{1,0:T(8,128)(2,1)S(1)} %get-tuple-element.38), channel_id=1, source_target_pairs={{0,6},{1,7},{2,4},{3,5},{4,2},{5,3},{6,0},{7,1},{8,14},{9,15},{10,... | collective-permute-start | bytes 393224 | tf_op jit(solution)/shard_map/ppermute | solution.py:19
  39.5 9.8 %collective-permute-start.15 = (bf16[128,512]{1,0:T(8,128)(2,1)S(1)}, bf16[128,512]{1,0:T(8,128)(2,1)S(1)}, u32[]{:S(2)}, u32[]{:S(2)}) collective-permute-start(bf16[128,512]{1,0:T(8,128)(2,1)S(1)} %weight_sum_square.1.refs_0_), channel_id=1, source_target_pairs={{0,8},{1,9},{2,10},{3,11},{4,12},{5,13},{6,14},{7,15},{8,0},{9,1},... | collective-permute-start | bytes 393224 | tf_op jit(solution)/shard_map/ppermute | solution.py:19
  43.1 17.8 %collective-permute-start.5 = (bf16[256,512]{1,0:T(8,128)(2,1)S(1)}, bf16[256,512]{1,0:T(8,128)(2,1)S(1)}, u32[]{:S(2)}, u32[]{:S(2)}) collective-permute-start(bf16[256,512]{1,0:T(8,128)(2,1)S(1)} %get-tuple-element.28), channel_id=1, source_target_pairs={{0,2},{1,3},{2,0},{3,1},{4,6},{5,7},{6,4},{7,5},{8,10},{9,11},{10,... | collective-permute-start | bytes 786440 | tf_op jit(solution)/shard_map/ppermute | solution.py:19
  44.7 16.9 %collective-permute-start.6 = (bf16[256,512]{1,0:T(8,128)(2,1)S(1)}, bf16[256,512]{1,0:T(8,128)(2,1)S(1)}, u32[]{:S(2)}, u32[]{:S(2)}) collective-permute-start(bf16[256,512]{1,0:T(8,128)(2,1)S(1)} %get-tuple-element.29), channel_id=1, source_target_pairs={{0,4},{1,5},{2,6},{3,7},{4,0},{5,1},{6,2},{7,3},{8,12},{9,13},{10,... | collective-permute-start | bytes 786440 | tf_op jit(solution)/shard_map/ppermute | solution.py:19
  46.2 15.4 %collective-permute-start.7 = (bf16[256,512]{1,0:T(8,128)(2,1)S(1)}, bf16[256,512]{1,0:T(8,128)(2,1)S(1)}, u32[]{:S(2)}, u32[]{:S(2)}) collective-permute-start(bf16[256,512]{1,0:T(8,128)(2,1)S(1)} %get-tuple-element.30), channel_id=1, source_target_pairs={{0,6},{1,7},{2,4},{3,5},{4,2},{5,3},{6,0},{7,1},{8,14},{9,15},{10,... | collective-permute-start | bytes 786440 | tf_op jit(solution)/shard_map/ppermute | solution.py:19
  46.6 11.3 %collective-permute-start.16 = (bf16[128,512]{1,0:T(8,128)(2,1)S(1)}, bf16[128,512]{1,0:T(8,128)(2,1)S(1)}, u32[]{:S(2)}, u32[]{:S(2)}) collective-permute-start(bf16[128,512]{1,0:T(8,128)(2,1)S(1)} %weight_sum_square.1.refs_0_), channel_id=1, source_target_pairs={{0,16},{1,17},{2,18},{3,19},{4,20},{5,21},{6,22},{7,23},{8,24},{9,... | collective-permute-start | bytes 393224 | tf_op jit(solution)/shard_map/ppermute | solution.py:19
  49.2 8.7 %collective-permute-start.17 = (bf16[128,512]{1,0:T(8,128)(2,1)S(1)}, bf16[128,512]{1,0:T(8,128)(2,1)S(1)}, u32[]{:S(2)}, u32[]{:S(2)}) collective-permute-start(bf16[128,512]{1,0:T(8,128)(2,1)S(1)} %weight_sum_square.1.refs_0_), channel_id=1, source_target_pairs={{0,24},{1,25},{2,26},{3,27},{4,28},{5,29},{6,30},{7,31},{8,16},{9,... | collective-permute-start | bytes 393224 | tf_op jit(solution)/shard_map/ppermute | solution.py:19
  58.1 12.7 %collective-permute-start.18 = (bf16[128,512]{1,0:T(8,128)(2,1)S(1)}, bf16[128,512]{1,0:T(8,128)(2,1)S(1)}, u32[]{:S(2)}, u32[]{:S(2)}) collective-permute-start(bf16[128,512]{1,0:T(8,128)(2,1)S(1)} %weight_sum_layers.1.refs_0_), channel_id=1, source_target_pairs={{0,2},{1,3},{2,0},{3,1},{4,6},{5,7},{6,4},{7,5},{8,10},{9,11},{10,... | collective-permute-start | bytes 393224 | tf_op jit(solution)/shard_map/ppermute | solution.py:19
  59.4 11.9 %collective-permute-start.19 = (bf16[128,512]{1,0:T(8,128)(2,1)S(1)}, bf16[128,512]{1,0:T(8,128)(2,1)S(1)}, u32[]{:S(2)}, u32[]{:S(2)}) collective-permute-start(bf16[128,512]{1,0:T(8,128)(2,1)S(1)} %weight_sum_layers.1.refs_0_), channel_id=1, source_target_pairs={{0,4},{1,5},{2,6},{3,7},{4,0},{5,1},{6,2},{7,3},{8,12},{9,13},{10,... | collective-permute-start | bytes 393224 | tf_op jit(solution)/shard_map/ppermute | solution.py:19
  60.9 10.5 %collective-permute-start.20 = (bf16[128,512]{1,0:T(8,128)(2,1)S(1)}, bf16[128,512]{1,0:T(8,128)(2,1)S(1)}, u32[]{:S(2)}, u32[]{:S(2)}) collective-permute-start(bf16[128,512]{1,0:T(8,128)(2,1)S(1)} %weight_sum_layers.1.refs_0_), channel_id=1, source_target_pairs={{0,6},{1,7},{2,4},{3,5},{4,2},{5,3},{6,0},{7,1},{8,14},{9,15},{10,... | collective-permute-start | bytes 393224 | tf_op jit(solution)/shard_map/ppermute | solution.py:19
  61.6 10.2 %copy-start.5 = (bf16[512,512]{1,0:T(8,128)(2,1)S(1)}, bf16[512,512]{1,0:T(8,128)(2,1)}, u32[]{:S(2)}) copy-start(bf16[512,512]{1,0:T(8,128)(2,1)} %ws_ref.1) | copy-start | bytes 1572868
  62.4 4.3 %collective-permute-start.8 = (bf16[64,512]{1,0:T(8,128)(2,1)S(1)}, bf16[64,512]{1,0:T(8,128)(2,1)S(1)}, u32[]{:S(2)}, u32[]{:S(2)}) collective-permute-start(bf16[64,512]{1,0:T(8,128)(2,1)S(1)} %get-tuple-element.32), channel_id=1, source_target_pairs={{0,8},{1,9},{2,10},{3,11},{4,12},{5,13},{6,14},{7,15},{8,0},{9,1},... | collective-permute-start | bytes 196616 | tf_op jit(solution)/shard_map/ppermute | solution.py:19
  64.4 6.3 %collective-permute-start.9 = (bf16[64,512]{1,0:T(8,128)(2,1)S(1)}, bf16[64,512]{1,0:T(8,128)(2,1)S(1)}, u32[]{:S(2)}, u32[]{:S(2)}) collective-permute-start(bf16[64,512]{1,0:T(8,128)(2,1)S(1)} %get-tuple-element.33), channel_id=1, source_target_pairs={{0,16},{1,17},{2,18},{3,19},{4,20},{5,21},{6,22},{7,23},{8,24},{9,... | collective-permute-start | bytes 196616 | tf_op jit(solution)/shard_map/ppermute | solution.py:19
  66.7 6.4 %collective-permute-start.10 = (bf16[64,512]{1,0:T(8,128)(2,1)S(1)}, bf16[64,512]{1,0:T(8,128)(2,1)S(1)}, u32[]{:S(2)}, u32[]{:S(2)}) collective-permute-start(bf16[64,512]{1,0:T(8,128)(2,1)S(1)} %get-tuple-element.34), channel_id=1, source_target_pairs={{0,24},{1,25},{2,26},{3,27},{4,28},{5,29},{6,30},{7,31},{8,16},{9,... | collective-permute-start | bytes 196616 | tf_op jit(solution)/shard_map/ppermute | solution.py:19
  70.7 3.2 %collective-permute-start.21 = (bf16[128,512]{1,0:T(8,128)(2,1)S(1)}, bf16[128,512]{1,0:T(8,128)(2,1)S(1)}, u32[]{:S(2)}, u32[]{:S(2)}) collective-permute-start(bf16[128,512]{1,0:T(8,128)(2,1)S(1)} %weight_sum_layers.1.refs_0_), channel_id=1, source_target_pairs={{0,1},{1,0},{2,3},{3,2},{4,5},{5,4},{6,7},{7,6},{8,9},{9,8},{10,11... | collective-permute-start | bytes 393224 | tf_op jit(solution)/shard_map/ppermute | solution.py:19
  70.8 3.2 %collective-permute-start.22 = (bf16[128,512]{1,0:T(8,128)(2,1)S(1)}, bf16[128,512]{1,0:T(8,128)(2,1)S(1)}, u32[]{:S(2)}, u32[]{:S(2)}) collective-permute-start(bf16[128,512]{1,0:T(8,128)(2,1)S(1)} %collective-permute-done.18.refs_1_), channel_id=1, source_target_pairs={{0,1},{1,0},{2,3},{3,2},{4,5},{5,4},{6,7},{7,6},{8,9},{9,8},{10,11... | collective-permute-start | bytes 393224 | tf_op jit(solution)/shard_map/ppermute | solution.py:19
  71.3 2.7 %collective-permute-start.23 = (bf16[128,512]{1,0:T(8,128)(2,1)S(1)}, bf16[128,512]{1,0:T(8,128)(2,1)S(1)}, u32[]{:S(2)}, u32[]{:S(2)}) collective-permute-start(bf16[128,512]{1,0:T(8,128)(2,1)S(1)} %collective-permute-done.19.refs_2_), channel_id=1, source_target_pairs={{0,1},{1,0},{2,3},{3,2},{4,5},{5,4},{6,7},{7,6},{8,9},{9,8},{10,11... | collective-permute-start | bytes 393224 | tf_op jit(solution)/shard_map/ppermute | solution.py:19
  71.3 2.7 %collective-permute-start.24 = (bf16[128,512]{1,0:T(8,128)(2,1)S(1)}, bf16[128,512]{1,0:T(8,128)(2,1)S(1)}, u32[]{:S(2)}, u32[]{:S(2)}) collective-permute-start(bf16[128,512]{1,0:T(8,128)(2,1)S(1)} %collective-permute-done.20.refs_3_), channel_id=1, source_target_pairs={{0,1},{1,0},{2,3},{3,2},{4,5},{5,4},{6,7},{7,6},{8,9},{9,8},{10,11... | collective-permute-start | bytes 393224 | tf_op jit(solution)/shard_map/ppermute | solution.py:19
  (2 other events, 1.4 us)

commit v2 on v0

v2 whole, which is shorter than its diff:
```python
import functools

import jax
import jax.numpy as jnp
from jax import lax
from jax.experimental import pallas as pl
from jax.experimental.pallas import tpu as pltpu
from jax.sharding import PartitionSpec as P

AXES = ("row", "blk")
BF16 = jnp.bfloat16
F32 = jnp.float32
SMEM = pl.BlockSpec(memory_space=pltpu.SMEM)
VMEM = pl.BlockSpec(memory_space=pltpu.VMEM)
HBM = pl.BlockSpec(memory_space=pltpu.HBM)
ROWS = ((0,), (0,))
LANES = ((1,), (1,))


def swap(value, mask, devices):
    return lax.ppermute(value, AXES, [(i, i ^ mask) for i in range(devices)])


def call(body, name, out_shape, scalars=0, inputs=0, flops=0, moved=1 << 20, **more):
    return pl.pallas_call(
        body,
        name=name,
        in_specs=[SMEM] * scalars + [VMEM] * inputs,
        out_shape=out_shape,
        compiler_params=pltpu.CompilerParams(vmem_limit_bytes=20 << 20),
        cost_estimate=pl.CostEstimate(flops=flops, bytes_accessed=moved, transcendentals=0),
        **more,
    )


def shaped(shape, dtype):
    return jax.ShapeDtypeStruct(shape, dtype)


def mm(a, b, dims=((1,), (0,))):
    return lax.dot_general(a, b, (dims, ((), ())), preferred_element_type=F32)


def pattern(rows, lanes):
    return (rows == lanes).astype(F32).astype(BF16)


def part(ref, core):
    half = ref.shape[1] // 2
    return ref[:, pl.ds(pl.multiple_of(core * half, half), half)]


def inverse(lengths_ref, i, width):
    return 1.0 / jnp.full((1, width), lengths_ref[i], jnp.int32).astype(F32)


def linked(column, s_ref):
    lanes = lax.broadcasted_iota(jnp.int32, (column.shape[0], s_ref.shape[0]), 1)
    return mm(pattern(column, lanes), s_ref[...])


def gather_first(place_ref, links0_ref, links1_ref, s_ref, t_ref, ws_ref, columns_ref, own_ref, h_ref, weight_ref, near_ref):
    block = place_ref[3]
    rows = t_ref.shape[0]
    weight = part(ws_ref, place_ref[0])
    weight_ref[...] = weight
    own_ref[...] = mm(t_ref[...], weight)
    for i, links_ref in enumerate((links0_ref, links1_ref)):
        span = pl.ds(i * rows, rows)
        for m in range(links_ref.shape[0]):
            near_ref[m : m + 1, :] = links_ref[pl.ds(block ^ m, 1), :]
        columns = near_ref[...].T
        columns_ref[span, :] = columns
        h_ref[span, :] = linked(columns[:, 0:1], s_ref)


def gather_middle(order, place_ref, columns_ref, h0_ref, t_ref, weight_ref, *refs):
    s_refs, own_ref, h_ref = refs[:-2], refs[-2], refs[-1]
    rows = t_ref.shape[0]
    own_ref[...] = mm(t_ref[...], weight_ref[...])
    add_linked(order, columns_ref, h0_ref, s_refs, h_ref, rows)


def gather_more(order, columns_ref, h0_ref, *refs):
    add_linked(order, columns_ref, h0_ref, refs[:-1], refs[-1], h0_ref.shape[0] // 2)


def add_linked(order, columns_ref, h0_ref, s_refs, h_ref, rows):
    for i in range(2):
        span = pl.ds(i * rows, rows)
        total = h0_ref[span, :]
        for m, s_ref in zip(order, s_refs):
            total = total + linked(columns_ref[span, m : m + 1], s_ref)
        h_ref[span, :] = total


def forward(order, place_ref, lengths_ref, columns_ref, h0_ref, own0_ref, own1_ref, wm_ref, t0_ref, t1_ref, c0_ref, c1_ref, *refs):
    s_refs, (h_ref, grad_ref, updated_ref) = refs[:-3], refs[-3:]
    core = place_ref[0]
    rows, width = t0_ref.shape
    weight = part(wm_ref, core)
    for i, (t_ref, c_ref, own_ref) in enumerate(((t0_ref, c0_ref, own0_ref), (t1_ref, c1_ref, own1_ref))):
        span = pl.ds(i * rows, rows)
        total = h0_ref[span, :]
        for m, s_ref in zip(order, s_refs):
            total = total + linked(columns_ref[span, m : m + 1], s_ref)
        gathered = (total * inverse(lengths_ref, i, width)).astype(BF16)
        h_ref[span, :] = gathered
        preact = own_ref[...] + mm(gathered, weight)
        sig = jax.nn.sigmoid(preact)
        updated_ref[span, :] = (part(t_ref, core).astype(F32) + preact * sig).astype(BF16)
        upstream = part(c_ref, core).astype(F32)
        grad_ref[span, :] = (upstream * sig * (1.0 + preact * (1.0 - sig))).astype(BF16)


def weight_terms(place_ref, t0_ref, t1_ref, h_ref, grad_ref, *refs):
    own_ref, sent_refs, total_ref = refs[0], refs[1:-1], refs[-1]
    quad = place_ref[1]
    rows, width = t0_ref.shape
    piece = own_ref.shape[0]
    total_ref[0:width, :] = mm(t0_ref[...], grad_ref[0:rows, :], ROWS) + mm(t1_ref[...], grad_ref[rows:, :], ROWS)
    total_ref[width:, :] = mm(h_ref[...], grad_ref[...], ROWS)
    for m, ref in enumerate((own_ref, *sent_refs)):
        at = pl.multiple_of((quad ^ m) * piece, piece)
        ref[...] = total_ref[pl.ds(at, piece), :].astype(ref.dtype)


def source_terms(share, sides, orders, place_ref, lengths_ref, links0_ref, links1_ref, grad_ref, other_ref, *refs):
    core, quad, layer = place_ref[0], place_ref[1], place_ref[2]
    targets = links0_ref.shape[1]
    half = grad_ref.shape[1]
    rows = 2 * refs[0].shape[0] // len(orders[0])
    position = lax.broadcasted_iota(jnp.int32, (rows, targets), 0)
    inverses = [inverse(lengths_ref, i, half) for i in range(2)]
    for n, order in enumerate(orders):
        far = reverse_bits(position // share + n * (rows // share), 2 * rows // share)
        inside = (layer ^ far) * (2 * share) + position % share
        for j, m in enumerate(order):
            ref = refs[2 * n + j // (len(order) // 2)]
            at = (j % (len(order) // 2)) * rows
            to = quad ^ m
            row_at = inside + (to // sides) * share
            block = (to % sides) * 2 + core
            totals = [None, None]
            for i, links_ref in enumerate((links0_ref, links1_ref)):
                chosen = pattern(links_ref[pl.ds(block, 1), :], row_at)
                for c, g_ref in enumerate((grad_ref, other_ref)):
                    at_target = (i ^ c) * targets
                    added = mm(chosen, g_ref[at_target : at_target + targets, :]) * inverses[i]
                    totals[c] = added if totals[c] is None else totals[c] + added
            first = core == 0
            ref[at : at + rows, 0:half] = jnp.where(first, totals[0], totals[1]).astype(ref.dtype)
            ref[at : at + rows, half:] = jnp.where(first, totals[1], totals[0]).astype(ref.dtype)


def reverse_bits(value, size):
    result, low, high = value * 0, 1, size // 2
    while high:
        result = result + ((value // low) % 2) * high
        low, high = low * 2, high // 2
    return result


def halve(own_ref, received_ref, *refs):
    rows = refs[0].shape[0]
    for n, ref in enumerate(refs):
        span = pl.ds(n * rows, rows)
        ref[...] = (own_ref[span, :] + received_ref[span, :].astype(F32)).astype(ref.dtype)


def add_up(*refs):
    total = refs[0][...].astype(F32)
    for ref in refs[1:-1]:
        total = total + ref[...].astype(F32)
    refs[-1][...] = total.astype(BF16)


def finish_source(wm_ref, own_ref, received_ref, out_ref):
    total = (own_ref[...] + received_ref[...].astype(F32)).astype(BF16)
    out_ref[...] = mm(total, wm_ref[...], LANES).astype(BF16)


def target_side(place_ref, ws_ref, cot_ref, grad_ref, grad_received_ref, held_ref, held_received_ref, out_ref, updated_ref):
    core = place_ref[0]
    rows = cot_ref.shape[0]
    out_ref[...] = (
        cot_ref[...].astype(F32)
        + mm(grad_ref[0:rows, :], part(ws_ref, core), LANES)
        + mm(grad_received_ref[rows:, :], part(ws_ref, 1 - core), LANES)
    ).astype(BF16)
    half = held_ref.shape[1]
    updated_ref[:, pl.ds(pl.multiple_of(core * half, half), half)] = held_ref[0:rows, :]
    updated_ref[:, pl.ds(pl.multiple_of((1 - core) * half, half), half)] = held_received_ref[...]


def finish_weights(quads, scales, place_ref, *refs):
    refs, outs, buffer, sems = refs[: 2 * quads], refs[-4:-2], refs[-2], refs[-1]
    core, quad = place_ref[0], place_ref[1]
    count = quads // 2
    rows, half = refs[0].shape

    def copies(n):
        slot = quad ^ (n % quads)
        column = pl.multiple_of((core if n < quads else 1 - core) * half, half)
        row = pl.multiple_of((slot % count) * rows, rows)
        return slot // count, [
            pltpu.make_async_copy(buffer.at[n], out.at[pl.ds(row, rows), pl.ds(column, half)], sems.at[n]) for out in outs
        ]

    for n, ref in enumerate(refs):
        which, pair = copies(n)
        buffer[n] = ref[...].astype(F32) * jnp.where(which == 0, scales[0], scales[1])
        for k in range(2):
            pl.when(which == k)(pair[k].start)
    for n in range(2 * quads):
        which, pair = copies(n)
        for k in range(2):
            pl.when(which == k)(pair[k].wait)


def local(row_devices, blk_devices, source_table, target_table, message_weight, self_weight, tile_lists, key_offsets, list_lengths, cotangent):
    devices = row_devices * blk_devices
    targets, width = target_table.shape
    block_rows = source_table.shape[0]
    slots = tile_lists.shape[1]
    assert tile_lists.shape[0] == 1 and block_rows == targets and slots == blk_devices
    half = width // 2
    sides = blk_devices // 2
    quads = blk_devices
    layers = row_devices // 2
    share = block_rows // row_devices
    square = 2 * targets * width * width

    row_at = lax.axis_index("row")
    blk_at = lax.axis_index("blk")
    quad = (row_at % 2) * sides + blk_at // 2
    place = jnp.stack([blk_at % 2, quad, row_at // 2, blk_at]).astype(jnp.int32)

    direct = list(range(2, blk_devices, 2))
    held = {m: swap(source_table, m, devices) for m in direct}

    blocks = lax.iota(jnp.int32, blk_devices)
    used = (tile_lists[0][None, :] == blocks[:, None]) & (lax.iota(jnp.int32, slots)[None, :] < list_lengths[0])
    links = jnp.max(jnp.where(used[:, :, None], key_offsets.T[None, :, :], -1), axis=1)
    packed = jnp.concatenate([links, jnp.broadcast_to(list_lengths[:, None], (8 - slots % 8, targets))], axis=0)
    their_packed = swap(packed, 1, devices)
    lengths = jnp.stack([packed[slots, 0], their_packed[slots, 0]])
    links, their_links = packed[:slots], their_packed[:slots]

    table0, cot0 = target_table, cotangent
    held[1] = swap(source_table, 1, devices)
    table1 = swap(table0, 1, devices)
    cot1 = swap(cot0, 1, devices)

    columns, own0, gathered, weight = call(
        gather_first,
        "gather_first",
        (
            shaped((2 * targets, slots), jnp.int32),
            shaped((targets, half), F32),
            shaped((2 * targets, width), F32),
            shaped((width, half), BF16),
        ),
        scalars=1,
        inputs=5,
        moved=0,
        scratch_shapes=[pltpu.VMEM((slots, targets), jnp.int32)],
    )(place, links, their_links, source_table, table0, self_weight)
    own1, gathered = call(
        functools.partial(gather_middle, [1]),
        "gather_middle",
        (shaped((targets, half), F32), shaped((2 * targets, width), F32)),
        scalars=1,
        inputs=5,
        moved=0,
    )(place, columns, gathered, table1, weight, held[1])
    ready = lax.optimization_barrier((columns, own0, own1, gathered, lengths, place, *[held[m] for m in direct]))
    columns, own0, own1, gathered, lengths, place = ready[:6]
    for m, value in zip(direct, ready[6:]):
        held[m] = value
        held[m + 1] = swap(value, 1, devices)
    gathered = call(
        functools.partial(gather_more, direct),
        "gather_more",
        shaped((2 * targets, width), F32),
        inputs=2 + len(direct),
        flops=2 * square,
    )(columns, gathered, *[held[m] for m in direct])
    order = [m + 1 for m in direct]
    gathered, grad, updated = call(
        functools.partial(forward, order),
        "forward",
        (
            shaped((2 * targets, width), BF16),
            shaped((2 * targets, half), BF16),
            shaped((2 * targets, half), BF16),
        ),
        scalars=2,
        inputs=9 + len(order),
        flops=2 * sides * square,
    )(
        place, lengths, columns, gathered, own0, own1, message_weight, table0, table1, cot0, cot1,
        *[held[m] for m in order],
    )

    piece = 2 * width // quads
    terms = call(
        weight_terms,
        "weight_terms",
        [shaped((piece, half), F32)] + [shaped((piece, half), BF16)] * (quads - 1),
        scalars=1,
        inputs=4,
        flops=2 * square,
        scratch_shapes=[pltpu.VMEM((2 * width, half), F32)],
    )(place, table0, table1, gathered, grad)
    received = [swap(terms[m], 2 * m, devices) for m in reversed(range(1, quads))]

    grad_received = swap(grad, 1, devices)
    updated_received = swap(updated[targets:], 1, devices)
    grad_received, updated_received = lax.optimization_barrier((grad_received, updated_received))
    masks = [1 << i for i in range(quads.bit_length() - 1)]
    routes = (masks, masks[::-1])
    orders = [[sum(mask * ((j >> (len(masks) - 1 - i)) & 1) for i, mask in enumerate(route)) for j in range(quads)] for route in routes]
    half_rows = layers * share // 2
    count = quads // 2 * half_rows
    sources = call(
        functools.partial(source_terms, share, sides, orders),
        "source_terms",
        [shaped((count, width), F32), shaped((count, width), BF16)] * 2,
        scalars=2,
        inputs=4,
        flops=4 * square,
    )(place, lengths, links, their_links, grad, grad_received)
    _, received = lax.optimization_barrier((sources, received))

    state = [[sources[0], sources[1]], [sources[2], sources[3]]]

    def source_step(n):
        return [swap(state[k][1], 2 * routes[k][n], devices) for k in range(2)]

    def source_add(n, came):
        for k in range(2):
            if n == len(masks) - 1:
                outs = [shaped((half_rows, width), (F32, BF16)[k])]
            else:
                rows = state[k][0].shape[0] // 2
                outs = [shaped((rows, width), F32), shaped((rows, width), BF16)]
            state[k] = call(halve, "source_sum", outs, inputs=2)(state[k][0], came[k])

    total = call(add_up, "weight_sum", shaped((piece, half), BF16), inputs=quads)(terms[0], *received)
    mask, n = 1, 0
    while mask < layers:
        other = swap(total, 2 * quads * mask, devices)
        came = source_step(n)
        total = call(add_up, "weight_sum", shaped((piece, half), BF16), inputs=2)(total, other)
        source_add(n, came)
        mask, n = 2 * mask, n + 1
    target_gradient, updated = call(
        target_side, "target_side", (shaped((targets, width), BF16),) * 2, scalars=1, inputs=6, flops=square
    )(place, self_weight, cot0, grad, grad_received, updated, updated_received)
    total, target_gradient, updated = lax.optimization_barrier((total, target_gradient, updated))
    while n < len(masks):
        source_add(n, source_step(n))
        n += 1
    stays, goes = state[0][0], state[1][0]
    pieces = {0: total}
    for m in reversed(range(1, quads)):
        pieces[m] = swap(total, 2 * m, devices)

    mask = 1
    while mask < layers:
        came = swap(goes, 2 * quads * mask, devices)
        mask *= 2
        if mask == layers:
            source_gradient = call(finish_source, "finish_source", shaped((share, width), BF16), inputs=3)(
                message_weight, stays, came
            )
        else:
            rows = stays.shape[0] // 2
            stays, goes = call(halve, "source_sum", [shaped((rows, width), F32), shaped((rows, width), BF16)], inputs=2)(
                stays, came
            )

    their_pieces = {m: swap(value, 1, devices) for m, value in pieces.items()}
    scales = ((targets * devices) ** (-0.5), (block_rows * blk_devices) ** (-0.5))
    self_gradient, message_gradient = call(
        functools.partial(finish_weights, quads, scales),
        "finish_weights",
        (shaped((width, width), F32),) * 2,
        scalars=1,
        inputs=2 * quads,
        out_specs=(HBM, HBM),
        scratch_shapes=[pltpu.VMEM((2 * quads, piece, half), F32), pltpu.SemaphoreType.DMA((2 * quads,))],
    )(place, *[values[m] for values in (pieces, their_pieces) for m in range(quads)])
    return (updated, target_gradient, source_gradient, self_gradient, message_gradient)


def solution(mesh):
    split = P(AXES, None)
    return jax.shard_map(
        functools.partial(local, mesh.shape["row"], mesh.shape["blk"]),
        mesh=mesh,
        in_specs=(P("blk", None), split, P(), P(), split, split, P(AXES), split),
        out_specs=(split, split, P(("blk", "row"), None), P(), P()),
        check_vma=False,
    )
```

time: 338 us -> 63.3 us (0.19)
  waiting for transfers between devices: 269 us -> 14.7 us
  starting transfers between devices: 0.16 us -> 26.3 us
  matrix products: 22.8 us -> 0 us
  Pallas kernels: 0 us -> 14.5 us
  between operations: 14.5 us -> 1.44 us
  loops' own time: 10.6 us -> 0 us
  other arithmetic: 11.9 us -> 2.27 us
  local copies, waits for them, and re-layouts: 8.48 us -> 3.68 us
    psum x1 -> x0, waiting for transfers between devices: 135 us -> none  [local(): lax.psum((self_partial, message_partial), ('row', 'blk'))]
    reduce_scatter x2 -> x0, waiting for transfers between devices: 110 us -> none  [the longest x1 65.7 us: local(): lax.psum_scatter(block_sum, 'row', scatter_dimension=0, tiled=True)]
    ppermute x0 -> x26, starting transfers between devices: none -> 26.3 us  [swap(): return lax.ppermute(value, AXES, [(i, i ^ mask) for i in range(devices)])]
    all_gather x1 -> x0, waiting for transfers between devices: 24.3 us -> none  [local(): pieces = lax.all_gather(projected, 'blk', axis=0, tiled=True)]
    dot_general x14 -> x0, matrix products: 22.8 us -> none  [the longest x4 6.48 us: gather_visit(): jnp.einsum('trc,cw->trw', pattern, source_tile, preferred_element_type=jn...]
    ppermute x0 -> x26, waiting for transfers between devices: none -> 14.7 us  [swap(): return lax.ppermute(value, AXES, [(i, i ^ mask) for i in range(devices)])]
    pallas_call x0 -> x17, Pallas kernels: none -> 14.5 us  [the longest x1 2.02 us: local(): call(functools.partial(forward, order), 'forward', (shaped((2 * targets,...]
    another operation x2 -> x0, loops' own time: 10.6 us -> none  [the longest x1 5.34 us: local(): gathered = lax.fori_loop(0, piece_tiles, gather_visit, start_sum)]
  transfers between devices with their start and end apart: 4 -> 26, of which waited for: 4 -> 11; matrix products, arithmetic and copies ran while one was open for 1% -> 4% of each run, Pallas kernels for 0% -> 18%
where the time goes in v2:
time: 63.3 us; the launch traced here: 62.9 us
  starting transfers between devices  26.3 us (42%)
  waiting for transfers between devices  14.7 us (23%)
  Pallas kernels  14.5 us (23%)
  local copies, waits for them, and re-layouts  3.68 us (6%)
  other arithmetic  2.27 us (4%)
  between operations  1.44 us (2%)
    ppermute x26, starting transfers between devices, swap(): return lax.ppermute(value, AXES, [(i, i ^ mask) for i in range(devices)])  26.3 us
    ppermute x26, waiting for transfers between devices, swap(): return lax.ppermute(value, AXES, [(i, i ^ mask) for i in range(devices)])  14.7 us
    unnamed x14, local copies, waits for them, and re-layouts  3.14 us
    pallas_call x1, Pallas kernels, local(): call(functools.partial(forward, order), 'forward', (shaped((2 * targets,...  2.02 us
    pallas_call x1, Pallas kernels, local(): call(functools.partial(source_terms, share, sides, orders), 'source_terms...  1.99 us
    pallas_call x1, Pallas kernels, local(): call(target_side, 'target_side', (shaped((targets, width), BF16),) * 2, s...  1.95 us
    pallas_call x1, Pallas kernels, local(): call(functools.partial(finish_weights, quads, scales), 'finish_weights',...  1.95 us
    pallas_call x1, Pallas kernels, local(): call(gather_first, 'gather_first', (shaped((2 * targets, slots), jnp.int3...  1.67 us
  transfers between devices with their start and end apart: 26, of which 11 were waited for; matrix products, arithmetic and copies ran while one was open for 4% of the time, Pallas kernels for 18%

profile of v2, /device:TPU:0, one launch (start us, length us, event | category | flops | bytes accessed | tf_op | source)
XLA Modules:
  0.0 62.9 jit_solution(1232747392004619746)
XLA Ops:
  1.1 2.6 %collective-permute-start.3 = (bf16[512,512]{1,0:T(8,128)(2,1)}, bf16[512,512]{1,0:T(8,128)(2,1)S(1)}, u32[]{:S(2)}, u32[]{:S(2)}) collective-permute-start(bf16[512,512]{1,0:T(8,128)(2,1)} %s_ref.1), channel_id=1, source_target_pairs={{0,2},{1,3},{2,0},{3,1},{4,6},{5,7},{6,4},{7,5},{8,10},{9,11},{10,... | collective-permute-start | bytes 1572872 | tf_op jit(solution)/shard_map/ppermute | solution.py:21
  5.2 0.8 %select_reduce_fusion.links0_ref = s32[4,512]{1,0:T(4,128)S(1)} fusion(s32[4,512]{1,0:T(4,128)} %bitcast.10, pred[4,4]{1,0:T(4,128)(4,1)S(1)} %fusion), kind=kLoop, calls=%fused_computation | loop fusion | flops 14336 | bytes 16400 | tf_op jit(solution)/shard_map/reduce_max | solution.py:244
  7.3 1.0 %copy-done = bf16[512,512]{1,0:T(8,128)(2,1)S(1)} copy-done((bf16[512,512]{1,0:T(8,128)(2,1)S(1)}, bf16[512,512]{1,0:T(8,128)(2,1)}, u32[]{:S(2)}) %copy-start) | copy-done | bytes 524312
  8.4 1.0 %copy-done.4 = bf16[512,512]{1,0:T(8,128)(2,1)S(1)} copy-done((bf16[512,512]{1,0:T(8,128)(2,1)S(1)}, bf16[512,512]{1,0:T(8,128)(2,1)}, u32[]{:S(2)}) %copy-start.4) | copy-done | bytes 524312
  9.4 1.0 %copy-done.6 = bf16[512,512]{1,0:T(8,128)(2,1)S(1)} copy-done((bf16[512,512]{1,0:T(8,128)(2,1)S(1)}, bf16[512,512]{1,0:T(8,128)(2,1)}, u32[]{:S(2)}) %copy-start.6) | copy-done | bytes 524312
  10.4 1.7 %gather_first.1 = (s32[1024,4]{1,0:T(8,128)S(1)}, f32[512,256]{1,0:T(8,128)S(1)}, f32[1024,512]{1,0:T(8,128)S(1)}, bf16[512,256]{1,0:T(8,128)(2,1)S(1)}) custom-call(s32[4]{0:T(128)S(1)} %pad_add_fusion.place_ref, s32[4,512]{1,0:T(4,128)S(1)} %select_reduce_fusion.links0_ref, s32[4,512]{1,0:T(4,128)S(1)} %slice.13.links1_ref, ...), custom_call_target="tpu_custom_call" | custom-call | tf_op jit(solution)/shard_map/gather_first/pallas_call | solution.py:255
  13.3 1.5 %gather_middle.1 = (f32[512,256]{1,0:T(8,128)S(1)}, f32[1024,512]{1,0:T(8,128)S(1)}) custom-call(s32[4]{0:T(128)S(1)} %pad_add_fusion.place_ref, s32[1024,4]{1,0:T(8,128)S(1)} %get-tuple-element.55.columns_ref, f32[1024,512]{1,0:T(8,128)S(1)} %get-tuple-element.49.h0_ref, bf16[512,512]{1,0:T(8,128)(2,1)S(1)} %collective-permute-done.1.t_ref.t1_ref, ...), custom_call_target="tpu_custom_call" | custom-call | tf_op jit(solution)/shard_map/gather_middle/pallas_call | solution.py:269
  14.8 1.6 %collective-permute-done.3.refs_0_ = bf16[512,512]{1,0:T(8,128)(2,1)S(1)} collective-permute-done((bf16[512,512]{1,0:T(8,128)(2,1)}, bf16[512,512]{1,0:T(8,128)(2,1)S(1)}, u32[]{:S(2)}, u32[]{:S(2)}) %collective-permute-start.3) | collective-permute-done | bytes 524320 | tf_op jit(solution)/shard_map/ppermute | solution.py:21
  16.5 0.8 %gather_more.1.h0_ref = f32[1024,512]{1,0:T(8,128)S(1)} custom-call(s32[1024,4]{1,0:T(8,128)S(1)} %get-tuple-element.55.columns_ref, f32[1024,512]{1,0:T(8,128)S(1)} %get-tuple-element.56.h0_ref, bf16[512,512]{1,0:T(8,128)(2,1)S(1)} %collective-permute-done.3.refs_0_), custom_call_target="tpu_custom_call" | custom-call | flops 536870912 | bytes 1048576 | tf_op jit(solution)/shard_map/gather_more/pallas_call | solution.py:282
  17.3 1.1 %collective-permute-done.5.refs_0_ = bf16[512,512]{1,0:T(8,128)(2,1)S(1)} collective-permute-done((bf16[512,512]{1,0:T(8,128)(2,1)S(1)}, bf16[512,512]{1,0:T(8,128)(2,1)S(1)}, u32[]{:S(2)}, u32[]{:S(2)}) %collective-permute-start.5) | collective-permute-done | bytes 524320 | tf_op jit(solution)/shard_map/ppermute | solution.py:21
  18.4 2.0 %forward.1 = (bf16[1024,512]{1,0:T(8,128)(2,1)S(1)}, bf16[1024,256]{1,0:T(8,128)(2,1)S(1)}, bf16[1024,256]{1,0:T(8,128)(2,1)S(1)}) custom-call(s32[4]{0:T(128)S(1)} %pad_add_fusion.place_ref, s32[2]{0:T(128)S(1)} %pad_add_fusion.1.lengths_ref, s32[1024,4]{1,0:T(8,128)S(1)} %get-tuple-element.55.columns_ref, f32[1024,512]{1,0:T(8,128)S(1)} %gather_more.1.h0_ref, ...), custom_call_target="tpu_custom_call" | custom-call | flops 1073741824 | bytes 1048576 | tf_op jit(solution)/shard_map/forward/pallas_call | solution.py:290
  21.1 1.3 %weight_terms.1 = (f32[256,256]{1,0:T(8,128)S(1)}, bf16[256,256]{1,0:T(8,128)(2,1)S(1)}, bf16[256,256]{1,0:T(8,128)(2,1)S(1)}, bf16[256,256]{1,0:T(8,128)(2,1)S(1)}) custom-call(s32[4]{0:T(128)S(1)} %pad_add_fusion.place_ref, bf16[512,512]{1,0:T(8,128)(2,1)S(1)} %copy-done.1, bf16[512,512]{1,0:T(8,128)(2,1)S(1)} %collective-permute-done.1.t_ref.t1_ref, ...), custom_call_target="tpu_custom_call" | custom-call | flops 536870912 | bytes 1048576 | tf_op jit(solution)/shard_map/weight_terms/pallas_call | solution.py:307
  22.4 1.8 %collective-permute-start.10 = (bf16[256,256]{1,0:T(8,128)(2,1)S(1)}, bf16[256,256]{1,0:T(8,128)(2,1)S(1)}, u32[]{:S(2)}, u32[]{:S(2)}) collective-permute-start(bf16[256,256]{1,0:T(8,128)(2,1)S(1)} %get-tuple-element.71), channel_id=1, source_target_pairs={{0,2},{1,3},{2,0},{3,1},{4,6},{5,7},{6,4},{7,5},{8,10},{9,11},{10,... | collective-permute-start | bytes 393224 | tf_op jit(solution)/shard_map/ppermute | solution.py:21
  24.3 1.4 %collective-permute-start.8 = (bf16[256,256]{1,0:T(8,128)(2,1)S(1)}, bf16[256,256]{1,0:T(8,128)(2,1)S(1)}, u32[]{:S(2)}, u32[]{:S(2)}) collective-permute-start(bf16[256,256]{1,0:T(8,128)(2,1)S(1)} %get-tuple-element.69), channel_id=1, source_target_pairs={{0,6},{1,7},{2,4},{3,5},{4,2},{5,3},{6,0},{7,1},{8,14},{9,15},{10,... | collective-permute-start | bytes 393224 | tf_op jit(solution)/shard_map/ppermute | solution.py:21
  26.0 2.0 %source_terms.1 = (f32[256,512]{1,0:T(8,128)S(1)}, bf16[256,512]{1,0:T(8,128)(2,1)S(1)}, f32[256,512]{1,0:T(8,128)S(1)}, bf16[256,512]{1,0:T(8,128)(2,1)S(1)}) custom-call(s32[4]{0:T(128)S(1)} %pad_add_fusion.place_ref, s32[2]{0:T(128)S(1)} %pad_add_fusion.1.lengths_ref, s32[4,512]{1,0:T(4,128)S(1)} %select_reduce_fusion.links0_ref, ...), custom_call_target="tpu_custom_call" | custom-call | flops 1073741824 | bytes 1048576 | tf_op jit(solution)/shard_map/source_terms/pallas_call | solution.py:326
  28.0 1.8 %collective-permute-start.15 = (bf16[256,512]{1,0:T(8,128)(2,1)S(1)}, bf16[256,512]{1,0:T(8,128)(2,1)S(1)}, u32[]{:S(2)}, u32[]{:S(2)}) collective-permute-start(bf16[256,512]{1,0:T(8,128)(2,1)S(1)} %get-tuple-element.68), channel_id=1, source_target_pairs={{0,4},{1,5},{2,6},{3,7},{4,0},{5,1},{6,2},{7,3},{8,12},{9,13},{10,... | collective-permute-start | bytes 786440 | tf_op jit(solution)/shard_map/ppermute | solution.py:21
  29.8 1.5 %collective-permute-start.13 = (bf16[256,512]{1,0:T(8,128)(2,1)S(1)}, bf16[256,512]{1,0:T(8,128)(2,1)S(1)}, u32[]{:S(2)}, u32[]{:S(2)}) collective-permute-start(bf16[256,512]{1,0:T(8,128)(2,1)S(1)} %get-tuple-element.66), channel_id=1, source_target_pairs={{0,2},{1,3},{2,0},{3,1},{4,6},{5,7},{6,4},{7,5},{8,10},{9,11},{10,... | collective-permute-start | bytes 786440 | tf_op jit(solution)/shard_map/ppermute | solution.py:21
  31.5 1.6 %collective-permute-done.9.refs_2_ = bf16[256,256]{1,0:T(8,128)(2,1)S(1)} collective-permute-done((bf16[256,256]{1,0:T(8,128)(2,1)S(1)}, bf16[256,256]{1,0:T(8,128)(2,1)S(1)}, u32[]{:S(2)}, u32[]{:S(2)}) %collective-permute-start.9) | collective-permute-done | bytes 131104 | tf_op jit(solution)/shard_map/ppermute | solution.py:21
  33.2 1.9 %collective-permute-start.11 = (bf16[256,256]{1,0:T(8,128)(2,1)S(1)}, bf16[256,256]{1,0:T(8,128)(2,1)S(1)}, u32[]{:S(2)}, u32[]{:S(2)}) collective-permute-start(bf16[256,256]{1,0:T(8,128)(2,1)S(1)} %weight_sum.3.refs_0_), channel_id=1, source_target_pairs={{0,8},{1,9},{2,10},{3,11},{4,12},{5,13},{6,14},{7,15},{8,0},{9,1},... | collective-permute-start | bytes 393224 | tf_op jit(solution)/shard_map/ppermute | solution.py:21
  35.1 3.1 %collective-permute-done.11.refs_1_ = bf16[256,256]{1,0:T(8,128)(2,1)S(1)} collective-permute-done((bf16[256,256]{1,0:T(8,128)(2,1)S(1)}, bf16[256,256]{1,0:T(8,128)(2,1)S(1)}, u32[]{:S(2)}, u32[]{:S(2)}) %collective-permute-start.11) | collective-permute-done | bytes 131104 | tf_op jit(solution)/shard_map/ppermute | solution.py:21
  38.3 3.2 %collective-permute-start.12 = (bf16[256,256]{1,0:T(8,128)(2,1)S(1)}, bf16[256,256]{1,0:T(8,128)(2,1)S(1)}, u32[]{:S(2)}, u32[]{:S(2)}) collective-permute-start(bf16[256,256]{1,0:T(8,128)(2,1)S(1)} %weight_sum.4.refs_0_), channel_id=1, source_target_pairs={{0,16},{1,17},{2,18},{3,19},{4,20},{5,21},{6,22},{7,23},{8,24},{9,... | collective-permute-start | bytes 393224 | tf_op jit(solution)/shard_map/ppermute | solution.py:21
  41.5 1.6 %collective-permute-start.16 = (bf16[128,512]{1,0:T(8,128)(2,1)S(1)}, bf16[128,512]{1,0:T(8,128)(2,1)S(1)}, u32[]{:S(2)}, u32[]{:S(2)}) collective-permute-start(bf16[128,512]{1,0:T(8,128)(2,1)S(1)} %get-tuple-element.83), channel_id=1, source_target_pairs={{0,2},{1,3},{2,0},{3,1},{4,6},{5,7},{6,4},{7,5},{8,10},{9,11},{10,... | collective-permute-start | bytes 393224 | tf_op jit(solution)/shard_map/ppermute | solution.py:21
  43.1 2.0 %target_side.1 = (bf16[512,512]{1,0:T(8,128)(2,1)}, bf16[512,512]{1,0:T(8,128)(2,1)}) custom-call(s32[4]{0:T(128)S(1)} %pad_add_fusion.place_ref, bf16[512,512]{1,0:T(8,128)(2,1)S(1)} %copy-done.5, bf16[512,512]{1,0:T(8,128)(2,1)S(1)} %copy-done.3, bf16[1024,256]{1,0:T(8,128)(2,1)S(1)} %get-tuple-element.61.grad_ref, ...), custom_call_target="tpu_custom_call" | custom-call | flops 268435456 | bytes 1048576 | tf_op jit(solution)/shard_map/target_side/pallas_call | solution.py:358
  45.2 1.5 %collective-permute-start.14 = (bf16[128,512]{1,0:T(8,128)(2,1)S(1)}, bf16[128,512]{1,0:T(8,128)(2,1)S(1)}, u32[]{:S(2)}, u32[]{:S(2)}) collective-permute-start(bf16[128,512]{1,0:T(8,128)(2,1)S(1)} %get-tuple-element.81), channel_id=1, source_target_pairs={{0,4},{1,5},{2,6},{3,7},{4,0},{5,1},{6,2},{7,3},{8,12},{9,13},{10,... | collective-permute-start | bytes 393224 | tf_op jit(solution)/shard_map/ppermute | solution.py:21
  47.5 1.5 %collective-permute-start.20 = (bf16[256,256]{1,0:T(8,128)(2,1)S(1)}, bf16[256,256]{1,0:T(8,128)(2,1)S(1)}, u32[]{:S(2)}, u32[]{:S(2)}) collective-permute-start(bf16[256,256]{1,0:T(8,128)(2,1)S(1)} %weight_sum.5.refs_0_), channel_id=1, source_target_pairs={{0,4},{1,5},{2,6},{3,7},{4,0},{5,1},{6,2},{7,3},{8,12},{9,13},{10,... | collective-permute-start | bytes 393224 | tf_op jit(solution)/shard_map/ppermute | solution.py:21
  49.0 1.3 %collective-permute-start.21 = (bf16[256,256]{1,0:T(8,128)(2,1)S(1)}, bf16[256,256]{1,0:T(8,128)(2,1)S(1)}, u32[]{:S(2)}, u32[]{:S(2)}) collective-permute-start(bf16[256,256]{1,0:T(8,128)(2,1)S(1)} %weight_sum.5.refs_0_), channel_id=1, source_target_pairs={{0,6},{1,7},{2,4},{3,5},{4,2},{5,3},{6,0},{7,1},{8,14},{9,15},{10,... | collective-permute-start | bytes 393224 | tf_op jit(solution)/shard_map/ppermute | solution.py:21
  50.3 1.4 %collective-permute-start.17 = (bf16[128,512]{1,0:T(8,128)(2,1)S(1)}, bf16[128,512]{1,0:T(8,128)(2,1)S(1)}, u32[]{:S(2)}, u32[]{:S(2)}) collective-permute-start(bf16[128,512]{1,0:T(8,128)(2,1)S(1)} %source_sum.8), channel_id=1, source_target_pairs={{0,8},{1,9},{2,10},{3,11},{4,12},{5,13},{6,14},{7,15},{8,0},{9,1},... | collective-permute-start | bytes 393224 | tf_op jit(solution)/shard_map/ppermute | solution.py:21
  52.5 2.4 %collective-permute-done.21.refs_3_ = bf16[256,256]{1,0:T(8,128)(2,1)S(1)} collective-permute-done((bf16[256,256]{1,0:T(8,128)(2,1)S(1)}, bf16[256,256]{1,0:T(8,128)(2,1)S(1)}, u32[]{:S(2)}, u32[]{:S(2)}) %collective-permute-start.21) | collective-permute-done | bytes 131104 | tf_op jit(solution)/shard_map/ppermute | solution.py:21
  55.4 1.4 %collective-permute-start.18 = (bf16[64,512]{1,0:T(8,128)(2,1)S(1)}, bf16[64,512]{1,0:T(8,128)(2,1)S(1)}, u32[]{:S(2)}, u32[]{:S(2)}) collective-permute-start(bf16[64,512]{1,0:T(8,128)(2,1)S(1)} %get-tuple-element.85), channel_id=1, source_target_pairs={{0,16},{1,17},{2,18},{3,19},{4,20},{5,21},{6,22},{7,23},{8,24},{9,... | collective-permute-start | bytes 196616 | tf_op jit(solution)/shard_map/ppermute | solution.py:21
  56.8 1.9 %finish_weights.1 = (f32[512,512]{1,0:T(8,128)}, f32[512,512]{1,0:T(8,128)}) custom-call(s32[4]{0:T(128)S(1)} %pad_add_fusion.place_ref, bf16[256,256]{1,0:T(8,128)(2,1)S(1)} %weight_sum.5.refs_0_, bf16[256,256]{1,0:T(8,128)(2,1)S(1)} %collective-permute-done.19.refs_1_, bf16[256,256]{1,0:T(8,128)(2,1)S(1)} %collective-permute-done.20.refs_2_, ...), custom_call_target="tpu_custom_call" | custom-call | bytes 1048576 | tf_op jit(solution)/shard_map/finish_weights/pallas_call | solution.py:386
  58.8 3.3 %collective-permute-done.18.received_ref = bf16[64,512]{1,0:T(8,128)(2,1)S(1)} collective-permute-done((bf16[64,512]{1,0:T(8,128)(2,1)S(1)}, bf16[64,512]{1,0:T(8,128)(2,1)S(1)}, u32[]{:S(2)}, u32[]{:S(2)}) %collective-permute-start.18) | collective-permute-done | bytes 65568 | tf_op jit(solution)/shard_map/ppermute | solution.py:21
  62.0 0.9 %finish_source.1 = bf16[64,512]{1,0:T(8,128)(2,1)} custom-call(bf16[512,512]{1,0:T(8,128)(2,1)S(1)} %copy-done.2, f32[64,512]{1,0:T(8,128)S(1)} %get-tuple-element.84.own_ref, bf16[64,512]{1,0:T(8,128)(2,1)S(1)} %collective-permute-done.18.received_ref), custom_call_target="tpu_custom_call" | custom-call | bytes 1048576 | tf_op jit(solution)/shard_map/finish_source/pallas_call | solution.py:375
  (60 shorter events, 7.4 us)
Async XLA Ops:
  0.6 12.7 %collective-permute-start.2 = (bf16[512,512]{1,0:T(8,128)(2,1)}, bf16[512,512]{1,0:T(8,128)(2,1)S(1)}, u32[]{:S(2)}, u32[]{:S(2)}) collective-permute-start(bf16[512,512]{1,0:T(8,128)(2,1)} %s_ref.1), channel_id=1, source_target_pairs={{0,1},{1,0},{2,3},{3,2},{4,5},{5,4},{6,7},{7,6},{8,9},{9,8},{10,11... | collective-permute-start | bytes 1572872 | tf_op jit(solution)/shard_map/ppermute | solution.py:21
  1.1 15.3 %collective-permute-start.3 = (bf16[512,512]{1,0:T(8,128)(2,1)}, bf16[512,512]{1,0:T(8,128)(2,1)S(1)}, u32[]{:S(2)}, u32[]{:S(2)}) collective-permute-start(bf16[512,512]{1,0:T(8,128)(2,1)} %s_ref.1), channel_id=1, source_target_pairs={{0,2},{1,3},{2,0},{3,1},{4,6},{5,7},{6,4},{7,5},{8,10},{9,11},{10,... | collective-permute-start | bytes 1572872 | tf_op jit(solution)/shard_map/ppermute | solution.py:21
  3.7 9.6 %collective-permute-start.1 = (bf16[512,512]{1,0:T(8,128)(2,1)}, bf16[512,512]{1,0:T(8,128)(2,1)S(1)}, u32[]{:S(2)}, u32[]{:S(2)}) collective-permute-start(bf16[512,512]{1,0:T(8,128)(2,1)} %t0_ref.3), channel_id=1, source_target_pairs={{0,1},{1,0},{2,3},{3,2},{4,5},{5,4},{6,7},{7,6},{8,9},{9,8},{10,11... | collective-permute-start | bytes 1572872 | tf_op jit(solution)/shard_map/ppermute | solution.py:21
  6.1 1.3 %collective-permute-start = (s32[8,512]{1,0:T(8,128)S(1)}, s32[8,512]{1,0:T(8,128)S(1)}, u32[]{:S(2)}, u32[]{:S(2)}) collective-permute-start(s32[8,512]{1,0:T(8,128)S(1)} %concatenate.3), channel_id=1, source_target_pairs={{0,1},{1,0},{2,3},{3,2},{4,5},{5,4},{6,7},{7,6},{8,9},{9,8},{10,11... | collective-permute-start | bytes 49160 | tf_op jit(solution)/shard_map/ppermute | solution.py:21
  6.5 10.8 %collective-permute-start.4 = (bf16[512,512]{1,0:T(8,128)(2,1)}, bf16[512,512]{1,0:T(8,128)(2,1)S(1)}, u32[]{:S(2)}, u32[]{:S(2)}) collective-permute-start(bf16[512,512]{1,0:T(8,128)(2,1)} %cot_ref.1), channel_id=1, source_target_pairs={{0,1},{1,0},{2,3},{3,2},{4,5},{5,4},{6,7},{7,6},{8,9},{9,8},{10,11... | collective-permute-start | bytes 1572872 | tf_op jit(solution)/shard_map/ppermute | solution.py:21
  7.3 1.0 %copy-start = (bf16[512,512]{1,0:T(8,128)(2,1)S(1)}, bf16[512,512]{1,0:T(8,128)(2,1)}, u32[]{:S(2)}) copy-start(bf16[512,512]{1,0:T(8,128)(2,1)} %t0_ref.3) | copy-start | bytes 1572868
  8.4 1.0 %copy-start.4 = (bf16[512,512]{1,0:T(8,128)(2,1)S(1)}, bf16[512,512]{1,0:T(8,128)(2,1)}, u32[]{:S(2)}) copy-start(bf16[512,512]{1,0:T(8,128)(2,1)} %ws_ref.3) | copy-start | bytes 1572868
  16.5 1.9 %copy-start.1 = (bf16[512,512]{1,0:T(8,128)(2,1)S(1)}, bf16[512,512]{1,0:T(8,128)(2,1)}, u32[]{:S(2)}) copy-start(bf16[512,512]{1,0:T(8,128)(2,1)} %t0_ref.3) | copy-start | bytes 1572868
  16.5 1.9 %copy-start.2 = (bf16[512,512]{1,0:T(8,128)(2,1)S(1)}, bf16[512,512]{1,0:T(8,128)(2,1)}, u32[]{:S(2)}) copy-start(bf16[512,512]{1,0:T(8,128)(2,1)} %wm_ref.3) | copy-start | bytes 1572868
  16.5 1.9 %copy-start.3 = (bf16[512,512]{1,0:T(8,128)(2,1)S(1)}, bf16[512,512]{1,0:T(8,128)(2,1)}, u32[]{:S(2)}) copy-start(bf16[512,512]{1,0:T(8,128)(2,1)} %cot_ref.1) | copy-start | bytes 1572868
  16.5 1.9 %collective-permute-start.5 = (bf16[512,512]{1,0:T(8,128)(2,1)S(1)}, bf16[512,512]{1,0:T(8,128)(2,1)S(1)}, u32[]{:S(2)}, u32[]{:S(2)}) collective-permute-start(bf16[512,512]{1,0:T(8,128)(2,1)S(1)} %collective-permute-done.3.refs_0_), channel_id=1, source_target_pairs={{0,1},{1,0},{2,3},{3,2},{4,5},{5,4},{6,7},{7,6},{8,9},{9,8},{10,11... | collective-permute-start | bytes 1572872 | tf_op jit(solution)/shard_map/ppermute | solution.py:21
  20.4 5.6 %collective-permute-start.6 = (bf16[1024,256]{1,0:T(8,128)(2,1)S(1)}, bf16[1024,256]{1,0:T(8,128)(2,1)S(1)}, u32[]{:S(2)}, u32[]{:S(2)}) collective-permute-start(bf16[1024,256]{1,0:T(8,128)(2,1)S(1)} %get-tuple-element.61.grad_ref), channel_id=1, source_target_pairs={{0,1},{1,0},{2,3},{3,2},{4,5},{5,4},{6,7},{7,6},{8,9},{9,8},{10,11... | collective-permute-start | bytes 1572872 | tf_op jit(solution)/shard_map/ppermute | solution.py:21
  20.7 5.3 %collective-permute-start.7 = (bf16[512,256]{1,0:T(8,128)(2,1)S(1)}, bf16[512,256]{1,0:T(8,128)(2,1)S(1)}, u32[]{:S(2)}, u32[]{:S(2)}) collective-permute-start(bf16[512,256]{1,0:T(8,128)(2,1)S(1)} %slice.12), channel_id=1, source_target_pairs={{0,1},{1,0},{2,3},{3,2},{4,5},{5,4},{6,7},{7,6},{8,9},{9,8},{10,11... | collective-permute-start | bytes 786440 | tf_op jit(solution)/shard_map/ppermute | solution.py:21
  22.4 8.9 %collective-permute-start.10 = (bf16[256,256]{1,0:T(8,128)(2,1)S(1)}, bf16[256,256]{1,0:T(8,128)(2,1)S(1)}, u32[]{:S(2)}, u32[]{:S(2)}) collective-permute-start(bf16[256,256]{1,0:T(8,128)(2,1)S(1)} %get-tuple-element.71), channel_id=1, source_target_pairs={{0,2},{1,3},{2,0},{3,1},{4,6},{5,7},{6,4},{7,5},{8,10},{9,11},{10,... | collective-permute-start | bytes 393224 | tf_op jit(solution)/shard_map/ppermute | solution.py:21
  24.3 7.3 %collective-permute-start.8 = (bf16[256,256]{1,0:T(8,128)(2,1)S(1)}, bf16[256,256]{1,0:T(8,128)(2,1)S(1)}, u32[]{:S(2)}, u32[]{:S(2)}) collective-permute-start(bf16[256,256]{1,0:T(8,128)(2,1)S(1)} %get-tuple-element.69), channel_id=1, source_target_pairs={{0,6},{1,7},{2,4},{3,5},{4,2},{5,3},{6,0},{7,1},{8,14},{9,15},{10,... | collective-permute-start | bytes 393224 | tf_op jit(solution)/shard_map/ppermute | solution.py:21
  25.7 17.4 %copy-start.5 = (bf16[512,512]{1,0:T(8,128)(2,1)S(1)}, bf16[512,512]{1,0:T(8,128)(2,1)}, u32[]{:S(2)}) copy-start(bf16[512,512]{1,0:T(8,128)(2,1)} %ws_ref.3) | copy-start | bytes 1572868
  25.7 7.4 %collective-permute-start.9 = (bf16[256,256]{1,0:T(8,128)(2,1)S(1)}, bf16[256,256]{1,0:T(8,128)(2,1)S(1)}, u32[]{:S(2)}, u32[]{:S(2)}) collective-permute-start(bf16[256,256]{1,0:T(8,128)(2,1)S(1)} %get-tuple-element.70), channel_id=1, source_target_pairs={{0,4},{1,5},{2,6},{3,7},{4,0},{5,1},{6,2},{7,3},{8,12},{9,13},{10,... | collective-permute-start | bytes 393224 | tf_op jit(solution)/shard_map/ppermute | solution.py:21
  28.0 13.5 %collective-permute-start.15 = (bf16[256,512]{1,0:T(8,128)(2,1)S(1)}, bf16[256,512]{1,0:T(8,128)(2,1)S(1)}, u32[]{:S(2)}, u32[]{:S(2)}) collective-permute-start(bf16[256,512]{1,0:T(8,128)(2,1)S(1)} %get-tuple-element.68), channel_id=1, source_target_pairs={{0,4},{1,5},{2,6},{3,7},{4,0},{5,1},{6,2},{7,3},{8,12},{9,13},{10,... | collective-permute-start | bytes 786440 | tf_op jit(solution)/shard_map/ppermute | solution.py:21
  29.8 15.3 %collective-permute-start.13 = (bf16[256,512]{1,0:T(8,128)(2,1)S(1)}, bf16[256,512]{1,0:T(8,128)(2,1)S(1)}, u32[]{:S(2)}, u32[]{:S(2)}) collective-permute-start(bf16[256,512]{1,0:T(8,128)(2,1)S(1)} %get-tuple-element.66), channel_id=1, source_target_pairs={{0,2},{1,3},{2,0},{3,1},{4,6},{5,7},{6,4},{7,5},{8,10},{9,11},{10,... | collective-permute-start | bytes 786440 | tf_op jit(solution)/shard_map/ppermute | solution.py:21
  33.2 5.0 %collective-permute-start.11 = (bf16[256,256]{1,0:T(8,128)(2,1)S(1)}, bf16[256,256]{1,0:T(8,128)(2,1)S(1)}, u32[]{:S(2)}, u32[]{:S(2)}) collective-permute-start(bf16[256,256]{1,0:T(8,128)(2,1)S(1)} %weight_sum.3.refs_0_), channel_id=1, source_target_pairs={{0,8},{1,9},{2,10},{3,11},{4,12},{5,13},{6,14},{7,15},{8,0},{9,1},... | collective-permute-start | bytes 393224 | tf_op jit(solution)/shard_map/ppermute | solution.py:21
  38.3 8.4 %collective-permute-start.12 = (bf16[256,256]{1,0:T(8,128)(2,1)S(1)}, bf16[256,256]{1,0:T(8,128)(2,1)S(1)}, u32[]{:S(2)}, u32[]{:S(2)}) collective-permute-start(bf16[256,256]{1,0:T(8,128)(2,1)S(1)} %weight_sum.4.refs_0_), channel_id=1, source_target_pairs={{0,16},{1,17},{2,18},{3,19},{4,20},{5,21},{6,22},{7,23},{8,24},{9,... | collective-permute-start | bytes 393224 | tf_op jit(solution)/shard_map/ppermute | solution.py:21
  41.5 8.7 %collective-permute-start.16 = (bf16[128,512]{1,0:T(8,128)(2,1)S(1)}, bf16[128,512]{1,0:T(8,128)(2,1)S(1)}, u32[]{:S(2)}, u32[]{:S(2)}) collective-permute-start(bf16[128,512]{1,0:T(8,128)(2,1)S(1)} %get-tuple-element.83), channel_id=1, source_target_pairs={{0,2},{1,3},{2,0},{3,1},{4,6},{5,7},{6,4},{7,5},{8,10},{9,11},{10,... | collective-permute-start | bytes 393224 | tf_op jit(solution)/shard_map/ppermute | solution.py:21
  45.2 6.5 %collective-permute-start.14 = (bf16[128,512]{1,0:T(8,128)(2,1)S(1)}, bf16[128,512]{1,0:T(8,128)(2,1)S(1)}, u32[]{:S(2)}, u32[]{:S(2)}) collective-permute-start(bf16[128,512]{1,0:T(8,128)(2,1)S(1)} %get-tuple-element.81), channel_id=1, source_target_pairs={{0,4},{1,5},{2,6},{3,7},{4,0},{5,1},{6,2},{7,3},{8,12},{9,13},{10,... | collective-permute-start | bytes 393224 | tf_op jit(solution)/shard_map/ppermute | solution.py:21
  46.7 5.0 %collective-permute-start.19 = (bf16[256,256]{1,0:T(8,128)(2,1)S(1)}, bf16[256,256]{1,0:T(8,128)(2,1)S(1)}, u32[]{:S(2)}, u32[]{:S(2)}) collective-permute-start(bf16[256,256]{1,0:T(8,128)(2,1)S(1)} %weight_sum.5.refs_0_), channel_id=1, source_target_pairs={{0,2},{1,3},{2,0},{3,1},{4,6},{5,7},{6,4},{7,5},{8,10},{9,11},{10,... | collective-permute-start | bytes 393224 | tf_op jit(solution)/shard_map/ppermute | solution.py:21
  47.5 5.0 %collective-permute-start.20 = (bf16[256,256]{1,0:T(8,128)(2,1)S(1)}, bf16[256,256]{1,0:T(8,128)(2,1)S(1)}, u32[]{:S(2)}, u32[]{:S(2)}) collective-permute-start(bf16[256,256]{1,0:T(8,128)(2,1)S(1)} %weight_sum.5.refs_0_), channel_id=1, source_target_pairs={{0,4},{1,5},{2,6},{3,7},{4,0},{5,1},{6,2},{7,3},{8,12},{9,13},{10,... | collective-permute-start | bytes 393224 | tf_op jit(solution)/shard_map/ppermute | solution.py:21
  49.0 5.9 %collective-permute-start.21 = (bf16[256,256]{1,0:T(8,128)(2,1)S(1)}, bf16[256,256]{1,0:T(8,128)(2,1)S(1)}, u32[]{:S(2)}, u32[]{:S(2)}) collective-permute-start(bf16[256,256]{1,0:T(8,128)(2,1)S(1)} %weight_sum.5.refs_0_), channel_id=1, source_target_pairs={{0,6},{1,7},{2,4},{3,5},{4,2},{5,3},{6,0},{7,1},{8,14},{9,15},{10,... | collective-permute-start | bytes 393224 | tf_op jit(solution)/shard_map/ppermute | solution.py:21
  50.3 5.0 %collective-permute-start.17 = (bf16[128,512]{1,0:T(8,128)(2,1)S(1)}, bf16[128,512]{1,0:T(8,128)(2,1)S(1)}, u32[]{:S(2)}, u32[]{:S(2)}) collective-permute-start(bf16[128,512]{1,0:T(8,128)(2,1)S(1)} %source_sum.8), channel_id=1, source_target_pairs={{0,8},{1,9},{2,10},{3,11},{4,12},{5,13},{6,14},{7,15},{8,0},{9,1},... | collective-permute-start | bytes 393224 | tf_op jit(solution)/shard_map/ppermute | solution.py:21
  51.7 5.1 %collective-permute-start.22 = (bf16[256,256]{1,0:T(8,128)(2,1)S(1)}, bf16[256,256]{1,0:T(8,128)(2,1)S(1)}, u32[]{:S(2)}, u32[]{:S(2)}) collective-permute-start(bf16[256,256]{1,0:T(8,128)(2,1)S(1)} %weight_sum.5.refs_0_), channel_id=1, source_target_pairs={{0,1},{1,0},{2,3},{3,2},{4,5},{5,4},{6,7},{7,6},{8,9},{9,8},{10,11... | collective-permute-start | bytes 393224 | tf_op jit(solution)/shard_map/ppermute | solution.py:21
  51.8 5.0 %collective-permute-start.23 = (bf16[256,256]{1,0:T(8,128)(2,1)S(1)}, bf16[256,256]{1,0:T(8,128)(2,1)S(1)}, u32[]{:S(2)}, u32[]{:S(2)}) collective-permute-start(bf16[256,256]{1,0:T(8,128)(2,1)S(1)} %collective-permute-done.19.refs_1_), channel_id=1, source_target_pairs={{0,1},{1,0},{2,3},{3,2},{4,5},{5,4},{6,7},{7,6},{8,9},{9,8},{10,11... | collective-permute-start | bytes 393224 | tf_op jit(solution)/shard_map/ppermute | solution.py:21
  52.5 4.3 %collective-permute-start.24 = (bf16[256,256]{1,0:T(8,128)(2,1)S(1)}, bf16[256,256]{1,0:T(8,128)(2,1)S(1)}, u32[]{:S(2)}, u32[]{:S(2)}) collective-permute-start(bf16[256,256]{1,0:T(8,128)(2,1)S(1)} %collective-permute-done.20.refs_2_), channel_id=1, source_target_pairs={{0,1},{1,0},{2,3},{3,2},{4,5},{5,4},{6,7},{7,6},{8,9},{9,8},{10,11... | collective-permute-start | bytes 393224 | tf_op jit(solution)/shard_map/ppermute | solution.py:21
  54.9 1.9 %collective-permute-start.25 = (bf16[256,256]{1,0:T(8,128)(2,1)S(1)}, bf16[256,256]{1,0:T(8,128)(2,1)S(1)}, u32[]{:S(2)}, u32[]{:S(2)}) collective-permute-start(bf16[256,256]{1,0:T(8,128)(2,1)S(1)} %collective-permute-done.21.refs_3_), channel_id=1, source_target_pairs={{0,1},{1,0},{2,3},{3,2},{4,5},{5,4},{6,7},{7,6},{8,9},{9,8},{10,11... | collective-permute-start | bytes 393224 | tf_op jit(solution)/shard_map/ppermute | solution.py:21
  55.4 6.6 %collective-permute-start.18 = (bf16[64,512]{1,0:T(8,128)(2,1)S(1)}, bf16[64,512]{1,0:T(8,128)(2,1)S(1)}, u32[]{:S(2)}, u32[]{:S(2)}) collective-permute-start(bf16[64,512]{1,0:T(8,128)(2,1)S(1)} %get-tuple-element.85), channel_id=1, source_target_pairs={{0,16},{1,17},{2,18},{3,19},{4,20},{5,21},{6,22},{7,23},{8,24},{9,... | collective-permute-start | bytes 196616 | tf_op jit(solution)/shard_map/ppermute | solution.py:21
  (1 other events, 1.0 us)

commit v3 on v2

v3 whole, which is shorter than its diff:
```python
import functools

import jax
import jax.numpy as jnp
from jax import lax
from jax.experimental import pallas as pl
from jax.experimental.pallas import tpu as pltpu
from jax.sharding import PartitionSpec as P

AXES = ("row", "blk")
BF16 = jnp.bfloat16
F32 = jnp.float32
VMEM = pl.BlockSpec(memory_space=pltpu.VMEM)
HBM = pl.BlockSpec(memory_space=pltpu.HBM)
ROWS = ((0,), (0,))
LANES = ((1,), (1,))


def swap(value, mask, devices):
    return lax.ppermute(value, AXES, [(i, i ^ mask) for i in range(devices)])


def call(body, name, out_shape, inputs=0, flops=0, moved=1 << 20, **more):
    return pl.pallas_call(
        body,
        name=name,
        in_specs=[VMEM] * inputs,
        out_shape=out_shape,
        compiler_params=pltpu.CompilerParams(vmem_limit_bytes=20 << 20),
        cost_estimate=pl.CostEstimate(flops=flops, bytes_accessed=moved, transcendentals=0),
        **more,
    )


def shaped(shape, dtype):
    return jax.ShapeDtypeStruct(shape, dtype)


def mm(a, b, dims=((1,), (0,))):
    return lax.dot_general(a, b, (dims, ((), ())), preferred_element_type=F32)


def pattern(rows, lanes):
    return (rows == lanes).astype(F32).astype(BF16)


def here():
    row, block = lax.axis_index("row"), lax.axis_index("blk")
    sides = lax.axis_size("blk") // 2
    return block % 2, (row % 2) * sides + block // 2, row // 2, block


def part(ref, core):
    half = ref.shape[1] // 2
    return ref[:, pl.ds(pl.multiple_of(core * half, half), half)]


def inverse(links_ref, width):
    return 1.0 / links_ref[links_ref.shape[0] - 1 :, 0:width].astype(F32)


def linked(column, s_ref):
    lanes = lax.broadcasted_iota(jnp.int32, (column.shape[0], s_ref.shape[0]), 1)
    return mm(pattern(column, lanes), s_ref[...])


def gather_first(links0_ref, links1_ref, s_ref, t_ref, ws_ref, columns_ref, own_ref, h_ref, weight_ref, near_ref):
    core, _, _, block = here()
    rows = t_ref.shape[0]
    weight = part(ws_ref, core)
    weight_ref[...] = weight
    own_ref[...] = mm(t_ref[...], weight)
    for i, links_ref in enumerate((links0_ref, links1_ref)):
        span = pl.ds(i * rows, rows)
        for m in range(near_ref.shape[0]):
            near_ref[m : m + 1, :] = links_ref[pl.ds(block ^ m, 1), :]
        columns = near_ref[...].T
        columns_ref[span, :] = columns
        h_ref[span, :] = linked(columns[:, 0:1], s_ref)


def gather_more(order, columns_ref, h0_ref, t_ref, weight_ref, *refs):
    s_refs, own_ref, h_ref = refs[:-2], refs[-2], refs[-1]
    own_ref[...] = mm(t_ref[...], weight_ref[...])
    rows = t_ref.shape[0]
    for i in range(2):
        span = pl.ds(i * rows, rows)
        total = h0_ref[span, :]
        for m, s_ref in zip(order, s_refs):
            total = total + linked(columns_ref[span, m : m + 1], s_ref)
        h_ref[span, :] = total


def forward(order, links0_ref, links1_ref, columns_ref, h0_ref, own0_ref, own1_ref, wm_ref, t0_ref, t1_ref, c0_ref, c1_ref, *refs):
    s_refs, (h_ref, grad_ref, *updated_refs) = refs[:-4], refs[-4:]
    core = here()[0]
    rows, width = t0_ref.shape
    weight = part(wm_ref, core)
    sides = ((links0_ref, t0_ref, c0_ref, own0_ref), (links1_ref, t1_ref, c1_ref, own1_ref))
    for i, (links_ref, t_ref, c_ref, own_ref) in enumerate(sides):
        span = pl.ds(i * rows, rows)
        total = h0_ref[span, :]
        for m, s_ref in zip(order, s_refs):
            total = total + linked(columns_ref[span, m : m + 1], s_ref)
        gathered = (total * inverse(links_ref, width)).astype(BF16)
        h_ref[span, :] = gathered
        preact = own_ref[...] + mm(gathered, weight)
        sig = jax.nn.sigmoid(preact)
        updated_refs[i][...] = (part(t_ref, core).astype(F32) + preact * sig).astype(BF16)
        upstream = part(c_ref, core).astype(F32)
        grad_ref[span, :] = (upstream * sig * (1.0 + preact * (1.0 - sig))).astype(BF16)


def weight_terms(t0_ref, t1_ref, h_ref, grad_ref, *refs):
    own_ref, sent_refs, total_ref = refs[0], refs[1:-1], refs[-1]
    quad = here()[1]
    rows, width = t0_ref.shape
    piece = own_ref.shape[0]
    total_ref[0:width, :] = mm(t0_ref[...], grad_ref[0:rows, :], ROWS) + mm(t1_ref[...], grad_ref[rows:, :], ROWS)
    total_ref[width:, :] = mm(h_ref[...], grad_ref[...], ROWS)
    for m, ref in enumerate((own_ref, *sent_refs)):
        at = pl.multiple_of((quad ^ m) * piece, piece)
        ref[...] = total_ref[pl.ds(at, piece), :].astype(ref.dtype)


def source_terms(share, sides, orders, links0_ref, links1_ref, grad_ref, other_ref, *refs):
    core, quad, layer, _ = here()
    targets = links0_ref.shape[1]
    half = grad_ref.shape[1]
    rows = 2 * refs[0].shape[0] // len(orders[0])
    position = lax.broadcasted_iota(jnp.int32, (rows, targets), 0)
    inverses = [inverse(ref, half) for ref in (links0_ref, links1_ref)]
    for n, order in enumerate(orders):
        far = position // share + n * (rows // share)
        inside = (layer ^ far) * (2 * share) + position % share
        for j, m in enumerate(order):
            ref = refs[2 * n + j // (len(order) // 2)]
            at = (j % (len(order) // 2)) * rows
            to = quad ^ m
            row_at = inside + (to // sides) * share
            block = (to % sides) * 2 + core
            totals = [None, None]
            for i, links_ref in enumerate((links0_ref, links1_ref)):
                chosen = pattern(links_ref[pl.ds(block, 1), :], row_at)
                for c, g_ref in enumerate((grad_ref, other_ref)):
                    at_target = (i ^ c) * targets
                    added = mm(chosen, g_ref[at_target : at_target + targets, :]) * inverses[i]
                    totals[c] = added if totals[c] is None else totals[c] + added
            first = core == 0
            ref[at : at + rows, 0:half] = jnp.where(first, totals[0], totals[1]).astype(ref.dtype)
            ref[at : at + rows, half:] = jnp.where(first, totals[1], totals[0]).astype(ref.dtype)


def halve(own_ref, received_ref, *refs):
    rows = refs[0].shape[0]
    for n, ref in enumerate(refs):
        span = pl.ds(n * rows, rows)
        ref[...] = (own_ref[span, :] + received_ref[span, :].astype(F32)).astype(ref.dtype)


def add_up(*refs):
    total = refs[0][...].astype(F32)
    for ref in refs[1:-1]:
        total = total + ref[...].astype(F32)
    refs[-1][...] = total.astype(BF16)


def finish_source(wm_ref, own_ref, received_ref, out_ref):
    total = (own_ref[...] + received_ref[...].astype(F32)).astype(BF16)
    out_ref[...] = mm(total, wm_ref[...], LANES).astype(BF16)


def target_side(ws_ref, cot_ref, grad_ref, grad_received_ref, held_ref, held_received_ref, out_ref, updated_ref):
    core = here()[0]
    rows = cot_ref.shape[0]
    out_ref[...] = (
        cot_ref[...].astype(F32)
        + mm(grad_ref[0:rows, :], part(ws_ref, core), LANES)
        + mm(grad_received_ref[rows:, :], part(ws_ref, 1 - core), LANES)
    ).astype(BF16)
    half = held_ref.shape[1]
    updated_ref[:, pl.ds(pl.multiple_of(core * half, half), half)] = held_ref[...]
    updated_ref[:, pl.ds(pl.multiple_of((1 - core) * half, half), half)] = held_received_ref[...]


def finish_weights(quads, scales, *refs):
    refs, outs, buffer, sems = refs[: 2 * quads], refs[-4:-2], refs[-2], refs[-1]
    core, quad, _, _ = here()
    count = quads // 2
    rows, half = refs[0].shape

    def copies(n):
        slot = quad ^ (n % quads)
        column = pl.multiple_of((core if n < quads else 1 - core) * half, half)
        row = pl.multiple_of((slot % count) * rows, rows)
        return slot // count, [
            pltpu.make_async_copy(buffer.at[n], out.at[pl.ds(row, rows), pl.ds(column, half)], sems.at[n]) for out in outs
        ]

    for n, ref in enumerate(refs):
        which, pair = copies(n)
        buffer[n] = ref[...].astype(F32) * jnp.where(which == 0, scales[0], scales[1])
        for k in range(2):
            pl.when(which == k)(pair[k].start)
    for n in range(2 * quads):
        which, pair = copies(n)
        for k in range(2):
            pl.when(which == k)(pair[k].wait)


def local(row_devices, blk_devices, source_table, target_table, message_weight, self_weight, tile_lists, key_offsets, list_lengths, cotangent):
    devices = row_devices * blk_devices
    targets, width = target_table.shape
    block_rows = source_table.shape[0]
    slots = tile_lists.shape[1]
    assert tile_lists.shape[0] == 1 and block_rows == targets and slots == blk_devices
    half = width // 2
    sides = blk_devices // 2
    quads = blk_devices
    layers = row_devices // 2
    share = block_rows // row_devices
    square = 2 * targets * width * width

    direct = list(range(2, blk_devices, 2))
    held = {m: swap(source_table, m, devices) for m in direct}

    blocks = lax.iota(jnp.int32, blk_devices)
    used = (tile_lists[0][None, :] == blocks[:, None]) & (lax.iota(jnp.int32, slots)[None, :] < list_lengths[0])
    links = jnp.max(jnp.where(used[:, :, None], key_offsets.T[None, :, :], -1), axis=1)
    links = jnp.concatenate([links, jnp.broadcast_to(list_lengths[:, None], (8 - slots % 8, targets))], axis=0)
    their_links = swap(links, 1, devices)

    table0, cot0 = target_table, cotangent
    held[1] = swap(source_table, 1, devices)
    table1 = swap(table0, 1, devices)
    cot1 = swap(cot0, 1, devices)

    columns, own0, gathered, weight = call(
        gather_first,
        "gather_first",
        (
            shaped((2 * targets, slots), jnp.int32),
            shaped((targets, half), F32),
            shaped((2 * targets, width), F32),
            shaped((width, half), BF16),
        ),
        inputs=5,
        moved=0,
        scratch_shapes=[pltpu.VMEM((slots, targets), jnp.int32)],
    )(links, their_links, source_table, table0, self_weight)
    ready = lax.optimization_barrier((columns, own0, gathered, weight, *[held[m] for m in direct]))
    columns, own0, gathered, weight = ready[:4]
    for m, value in zip(direct, ready[4:]):
        held[m] = value
        held[m + 1] = swap(value, 1, devices)
    order = [1, *direct]
    own1, gathered = call(
        functools.partial(gather_more, order),
        "gather_more",
        (shaped((targets, half), F32), shaped((2 * targets, width), F32)),
        inputs=4 + len(order),
        flops=2 * square,
    )(columns, gathered, table1, weight, *[held[m] for m in order])
    order = [m + 1 for m in direct]
    gathered, grad, updated, updated_there = call(
        functools.partial(forward, order),
        "forward",
        (shaped((2 * targets, width), BF16), shaped((2 * targets, half), BF16)) + (shaped((targets, half), BF16),) * 2,
        inputs=11 + len(order),
        flops=2 * sides * square,
    )(
        links, their_links, columns, gathered, own0, own1, message_weight, table0, table1, cot0, cot1,
        *[held[m] for m in order],
    )

    piece = 2 * width // quads
    terms = call(
        weight_terms,
        "weight_terms",
        [shaped((piece, half), F32)] + [shaped((piece, half), BF16)] * (quads - 1),
        inputs=4,
        flops=2 * square,
        scratch_shapes=[pltpu.VMEM((2 * width, half), F32)],
    )(table0, table1, gathered, grad)
    received = [swap(terms[m], 2 * m, devices) for m in reversed(range(1, quads))]

    terms, grad_sent, updated_there = lax.optimization_barrier((terms, grad, updated_there))
    grad_received = swap(grad_sent, 1, devices)
    updated_received = swap(updated_there, 1, devices)
    masks = [1 << i for i in range(quads.bit_length() - 1)]
    routes = (masks, masks[::-1])
    orders = [[sum(mask * ((j >> (len(masks) - 1 - i)) & 1) for i, mask in enumerate(route)) for j in range(quads)] for route in routes]
    half_rows = layers * share // 2
    count = quads // 2 * half_rows
    terms, grad_received = lax.optimization_barrier((terms, grad_received))
    sources = call(
        functools.partial(source_terms, share, sides, orders),
        "source_terms",
        [shaped((count, width), F32), shaped((count, width), BF16)] * 2,
        inputs=4,
        flops=4 * square,
    )(links, their_links, grad, grad_received)
    _, received = lax.optimization_barrier((sources, received))

    state = [[sources[0], sources[1]], [sources[2], sources[3]]]

    def source_step(n):
        return [swap(state[k][1], 2 * routes[k][n], devices) for k in range(2)]

    def source_add(n, came):
        for k in range(2):
            if n == len(masks) - 1:
                outs = [shaped((half_rows, width), (F32, BF16)[k])]
            else:
                rows = state[k][0].shape[0] // 2
                outs = [shaped((rows, width), F32), shaped((rows, width), BF16)]
            state[k] = call(halve, "source_sum", outs, inputs=2)(state[k][0], came[k])

    total = call(add_up, "weight_sum", shaped((piece, half), BF16), inputs=quads)(terms[0], *received)
    mask, n = 1, 0
    while mask < layers:
        other = swap(total, 2 * quads * mask, devices)
        came = source_step(n)
        if mask == 1:
            target_gradient, updated = call(
                target_side, "target_side", (shaped((targets, width), BF16),) * 2, inputs=6, flops=square
            )(self_weight, cot0, grad, grad_received, updated, updated_received)
            other, target_gradient, updated = lax.optimization_barrier((other, target_gradient, updated))
        total = call(add_up, "weight_sum", shaped((piece, half), BF16), inputs=2)(total, other)
        source_add(n, came)
        mask, n = 2 * mask, n + 1
    while n < len(masks):
        source_add(n, source_step(n))
        n += 1
    stays, goes = state[0][0], state[1][0]
    pieces = {0: total}
    for m in reversed(range(1, quads)):
        pieces[m] = swap(total, 2 * m, devices)

    mask = layers
    while mask > 1:
        mask //= 2
        came = swap(goes, 2 * quads * mask, devices)
        if mask == 1:
            source_gradient = call(finish_source, "finish_source", shaped((share, width), BF16), inputs=3)(
                message_weight, stays, came
            )
        else:
            rows = stays.shape[0] // 2
            stays, goes = call(halve, "source_sum", [shaped((rows, width), F32), shaped((rows, width), BF16)], inputs=2)(
                stays, came
            )

    their_pieces = {m: swap(value, 1, devices) for m, value in pieces.items()}
    scales = ((targets * devices) ** (-0.5), (block_rows * blk_devices) ** (-0.5))
    self_gradient, message_gradient = call(
        functools.partial(finish_weights, quads, scales),
        "finish_weights",
        (shaped((width, width), F32),) * 2,
        inputs=2 * quads,
        out_specs=(HBM, HBM),
        scratch_shapes=[pltpu.VMEM((2 * quads, piece, half), F32), pltpu.SemaphoreType.DMA((2 * quads,))],
    )(*[values[m] for values in (pieces, their_pieces) for m in range(quads)])
    return (updated, target_gradient, source_gradient, self_gradient, message_gradient)


def solution(mesh):
    split = P(AXES, None)
    return jax.shard_map(
        functools.partial(local, mesh.shape["row"], mesh.shape["blk"]),
        mesh=mesh,
        in_specs=(P("blk", None), split, P(), P(), split, split, P(AXES), split),
        out_specs=(split, split, P(("blk", "row"), None), P(), P()),
        check_vma=False,
    )
```

time: 63.3 us -> 60.3 us (0.953)
  waiting for transfers between devices: 14.7 us -> 20.7 us
  Pallas kernels: 14.5 us -> 10 us
  starting transfers between devices: 26.3 us -> 23.1 us
  other arithmetic: 2.27 us -> 1.47 us
    ppermute x26, waiting for transfers between devices: 14.7 us -> 20.7 us  [swap(): return lax.ppermute(value, AXES, [(i, i ^ mask) for i in range(devices)])]
    ppermute x26, starting transfers between devices: 26.3 us -> 23.1 us  [swap(): return lax.ppermute(value, AXES, [(i, i ^ mask) for i in range(devices)])]
    pallas_call x3 -> x2, Pallas kernels: 4.23 us -> 2.79 us  [the longest x1 1.4 us: local(): call(target_side, 'target_side', (shaped((targets, width), BF16),) * 2, i...]
    another operation x2 -> x0, other arithmetic: 0.79 us -> none  [the longest x1 0.72 us: local(): lengths = jnp.stack([packed[slots, 0], their_packed[slots, 0]])]
    pallas_call x1, Pallas kernels: 1.99 us -> 1.31 us  [local(): call(functools.partial(source_terms, share, sides, orders), 'source_terms...]
    pallas_call x1, Pallas kernels: 2.02 us -> 1.38 us  [local(): call(functools.partial(forward, order), 'forward', (shaped((2 * targets,...]
  transfers between devices with their start and end apart: 26 -> 26, of which waited for: 11 -> 12; matrix products, arithmetic and copies ran while one was open for 4% -> 2% of each run, Pallas kernels for 18% -> 12%
where the time goes in v3:
time: 60.3 us; the launch traced here: 60 us
  starting transfers between devices  23.1 us (38%)
  waiting for transfers between devices  20.7 us (34%)
  Pallas kernels  10 us (17%)
  local copies, waits for them, and re-layouts  3.15 us (5%)
  between operations  1.48 us (2%)
  other arithmetic  1.47 us (2%)
    ppermute x26, starting transfers between devices, swap(): return lax.ppermute(value, AXES, [(i, i ^ mask) for i in range(devices)])  23.1 us
    ppermute x26, waiting for transfers between devices, swap(): return lax.ppermute(value, AXES, [(i, i ^ mask) for i in range(devices)])  20.7 us
    unnamed x14, local copies, waits for them, and re-layouts  3.14 us
    pallas_call x1, Pallas kernels, local(): call(functools.partial(finish_weights, quads, scales), 'finish_weights',...  1.42 us
    pallas_call x1, Pallas kernels, local(): call(target_side, 'target_side', (shaped((targets, width), BF16),) * 2, i...  1.4 us
    pallas_call x1, Pallas kernels, local(): call(functools.partial(gather_more, order), 'gather_more', (shaped((targe...  1.39 us
    pallas_call x1, Pallas kernels, local(): call(functools.partial(forward, order), 'forward', (shaped((2 * targets,...  1.38 us
    pallas_call x1, Pallas kernels, local(): call(functools.partial(source_terms, share, sides, orders), 'source_terms...  1.31 us
  transfers between devices with their start and end apart: 26, of which 12 were waited for; matrix products, arithmetic and copies ran while one was open for 2% of the time, Pallas kernels for 12%

profile of v3, /device:TPU:0, one launch (start us, length us, event | category | flops | bytes accessed | tf_op | source)
XLA Modules:
  0.0 60.0 jit_solution(6812449526971222406)
XLA Ops:
  0.6 3.0 %collective-permute-start.2 = (bf16[512,512]{1,0:T(8,128)(2,1)}, bf16[512,512]{1,0:T(8,128)(2,1)S(1)}, u32[]{:S(2)}, u32[]{:S(2)}) collective-permute-start(bf16[512,512]{1,0:T(8,128)(2,1)} %s_ref.1), channel_id=1, source_target_pairs={{0,2},{1,3},{2,0},{3,1},{4,6},{5,7},{6,4},{7,5},{8,10},{9,11},{10,... | collective-permute-start | bytes 1572872 | tf_op jit(solution)/shard_map/ppermute | solution.py:20
  5.5 0.8 %select_reduce_fusion = s32[4,512]{1,0:T(4,128)S(1)} fusion(s32[4,512]{1,0:T(4,128)} %bitcast.5, pred[4,4]{1,0:T(4,128)(4,1)S(1)} %fusion), kind=kLoop, calls=%fused_computation | loop fusion | flops 14336 | bytes 16400 | tf_op jit(solution)/shard_map/reduce_max | solution.py:229
  7.6 1.0 %copy-done = bf16[512,512]{1,0:T(8,128)(2,1)S(1)} copy-done((bf16[512,512]{1,0:T(8,128)(2,1)S(1)}, bf16[512,512]{1,0:T(8,128)(2,1)}, u32[]{:S(2)}) %copy-start) | copy-done | bytes 524312
  8.6 1.0 %copy-done.2 = bf16[512,512]{1,0:T(8,128)(2,1)S(1)} copy-done((bf16[512,512]{1,0:T(8,128)(2,1)S(1)}, bf16[512,512]{1,0:T(8,128)(2,1)}, u32[]{:S(2)}) %copy-start.2) | copy-done | bytes 524312
  9.7 1.0 %copy-done.6 = bf16[512,512]{1,0:T(8,128)(2,1)S(1)} copy-done((bf16[512,512]{1,0:T(8,128)(2,1)S(1)}, bf16[512,512]{1,0:T(8,128)(2,1)}, u32[]{:S(2)}) %copy-start.6) | copy-done | bytes 524312
  10.7 1.1 %gather_first.1 = (s32[1024,4]{1,0:T(8,128)S(1)}, f32[512,256]{1,0:T(8,128)S(1)}, f32[1024,512]{1,0:T(8,128)S(1)}, bf16[512,256]{1,0:T(8,128)(2,1)S(1)}) custom-call(s32[8,512]{1,0:T(8,128)S(1)} %concatenate.3.links0_ref, s32[8,512]{1,0:T(8,128)S(1)} %collective-permute-done.1.links1_ref, bf16[512,512]{1,0:T(8,128)(2,1)S(1)} %copy-done.6, ...), custom_call_target="tpu_custom_call" | custom-call | tf_op jit(solution)/shard_map/gather_first/pallas_call | solution.py:238
  11.8 4.0 %collective-permute-done.2.refs_1_ = bf16[512,512]{1,0:T(8,128)(2,1)S(1)} collective-permute-done((bf16[512,512]{1,0:T(8,128)(2,1)}, bf16[512,512]{1,0:T(8,128)(2,1)S(1)}, u32[]{:S(2)}, u32[]{:S(2)}) %collective-permute-start.2) | collective-permute-done | bytes 524320 | tf_op jit(solution)/shard_map/ppermute | solution.py:20
  15.8 1.4 %gather_more.1 = (f32[512,256]{1,0:T(8,128)S(1)}, f32[1024,512]{1,0:T(8,128)S(1)}) custom-call(s32[1024,4]{1,0:T(8,128)S(1)} %get-tuple-element.53.columns_ref, f32[1024,512]{1,0:T(8,128)S(1)} %get-tuple-element.54.h0_ref, bf16[512,512]{1,0:T(8,128)(2,1)S(1)} %collective-permute-done.t_ref.t1_ref, bf16[512,256]{1,0:T(8,128)(2,1)S(1)} %get-tuple-element.55.weight_ref, ...), custom_call_target="tpu_custom_call" | custom-call | flops 536870912 | bytes 1048576 | tf_op jit(solution)/shard_map/gather_more/pallas_call | solution.py:257
  17.7 1.4 %forward.1 = (bf16[1024,512]{1,0:T(8,128)(2,1)S(1)}, bf16[1024,256]{1,0:T(8,128)(2,1)S(1)}, bf16[512,256]{1,0:T(8,128)(2,1)S(1)}, bf16[512,256]{1,0:T(8,128)(2,1)S(1)}) custom-call(s32[8,512]{1,0:T(8,128)S(1)} %concatenate.3.links0_ref, s32[8,512]{1,0:T(8,128)S(1)} %collective-permute-done.1.links1_ref, s32[1024,4]{1,0:T(8,128)S(1)} %get-tuple-element.53.columns_ref, ...), custom_call_target="tpu_custom_call" | custom-call | flops 1073741824 | bytes 1048576 | tf_op jit(solution)/shard_map/forward/pallas_call | solution.py:265
  19.1 0.8 %weight_terms.1 = (f32[256,256]{1,0:T(8,128)S(1)}, bf16[256,256]{1,0:T(8,128)(2,1)S(1)}, bf16[256,256]{1,0:T(8,128)(2,1)S(1)}, bf16[256,256]{1,0:T(8,128)(2,1)S(1)}) custom-call(bf16[512,512]{1,0:T(8,128)(2,1)S(1)} %copy-done.1, bf16[512,512]{1,0:T(8,128)(2,1)S(1)} %collective-permute-done.t_ref.t1_ref, bf16[1024,512]{1,0:T(8,128)(2,1)S(1)} %get-tuple-element.60.h_ref, ...), custom_call_target="tpu_custom_call" | custom-call | flops 536870912 | bytes 1048576 | tf_op jit(solution)/shard_map/weight_terms/pallas_call | solution.py:277
  20.2 2.7 %collective-permute-start.7 = (bf16[256,256]{1,0:T(8,128)(2,1)S(1)}, bf16[256,256]{1,0:T(8,128)(2,1)S(1)}, u32[]{:S(2)}, u32[]{:S(2)}) collective-permute-start(bf16[256,256]{1,0:T(8,128)(2,1)S(1)} %get-tuple-element.65), channel_id=1, source_target_pairs={{0,6},{1,7},{2,4},{3,5},{4,2},{5,3},{6,0},{7,1},{8,14},{9,15},{10,... | collective-permute-start | bytes 393224 | tf_op jit(solution)/shard_map/ppermute | solution.py:20
  23.7 1.3 %source_terms.1 = (f32[256,512]{1,0:T(8,128)S(1)}, bf16[256,512]{1,0:T(8,128)(2,1)S(1)}, f32[256,512]{1,0:T(8,128)S(1)}, bf16[256,512]{1,0:T(8,128)(2,1)S(1)}) custom-call(s32[8,512]{1,0:T(8,128)S(1)} %concatenate.3.links0_ref, s32[8,512]{1,0:T(8,128)S(1)} %collective-permute-done.1.links1_ref, bf16[1024,256]{1,0:T(8,128)(2,1)S(1)} %get-tuple-element.68.grad_ref, ...), custom_call_target="tpu_custom_call" | custom-call | flops 1073741824 | bytes 1048576 | tf_op jit(solution)/shard_map/source_terms/pallas_call | solution.py:296
  25.0 1.8 %collective-permute-start.14 = (bf16[256,512]{1,0:T(8,128)(2,1)S(1)}, bf16[256,512]{1,0:T(8,128)(2,1)S(1)}, u32[]{:S(2)}, u32[]{:S(2)}) collective-permute-start(bf16[256,512]{1,0:T(8,128)(2,1)S(1)} %get-tuple-element.74), channel_id=1, source_target_pairs={{0,4},{1,5},{2,6},{3,7},{4,0},{5,1},{6,2},{7,3},{8,12},{9,13},{10,... | collective-permute-start | bytes 786440 | tf_op jit(solution)/shard_map/ppermute | solution.py:20
  27.4 3.1 %collective-permute-done.8.refs_2_ = bf16[256,256]{1,0:T(8,128)(2,1)S(1)} collective-permute-done((bf16[256,256]{1,0:T(8,128)(2,1)S(1)}, bf16[256,256]{1,0:T(8,128)(2,1)S(1)}, u32[]{:S(2)}, u32[]{:S(2)}) %collective-permute-start.8) | collective-permute-done | bytes 131104 | tf_op jit(solution)/shard_map/ppermute | solution.py:20
  30.6 1.6 %collective-permute-start.10 = (bf16[256,256]{1,0:T(8,128)(2,1)S(1)}, bf16[256,256]{1,0:T(8,128)(2,1)S(1)}, u32[]{:S(2)}, u32[]{:S(2)}) collective-permute-start(bf16[256,256]{1,0:T(8,128)(2,1)S(1)} %weight_sum.3.refs_0_), channel_id=1, source_target_pairs={{0,8},{1,9},{2,10},{3,11},{4,12},{5,13},{6,14},{7,15},{8,0},{9,1},... | collective-permute-start | bytes 393224 | tf_op jit(solution)/shard_map/ppermute | solution.py:20
  32.2 0.8 %collective-permute-start.12 = (bf16[256,512]{1,0:T(8,128)(2,1)S(1)}, bf16[256,512]{1,0:T(8,128)(2,1)S(1)}, u32[]{:S(2)}, u32[]{:S(2)}) collective-permute-start(bf16[256,512]{1,0:T(8,128)(2,1)S(1)} %get-tuple-element.72), channel_id=1, source_target_pairs={{0,2},{1,3},{2,0},{3,1},{4,6},{5,7},{6,4},{7,5},{8,10},{9,11},{10,... | collective-permute-start | bytes 786440 | tf_op jit(solution)/shard_map/ppermute | solution.py:20
  33.1 1.4 %target_side.1 = (bf16[512,512]{1,0:T(8,128)(2,1)}, bf16[512,512]{1,0:T(8,128)(2,1)}) custom-call(bf16[512,512]{1,0:T(8,128)(2,1)S(1)} %copy-done.3, bf16[512,512]{1,0:T(8,128)(2,1)S(1)} %copy-done.4, bf16[1024,256]{1,0:T(8,128)(2,1)S(1)} %get-tuple-element.68.grad_ref, bf16[1024,256]{1,0:T(8,128)(2,1)S(1)} %collective-permute-done.6.other_ref.grad_received_ref, ...), custom_call_target="tpu_custom_call" | custom-call | flops 268435456 | bytes 1048576 | tf_op jit(solution)/shard_map/target_side/pallas_call | solution.py:325
  34.5 1.2 %collective-permute-done.10.refs_1_ = bf16[256,256]{1,0:T(8,128)(2,1)S(1)} collective-permute-done((bf16[256,256]{1,0:T(8,128)(2,1)S(1)}, bf16[256,256]{1,0:T(8,128)(2,1)S(1)}, u32[]{:S(2)}, u32[]{:S(2)}) %collective-permute-start.10) | collective-permute-done | bytes 131104 | tf_op jit(solution)/shard_map/ppermute | solution.py:20
  35.7 2.6 %collective-permute-start.18 = (bf16[256,256]{1,0:T(8,128)(2,1)S(1)}, bf16[256,256]{1,0:T(8,128)(2,1)S(1)}, u32[]{:S(2)}, u32[]{:S(2)}) collective-permute-start(bf16[256,256]{1,0:T(8,128)(2,1)S(1)} %weight_sum.4.refs_0_), channel_id=1, source_target_pairs={{0,16},{1,17},{2,18},{3,19},{4,20},{5,21},{6,22},{7,23},{8,24},{9,... | collective-permute-start | bytes 393224 | tf_op jit(solution)/shard_map/ppermute | solution.py:20
  38.4 1.4 %collective-permute-start.15 = (bf16[128,512]{1,0:T(8,128)(2,1)S(1)}, bf16[128,512]{1,0:T(8,128)(2,1)S(1)}, u32[]{:S(2)}, u32[]{:S(2)}) collective-permute-start(bf16[128,512]{1,0:T(8,128)(2,1)S(1)} %get-tuple-element.87), channel_id=1, source_target_pairs={{0,2},{1,3},{2,0},{3,1},{4,6},{5,7},{6,4},{7,5},{8,10},{9,11},{10,... | collective-permute-start | bytes 393224 | tf_op jit(solution)/shard_map/ppermute | solution.py:20
  39.8 1.6 %collective-permute-start.13 = (bf16[128,512]{1,0:T(8,128)(2,1)S(1)}, bf16[128,512]{1,0:T(8,128)(2,1)S(1)}, u32[]{:S(2)}, u32[]{:S(2)}) collective-permute-start(bf16[128,512]{1,0:T(8,128)(2,1)S(1)} %get-tuple-element.85), channel_id=1, source_target_pairs={{0,4},{1,5},{2,6},{3,7},{4,0},{5,1},{6,2},{7,3},{8,12},{9,13},{10,... | collective-permute-start | bytes 393224 | tf_op jit(solution)/shard_map/ppermute | solution.py:20
  41.3 1.8 %collective-permute-done.18.refs_1_ = bf16[256,256]{1,0:T(8,128)(2,1)S(1)} collective-permute-done((bf16[256,256]{1,0:T(8,128)(2,1)S(1)}, bf16[256,256]{1,0:T(8,128)(2,1)S(1)}, u32[]{:S(2)}, u32[]{:S(2)}) %collective-permute-start.18) | collective-permute-done | bytes 131104 | tf_op jit(solution)/shard_map/ppermute | solution.py:20
  43.2 2.2 %collective-permute-start.19 = (bf16[256,256]{1,0:T(8,128)(2,1)S(1)}, bf16[256,256]{1,0:T(8,128)(2,1)S(1)}, u32[]{:S(2)}, u32[]{:S(2)}) collective-permute-start(bf16[256,256]{1,0:T(8,128)(2,1)S(1)} %weight_sum.5.refs_0_), channel_id=1, source_target_pairs={{0,2},{1,3},{2,0},{3,1},{4,6},{5,7},{6,4},{7,5},{8,10},{9,11},{10,... | collective-permute-start | bytes 393224 | tf_op jit(solution)/shard_map/ppermute | solution.py:20
  45.4 1.5 %collective-permute-start.20 = (bf16[256,256]{1,0:T(8,128)(2,1)S(1)}, bf16[256,256]{1,0:T(8,128)(2,1)S(1)}, u32[]{:S(2)}, u32[]{:S(2)}) collective-permute-start(bf16[256,256]{1,0:T(8,128)(2,1)S(1)} %weight_sum.5.refs_0_), channel_id=1, source_target_pairs={{0,4},{1,5},{2,6},{3,7},{4,0},{5,1},{6,2},{7,3},{8,12},{9,13},{10,... | collective-permute-start | bytes 393224 | tf_op jit(solution)/shard_map/ppermute | solution.py:20
  47.0 1.7 %collective-permute-start.16 = (bf16[128,512]{1,0:T(8,128)(2,1)S(1)}, bf16[128,512]{1,0:T(8,128)(2,1)S(1)}, u32[]{:S(2)}, u32[]{:S(2)}) collective-permute-start(bf16[128,512]{1,0:T(8,128)(2,1)S(1)} %source_sum.8), channel_id=1, source_target_pairs={{0,16},{1,17},{2,18},{3,19},{4,20},{5,21},{6,22},{7,23},{8,24},{9,... | collective-permute-start | bytes 393224 | tf_op jit(solution)/shard_map/ppermute | solution.py:20
  48.6 0.7 %collective-permute-done.19.refs_1_ = bf16[256,256]{1,0:T(8,128)(2,1)S(1)} collective-permute-done((bf16[256,256]{1,0:T(8,128)(2,1)S(1)}, bf16[256,256]{1,0:T(8,128)(2,1)S(1)}, u32[]{:S(2)}, u32[]{:S(2)}) %collective-permute-start.19) | collective-permute-done | bytes 131104 | tf_op jit(solution)/shard_map/ppermute | solution.py:20
  49.3 1.6 %collective-permute-done.20.refs_2_ = bf16[256,256]{1,0:T(8,128)(2,1)S(1)} collective-permute-done((bf16[256,256]{1,0:T(8,128)(2,1)S(1)}, bf16[256,256]{1,0:T(8,128)(2,1)S(1)}, u32[]{:S(2)}, u32[]{:S(2)}) %collective-permute-start.20) | collective-permute-done | bytes 131104 | tf_op jit(solution)/shard_map/ppermute | solution.py:20
  50.9 1.8 %collective-permute-done.21.refs_3_ = bf16[256,256]{1,0:T(8,128)(2,1)S(1)} collective-permute-done((bf16[256,256]{1,0:T(8,128)(2,1)S(1)}, bf16[256,256]{1,0:T(8,128)(2,1)S(1)}, u32[]{:S(2)}, u32[]{:S(2)}) %collective-permute-start.21) | collective-permute-done | bytes 131104 | tf_op jit(solution)/shard_map/ppermute | solution.py:20
  52.8 1.9 %collective-permute-done.16.received_ref = bf16[128,512]{1,0:T(8,128)(2,1)S(1)} collective-permute-done((bf16[128,512]{1,0:T(8,128)(2,1)S(1)}, bf16[128,512]{1,0:T(8,128)(2,1)S(1)}, u32[]{:S(2)}, u32[]{:S(2)}) %collective-permute-start.16) | collective-permute-done | bytes 131104 | tf_op jit(solution)/shard_map/ppermute | solution.py:20
  54.8 1.4 %finish_weights.1 = (f32[512,512]{1,0:T(8,128)}, f32[512,512]{1,0:T(8,128)}) custom-call(bf16[256,256]{1,0:T(8,128)(2,1)S(1)} %weight_sum.5.refs_0_, bf16[256,256]{1,0:T(8,128)(2,1)S(1)} %collective-permute-done.19.refs_1_, bf16[256,256]{1,0:T(8,128)(2,1)S(1)} %collective-permute-done.20.refs_2_, bf16[256,256]{1,0:T(8,128)(2,1)S(1)} %collective-permute-done.21.refs_3_, ...), custom_call_target="tpu_custom_call" | custom-call | bytes 1048576 | tf_op jit(solution)/shard_map/finish_weights/pallas_call | solution.py:356
  56.3 2.8 %collective-permute-done.17.received_ref = bf16[64,512]{1,0:T(8,128)(2,1)S(1)} collective-permute-done((bf16[64,512]{1,0:T(8,128)(2,1)S(1)}, bf16[64,512]{1,0:T(8,128)(2,1)S(1)}, u32[]{:S(2)}, u32[]{:S(2)}) %collective-permute-start.17) | collective-permute-done | bytes 65568 | tf_op jit(solution)/shard_map/ppermute | solution.py:20
  59.1 0.9 %finish_source.1 = bf16[64,512]{1,0:T(8,128)(2,1)} custom-call(bf16[512,512]{1,0:T(8,128)(2,1)S(1)} %copy-done.5, f32[64,512]{1,0:T(8,128)S(1)} %get-tuple-element.88.own_ref, bf16[64,512]{1,0:T(8,128)(2,1)S(1)} %collective-permute-done.17.received_ref), custom_call_target="tpu_custom_call" | custom-call | bytes 1048576 | tf_op jit(solution)/shard_map/finish_source/pallas_call | solution.py:345
  (54 shorter events, 5.1 us)
Async XLA Ops:
  0.6 15.2 %collective-permute-start.2 = (bf16[512,512]{1,0:T(8,128)(2,1)}, bf16[512,512]{1,0:T(8,128)(2,1)S(1)}, u32[]{:S(2)}, u32[]{:S(2)}) collective-permute-start(bf16[512,512]{1,0:T(8,128)(2,1)} %s_ref.1), channel_id=1, source_target_pairs={{0,2},{1,3},{2,0},{3,1},{4,6},{5,7},{6,4},{7,5},{8,10},{9,11},{10,... | collective-permute-start | bytes 1572872 | tf_op jit(solution)/shard_map/ppermute | solution.py:20
  3.7 12.2 %collective-permute-start.3 = (bf16[512,512]{1,0:T(8,128)(2,1)}, bf16[512,512]{1,0:T(8,128)(2,1)S(1)}, u32[]{:S(2)}, u32[]{:S(2)}) collective-permute-start(bf16[512,512]{1,0:T(8,128)(2,1)} %s_ref.1), channel_id=1, source_target_pairs={{0,1},{1,0},{2,3},{3,2},{4,5},{5,4},{6,7},{7,6},{8,9},{9,8},{10,11... | collective-permute-start | bytes 1572872 | tf_op jit(solution)/shard_map/ppermute | solution.py:20
  3.7 12.2 %collective-permute-start = (bf16[512,512]{1,0:T(8,128)(2,1)}, bf16[512,512]{1,0:T(8,128)(2,1)S(1)}, u32[]{:S(2)}, u32[]{:S(2)}) collective-permute-start(bf16[512,512]{1,0:T(8,128)(2,1)} %t0_ref.3), channel_id=1, source_target_pairs={{0,1},{1,0},{2,3},{3,2},{4,5},{5,4},{6,7},{7,6},{8,9},{9,8},{10,11... | collective-permute-start | bytes 1572872 | tf_op jit(solution)/shard_map/ppermute | solution.py:20
  6.3 1.2 %collective-permute-start.1 = (s32[8,512]{1,0:T(8,128)S(1)}, s32[8,512]{1,0:T(8,128)S(1)}, u32[]{:S(2)}, u32[]{:S(2)}) collective-permute-start(s32[8,512]{1,0:T(8,128)S(1)} %concatenate.3.links0_ref), channel_id=1, source_target_pairs={{0,1},{1,0},{2,3},{3,2},{4,5},{5,4},{6,7},{7,6},{8,9},{9,8},{10,11... | collective-permute-start | bytes 49160 | tf_op jit(solution)/shard_map/ppermute | solution.py:20
  6.4 10.8 %collective-permute-start.4 = (bf16[512,512]{1,0:T(8,128)(2,1)}, bf16[512,512]{1,0:T(8,128)(2,1)S(1)}, u32[]{:S(2)}, u32[]{:S(2)}) collective-permute-start(bf16[512,512]{1,0:T(8,128)(2,1)} %cot_ref.1), channel_id=1, source_target_pairs={{0,1},{1,0},{2,3},{3,2},{4,5},{5,4},{6,7},{7,6},{8,9},{9,8},{10,11... | collective-permute-start | bytes 1572872 | tf_op jit(solution)/shard_map/ppermute | solution.py:20
  7.6 1.0 %copy-start = (bf16[512,512]{1,0:T(8,128)(2,1)S(1)}, bf16[512,512]{1,0:T(8,128)(2,1)}, u32[]{:S(2)}) copy-start(bf16[512,512]{1,0:T(8,128)(2,1)} %t0_ref.3) | copy-start | bytes 1572868
  8.6 1.0 %copy-start.2 = (bf16[512,512]{1,0:T(8,128)(2,1)S(1)}, bf16[512,512]{1,0:T(8,128)(2,1)}, u32[]{:S(2)}) copy-start(bf16[512,512]{1,0:T(8,128)(2,1)} %ws_ref.3) | copy-start | bytes 1572868
  15.8 1.9 %copy-start.1 = (bf16[512,512]{1,0:T(8,128)(2,1)S(1)}, bf16[512,512]{1,0:T(8,128)(2,1)}, u32[]{:S(2)}) copy-start(bf16[512,512]{1,0:T(8,128)(2,1)} %t0_ref.3) | copy-start | bytes 1572868
  15.8 1.9 %copy-start.4 = (bf16[512,512]{1,0:T(8,128)(2,1)S(1)}, bf16[512,512]{1,0:T(8,128)(2,1)}, u32[]{:S(2)}) copy-start(bf16[512,512]{1,0:T(8,128)(2,1)} %cot_ref.1) | copy-start | bytes 1572868
  15.8 1.9 %copy-start.5 = (bf16[512,512]{1,0:T(8,128)(2,1)S(1)}, bf16[512,512]{1,0:T(8,128)(2,1)}, u32[]{:S(2)}) copy-start(bf16[512,512]{1,0:T(8,128)(2,1)} %wm_ref.3) | copy-start | bytes 1572868
  15.8 1.9 %collective-permute-start.5 = (bf16[512,512]{1,0:T(8,128)(2,1)S(1)}, bf16[512,512]{1,0:T(8,128)(2,1)S(1)}, u32[]{:S(2)}, u32[]{:S(2)}) collective-permute-start(bf16[512,512]{1,0:T(8,128)(2,1)S(1)} %collective-permute-done.2.refs_1_), channel_id=1, source_target_pairs={{0,1},{1,0},{2,3},{3,2},{4,5},{5,4},{6,7},{7,6},{8,9},{9,8},{10,11... | collective-permute-start | bytes 1572872 | tf_op jit(solution)/shard_map/ppermute | solution.py:20
  19.9 13.1 %copy-start.3 = (bf16[512,512]{1,0:T(8,128)(2,1)S(1)}, bf16[512,512]{1,0:T(8,128)(2,1)}, u32[]{:S(2)}) copy-start(bf16[512,512]{1,0:T(8,128)(2,1)} %ws_ref.3) | copy-start | bytes 1572868
  19.9 3.8 %collective-permute-start.6 = (bf16[1024,256]{1,0:T(8,128)(2,1)S(1)}, bf16[1024,256]{1,0:T(8,128)(2,1)S(1)}, u32[]{:S(2)}, u32[]{:S(2)}) collective-permute-start(bf16[1024,256]{1,0:T(8,128)(2,1)S(1)} %get-tuple-element.68.grad_ref), channel_id=1, source_target_pairs={{0,1},{1,0},{2,3},{3,2},{4,5},{5,4},{6,7},{7,6},{8,9},{9,8},{10,11... | collective-permute-start | bytes 1572872 | tf_op jit(solution)/shard_map/ppermute | solution.py:20
  20.2 7.2 %collective-permute-start.7 = (bf16[256,256]{1,0:T(8,128)(2,1)S(1)}, bf16[256,256]{1,0:T(8,128)(2,1)S(1)}, u32[]{:S(2)}, u32[]{:S(2)}) collective-permute-start(bf16[256,256]{1,0:T(8,128)(2,1)S(1)} %get-tuple-element.65), channel_id=1, source_target_pairs={{0,6},{1,7},{2,4},{3,5},{4,2},{5,3},{6,0},{7,1},{8,14},{9,15},{10,... | collective-permute-start | bytes 393224 | tf_op jit(solution)/shard_map/ppermute | solution.py:20
  22.9 7.7 %collective-permute-start.8 = (bf16[256,256]{1,0:T(8,128)(2,1)S(1)}, bf16[256,256]{1,0:T(8,128)(2,1)S(1)}, u32[]{:S(2)}, u32[]{:S(2)}) collective-permute-start(bf16[256,256]{1,0:T(8,128)(2,1)S(1)} %get-tuple-element.64), channel_id=1, source_target_pairs={{0,4},{1,5},{2,6},{3,7},{4,0},{5,1},{6,2},{7,3},{8,12},{9,13},{10,... | collective-permute-start | bytes 393224 | tf_op jit(solution)/shard_map/ppermute | solution.py:20
  23.4 7.2 %collective-permute-start.9 = (bf16[256,256]{1,0:T(8,128)(2,1)S(1)}, bf16[256,256]{1,0:T(8,128)(2,1)S(1)}, u32[]{:S(2)}, u32[]{:S(2)}) collective-permute-start(bf16[256,256]{1,0:T(8,128)(2,1)S(1)} %get-tuple-element.63), channel_id=1, source_target_pairs={{0,2},{1,3},{2,0},{3,1},{4,6},{5,7},{6,4},{7,5},{8,10},{9,11},{10,... | collective-permute-start | bytes 393224 | tf_op jit(solution)/shard_map/ppermute | solution.py:20
  23.7 9.4 %collective-permute-start.11 = (bf16[512,256]{1,0:T(8,128)(2,1)S(1)}, bf16[512,256]{1,0:T(8,128)(2,1)S(1)}, u32[]{:S(2)}, u32[]{:S(2)}) collective-permute-start(bf16[512,256]{1,0:T(8,128)(2,1)S(1)} %get-tuple-element.79), channel_id=1, source_target_pairs={{0,1},{1,0},{2,3},{3,2},{4,5},{5,4},{6,7},{7,6},{8,9},{9,8},{10,11... | collective-permute-start | bytes 786440 | tf_op jit(solution)/shard_map/ppermute | solution.py:20
  25.0 13.3 %collective-permute-start.14 = (bf16[256,512]{1,0:T(8,128)(2,1)S(1)}, bf16[256,512]{1,0:T(8,128)(2,1)S(1)}, u32[]{:S(2)}, u32[]{:S(2)}) collective-permute-start(bf16[256,512]{1,0:T(8,128)(2,1)S(1)} %get-tuple-element.74), channel_id=1, source_target_pairs={{0,4},{1,5},{2,6},{3,7},{4,0},{5,1},{6,2},{7,3},{8,12},{9,13},{10,... | collective-permute-start | bytes 786440 | tf_op jit(solution)/shard_map/ppermute | solution.py:20
  30.6 5.0 %collective-permute-start.10 = (bf16[256,256]{1,0:T(8,128)(2,1)S(1)}, bf16[256,256]{1,0:T(8,128)(2,1)S(1)}, u32[]{:S(2)}, u32[]{:S(2)}) collective-permute-start(bf16[256,256]{1,0:T(8,128)(2,1)S(1)} %weight_sum.3.refs_0_), channel_id=1, source_target_pairs={{0,8},{1,9},{2,10},{3,11},{4,12},{5,13},{6,14},{7,15},{8,0},{9,1},... | collective-permute-start | bytes 393224 | tf_op jit(solution)/shard_map/ppermute | solution.py:20
  32.2 7.5 %collective-permute-start.12 = (bf16[256,512]{1,0:T(8,128)(2,1)S(1)}, bf16[256,512]{1,0:T(8,128)(2,1)S(1)}, u32[]{:S(2)}, u32[]{:S(2)}) collective-permute-start(bf16[256,512]{1,0:T(8,128)(2,1)S(1)} %get-tuple-element.72), channel_id=1, source_target_pairs={{0,2},{1,3},{2,0},{3,1},{4,6},{5,7},{6,4},{7,5},{8,10},{9,11},{10,... | collective-permute-start | bytes 786440 | tf_op jit(solution)/shard_map/ppermute | solution.py:20
  35.7 7.5 %collective-permute-start.18 = (bf16[256,256]{1,0:T(8,128)(2,1)S(1)}, bf16[256,256]{1,0:T(8,128)(2,1)S(1)}, u32[]{:S(2)}, u32[]{:S(2)}) collective-permute-start(bf16[256,256]{1,0:T(8,128)(2,1)S(1)} %weight_sum.4.refs_0_), channel_id=1, source_target_pairs={{0,16},{1,17},{2,18},{3,19},{4,20},{5,21},{6,22},{7,23},{8,24},{9,... | collective-permute-start | bytes 393224 | tf_op jit(solution)/shard_map/ppermute | solution.py:20
  38.4 8.6 %collective-permute-start.15 = (bf16[128,512]{1,0:T(8,128)(2,1)S(1)}, bf16[128,512]{1,0:T(8,128)(2,1)S(1)}, u32[]{:S(2)}, u32[]{:S(2)}) collective-permute-start(bf16[128,512]{1,0:T(8,128)(2,1)S(1)} %get-tuple-element.87), channel_id=1, source_target_pairs={{0,2},{1,3},{2,0},{3,1},{4,6},{5,7},{6,4},{7,5},{8,10},{9,11},{10,... | collective-permute-start | bytes 393224 | tf_op jit(solution)/shard_map/ppermute | solution.py:20
  39.8 8.9 %collective-permute-start.13 = (bf16[128,512]{1,0:T(8,128)(2,1)S(1)}, bf16[128,512]{1,0:T(8,128)(2,1)S(1)}, u32[]{:S(2)}, u32[]{:S(2)}) collective-permute-start(bf16[128,512]{1,0:T(8,128)(2,1)S(1)} %get-tuple-element.85), channel_id=1, source_target_pairs={{0,4},{1,5},{2,6},{3,7},{4,0},{5,1},{6,2},{7,3},{8,12},{9,13},{10,... | collective-permute-start | bytes 393224 | tf_op jit(solution)/shard_map/ppermute | solution.py:20
  43.2 6.1 %collective-permute-start.19 = (bf16[256,256]{1,0:T(8,128)(2,1)S(1)}, bf16[256,256]{1,0:T(8,128)(2,1)S(1)}, u32[]{:S(2)}, u32[]{:S(2)}) collective-permute-start(bf16[256,256]{1,0:T(8,128)(2,1)S(1)} %weight_sum.5.refs_0_), channel_id=1, source_target_pairs={{0,2},{1,3},{2,0},{3,1},{4,6},{5,7},{6,4},{7,5},{8,10},{9,11},{10,... | collective-permute-start | bytes 393224 | tf_op jit(solution)/shard_map/ppermute | solution.py:20
  45.4 5.5 %collective-permute-start.20 = (bf16[256,256]{1,0:T(8,128)(2,1)S(1)}, bf16[256,256]{1,0:T(8,128)(2,1)S(1)}, u32[]{:S(2)}, u32[]{:S(2)}) collective-permute-start(bf16[256,256]{1,0:T(8,128)(2,1)S(1)} %weight_sum.5.refs_0_), channel_id=1, source_target_pairs={{0,4},{1,5},{2,6},{3,7},{4,0},{5,1},{6,2},{7,3},{8,12},{9,13},{10,... | collective-permute-start | bytes 393224 | tf_op jit(solution)/shard_map/ppermute | solution.py:20
  46.9 5.9 %collective-permute-start.21 = (bf16[256,256]{1,0:T(8,128)(2,1)S(1)}, bf16[256,256]{1,0:T(8,128)(2,1)S(1)}, u32[]{:S(2)}, u32[]{:S(2)}) collective-permute-start(bf16[256,256]{1,0:T(8,128)(2,1)S(1)} %weight_sum.5.refs_0_), channel_id=1, source_target_pairs={{0,6},{1,7},{2,4},{3,5},{4,2},{5,3},{6,0},{7,1},{8,14},{9,15},{10,... | collective-permute-start | bytes 393224 | tf_op jit(solution)/shard_map/ppermute | solution.py:20
  47.0 7.7 %collective-permute-start.16 = (bf16[128,512]{1,0:T(8,128)(2,1)S(1)}, bf16[128,512]{1,0:T(8,128)(2,1)S(1)}, u32[]{:S(2)}, u32[]{:S(2)}) collective-permute-start(bf16[128,512]{1,0:T(8,128)(2,1)S(1)} %source_sum.8), channel_id=1, source_target_pairs={{0,16},{1,17},{2,18},{3,19},{4,20},{5,21},{6,22},{7,23},{8,24},{9,... | collective-permute-start | bytes 393224 | tf_op jit(solution)/shard_map/ppermute | solution.py:20
  48.6 6.2 %collective-permute-start.22 = (bf16[256,256]{1,0:T(8,128)(2,1)S(1)}, bf16[256,256]{1,0:T(8,128)(2,1)S(1)}, u32[]{:S(2)}, u32[]{:S(2)}) collective-permute-start(bf16[256,256]{1,0:T(8,128)(2,1)S(1)} %weight_sum.5.refs_0_), channel_id=1, source_target_pairs={{0,1},{1,0},{2,3},{3,2},{4,5},{5,4},{6,7},{7,6},{8,9},{9,8},{10,11... | collective-permute-start | bytes 393224 | tf_op jit(solution)/shard_map/ppermute | solution.py:20
  49.3 5.5 %collective-permute-start.23 = (bf16[256,256]{1,0:T(8,128)(2,1)S(1)}, bf16[256,256]{1,0:T(8,128)(2,1)S(1)}, u32[]{:S(2)}, u32[]{:S(2)}) collective-permute-start(bf16[256,256]{1,0:T(8,128)(2,1)S(1)} %collective-permute-done.19.refs_1_), channel_id=1, source_target_pairs={{0,1},{1,0},{2,3},{3,2},{4,5},{5,4},{6,7},{7,6},{8,9},{9,8},{10,11... | collective-permute-start | bytes 393224 | tf_op jit(solution)/shard_map/ppermute | solution.py:20
  50.9 3.9 %collective-permute-start.24 = (bf16[256,256]{1,0:T(8,128)(2,1)S(1)}, bf16[256,256]{1,0:T(8,128)(2,1)S(1)}, u32[]{:S(2)}, u32[]{:S(2)}) collective-permute-start(bf16[256,256]{1,0:T(8,128)(2,1)S(1)} %collective-permute-done.20.refs_2_), channel_id=1, source_target_pairs={{0,1},{1,0},{2,3},{3,2},{4,5},{5,4},{6,7},{7,6},{8,9},{9,8},{10,11... | collective-permute-start | bytes 393224 | tf_op jit(solution)/shard_map/ppermute | solution.py:20
  52.8 2.1 %collective-permute-start.25 = (bf16[256,256]{1,0:T(8,128)(2,1)S(1)}, bf16[256,256]{1,0:T(8,128)(2,1)S(1)}, u32[]{:S(2)}, u32[]{:S(2)}) collective-permute-start(bf16[256,256]{1,0:T(8,128)(2,1)S(1)} %collective-permute-done.21.refs_3_), channel_id=1, source_target_pairs={{0,1},{1,0},{2,3},{3,2},{4,5},{5,4},{6,7},{7,6},{8,9},{9,8},{10,11... | collective-permute-start | bytes 393224 | tf_op jit(solution)/shard_map/ppermute | solution.py:20
  54.7 4.3 %collective-permute-start.17 = (bf16[64,512]{1,0:T(8,128)(2,1)S(1)}, bf16[64,512]{1,0:T(8,128)(2,1)S(1)}, u32[]{:S(2)}, u32[]{:S(2)}) collective-permute-start(bf16[64,512]{1,0:T(8,128)(2,1)S(1)} %get-tuple-element.89), channel_id=1, source_target_pairs={{0,8},{1,9},{2,10},{3,11},{4,12},{5,13},{6,14},{7,15},{8,0},{9,1},... | collective-permute-start | bytes 196616 | tf_op jit(solution)/shard_map/ppermute | solution.py:20
  (1 other events, 1.0 us)

commit v4 on v3

--- a/solution.py
+++ b/solution.py
@@ -27,7 +27,7 @@
         in_specs=[VMEM] * inputs,
         out_shape=out_shape,
         compiler_params=pltpu.CompilerParams(vmem_limit_bytes=20 << 20),
-        cost_estimate=pl.CostEstimate(flops=flops, bytes_accessed=moved, transcendentals=0),
+        cost_estimate=pl.CostEstimate(flops=0, bytes_accessed=0, transcendentals=0),
         **more,
     )
 
@@ -131,14 +131,14 @@
     position = lax.broadcasted_iota(jnp.int32, (rows, targets), 0)
     inverses = [inverse(ref, half) for ref in (links0_ref, links1_ref)]
     for n, order in enumerate(orders):
-        far = position // share + n * (rows // share)
+        far = reverse_bits(position // share + n * (rows // share), 2 * rows // share)
         inside = (layer ^ far) * (2 * share) + position % share
         for j, m in enumerate(order):
             ref = refs[2 * n + j // (len(order) // 2)]
             at = (j % (len(order) // 2)) * rows
             to = quad ^ m
             row_at = inside + (to // sides) * share
-            block = (to % sides) * 2 + core
+            block = (to % sides) * 2 + 1 - core
             totals = [None, None]
             for i, links_ref in enumerate((links0_ref, links1_ref)):
                 chosen = pattern(links_ref[pl.ds(block, 1), :], row_at)
@@ -151,6 +151,14 @@
             ref[at : at + rows, half:] = jnp.where(first, totals[1], totals[0]).astype(ref.dtype)
 
 
+def reverse_bits(value, size):
+    result, low, high = value * 0, 1, size // 2
+    while high:
+        result = result + ((value // low) % 2) * high
+        low, high = low * 2, high // 2
+    return result
+
+
 def halve(own_ref, received_ref, *refs):
     rows = refs[0].shape[0]
     for n, ref in enumerate(refs):
@@ -163,11 +171,6 @@
     for ref in refs[1:-1]:
         total = total + ref[...].astype(F32)
     refs[-1][...] = total.astype(BF16)
-
-
-def finish_source(wm_ref, own_ref, received_ref, out_ref):
-    total = (own_ref[...] + received_ref[...].astype(F32)).astype(BF16)
-    out_ref[...] = mm(total, wm_ref[...], LANES).astype(BF16)
 
 
 def target_side(ws_ref, cot_ref, grad_ref, grad_received_ref, held_ref, held_received_ref, out_ref, updated_ref):
@@ -183,8 +186,12 @@
     updated_ref[:, pl.ds(pl.multiple_of((1 - core) * half, half), half)] = held_received_ref[...]
 
 
-def finish_weights(quads, scales, *refs):
-    refs, outs, buffer, sems = refs[: 2 * quads], refs[-4:-2], refs[-2], refs[-1]
+def project_back(total_ref, wm_ref, out_ref):
+    out_ref[...] = mm(total_ref[...], wm_ref[...], LANES).astype(BF16)
+
+
+def finish(quads, scales, rows_ref, *refs):
+    refs, outs, (buffer, sems) = refs[: 2 * quads], refs[2 * quads : 2 * quads + 3], refs[2 * quads + 3 :]
     core, quad, _, _ = here()
     count = quads // 2
     rows, half = refs[0].shape
@@ -194,9 +201,12 @@
         column = pl.multiple_of((core if n < quads else 1 - core) * half, half)
         row = pl.multiple_of((slot % count) * rows, rows)
         return slot // count, [
-            pltpu.make_async_copy(buffer.at[n], out.at[pl.ds(row, rows), pl.ds(column, half)], sems.at[n]) for out in outs
+            pltpu.make_async_copy(buffer.at[n], out.at[pl.ds(row, rows), pl.ds(column, half)], sems.at[n])
+            for out in outs[:2]
         ]
 
+    last = pltpu.make_async_copy(rows_ref, outs[2], sems.at[2 * quads])
+    last.start()
     for n, ref in enumerate(refs):
         which, pair = copies(n)
         buffer[n] = ref[...].astype(F32) * jnp.where(which == 0, scales[0], scales[1])
@@ -206,6 +216,7 @@
         which, pair = copies(n)
         for k in range(2):
             pl.when(which == k)(pair[k].wait)
+    last.wait()
 
 
 def local(row_devices, blk_devices, source_table, target_table, message_weight, self_weight, tile_lists, key_offsets, list_lengths, cotangent):
@@ -300,7 +311,10 @@
         inputs=4,
         flops=4 * square,
     )(links, their_links, grad, grad_received)
-    _, received = lax.optimization_barrier((sources, received))
+    target_gradient, updated = call(
+        target_side, "target_side", (shaped((targets, width), BF16),) * 2, inputs=6
+    )(self_weight, cot0, grad, grad_received, updated, updated_received)
+    _, received, target_gradient, updated = lax.optimization_barrier((sources, received, target_gradient, updated))
 
     state = [[sources[0], sources[1]], [sources[2], sources[3]]]
 
@@ -321,11 +335,6 @@
     while mask < layers:
         other = swap(total, 2 * quads * mask, devices)
         came = source_step(n)
-        if mask == 1:
-            target_gradient, updated = call(
-                target_side, "target_side", (shaped((targets, width), BF16),) * 2, inputs=6, flops=square
-            )(self_weight, cot0, grad, grad_received, updated, updated_received)
-            other, target_gradient, updated = lax.optimization_barrier((other, target_gradient, updated))
         total = call(add_up, "weight_sum", shaped((piece, half), BF16), inputs=2)(total, other)
         source_add(n, came)
         mask, n = 2 * mask, n + 1
@@ -333,17 +342,19 @@
         source_add(n, source_step(n))
         n += 1
     stays, goes = state[0][0], state[1][0]
+    total = lax.optimization_barrier((total, goes))[0]
     pieces = {0: total}
     for m in reversed(range(1, quads)):
         pieces[m] = swap(total, 2 * m, devices)
 
-    mask = layers
-    while mask > 1:
-        mask //= 2
+    mask = 1
+    while mask < layers:
         came = swap(goes, 2 * quads * mask, devices)
-        if mask == 1:
-            source_gradient = call(finish_source, "finish_source", shaped((share, width), BF16), inputs=3)(
-                message_weight, stays, came
+        mask *= 2
+        if mask == layers:
+            rounded = call(halve, "source_sum", [shaped((share, width), BF16)], inputs=2)(stays, came)[0]
+            source_rows = call(project_back, "project_back", pltpu.VMEM((share, width), BF16), inputs=2)(
+                swap(rounded, 1, devices), message_weight
             )
         else:
             rows = stays.shape[0] // 2
@@ -353,14 +364,17 @@
 
     their_pieces = {m: swap(value, 1, devices) for m, value in pieces.items()}
     scales = ((targets * devices) ** (-0.5), (block_rows * blk_devices) ** (-0.5))
-    self_gradient, message_gradient = call(
-        functools.partial(finish_weights, quads, scales),
-        "finish_weights",
-        (shaped((width, width), F32),) * 2,
-        inputs=2 * quads,
-        out_specs=(HBM, HBM),
-        scratch_shapes=[pltpu.VMEM((2 * quads, piece, half), F32), pltpu.SemaphoreType.DMA((2 * quads,))],
-    )(*[values[m] for values in (pieces, their_pieces) for m in range(quads)])
+    self_gradient, message_gradient, source_gradient = call(
+        functools.partial(finish, quads, scales),
+        "finish",
+        (shaped((width, width), F32),) * 2 + (shaped((share, width), BF16),),
+        inputs=1 + 2 * quads,
+        out_specs=(HBM, HBM, HBM),
+        scratch_shapes=[
+            pltpu.VMEM((2 * quads, piece, half), F32),
+            pltpu.SemaphoreType.DMA((2 * quads + 1,)),
+        ],
+    )(source_rows, *[values[m] for values in (pieces, their_pieces) for m in range(quads)])
     return (updated, target_gradient, source_gradient, self_gradient, message_gradient)
 
 

time: 60.3 us -> 57.3 us (0.950)
  waiting for transfers between devices: 20.7 us -> 16.6 us
  starting transfers between devices: 23.1 us -> 24.8 us
    ppermute x26 -> x27, waiting for transfers between devices: 20.7 us -> 16.6 us  [swap(): return lax.ppermute(value, AXES, [(i, i ^ mask) for i in range(devices)])]
    ppermute x26 -> x27, starting transfers between devices: 23.1 us -> 24.8 us  [swap(): return lax.ppermute(value, AXES, [(i, i ^ mask) for i in range(devices)])]
    pallas_call x2 -> x3, Pallas kernels: 2.34 us -> 1.73 us  [the longest x1 1.43 us: local(): call(functools.partial(finish, quads, scales), 'finish', (shaped((width,...]
  transfers between devices with their start and end apart: 26 -> 27, of which waited for: 12 -> 11; matrix products, arithmetic and copies ran while one was open for 2% -> 3% of each run, Pallas kernels for 12% -> 10%
where the time goes in v4:
time: 57.3 us; the launch traced here: 57 us
  starting transfers between devices  24.8 us (43%)
  waiting for transfers between devices  16.6 us (29%)
  Pallas kernels  9.44 us (16%)
  local copies, waits for them, and re-layouts  3.15 us (5%)
  between operations  1.49 us (3%)
  other arithmetic  1.47 us (3%)
    ppermute x27, starting transfers between devices, swap(): return lax.ppermute(value, AXES, [(i, i ^ mask) for i in range(devices)])  24.8 us
    ppermute x27, waiting for transfers between devices, swap(): return lax.ppermute(value, AXES, [(i, i ^ mask) for i in range(devices)])  16.6 us
    unnamed x14, local copies, waits for them, and re-layouts  3.14 us
    pallas_call x1, Pallas kernels, local(): call(functools.partial(finish, quads, scales), 'finish', (shaped((width,...  1.43 us
    pallas_call x1, Pallas kernels, local(): call(target_side, 'target_side', (shaped((targets, width), BF16),) * 2, i...  1.4 us
    pallas_call x1, Pallas kernels, local(): call(functools.partial(gather_more, order), 'gather_more', (shaped((targe...  1.39 us
    pallas_call x1, Pallas kernels, local(): call(functools.partial(forward, order), 'forward', (shaped((2 * targets,...  1.38 us
    pallas_call x1, Pallas kernels, local(): call(functools.partial(source_terms, share, sides, orders), 'source_terms...  1.34 us
  transfers between devices with their start and end apart: 27, of which 11 were waited for; matrix products, arithmetic and copies ran while one was open for 3% of the time, Pallas kernels for 10%

profile of v4, /device:TPU:0, one launch (start us, length us, event | category | flops | bytes accessed | tf_op | source)
XLA Modules:
  0.0 57.0 jit_solution(17528842895659840101)
XLA Ops:
  0.6 3.0 %collective-permute-start.1 = (bf16[512,512]{1,0:T(8,128)(2,1)}, bf16[512,512]{1,0:T(8,128)(2,1)S(1)}, u32[]{:S(2)}, u32[]{:S(2)}) collective-permute-start(bf16[512,512]{1,0:T(8,128)(2,1)} %s_ref.1), channel_id=1, source_target_pairs={{0,2},{1,3},{2,0},{3,1},{4,6},{5,7},{6,4},{7,5},{8,10},{9,11},{10,... | collective-permute-start | bytes 1572872 | tf_op jit(solution)/shard_map/ppermute | solution.py:20
  4.3 0.7 %fusion = pred[4,4]{1,0:T(4,128)(4,1)S(1)} fusion(s32[4]{0:T(128)} %bitcast.6, pred[4]{0:T(512)(128)(4,1)S(1)} %iota_compare_fusion.1), kind=kLoop, calls=%fused_computation.2 | loop fusion | flops 32 | bytes 36 | tf_op jit(solution)/shard_map/and | solution.py:239
  5.0 0.8 %select_reduce_fusion = s32[4,512]{1,0:T(4,128)S(1)} fusion(s32[4,512]{1,0:T(4,128)} %bitcast.5, pred[4,4]{1,0:T(4,128)(4,1)S(1)} %fusion), kind=kLoop, calls=%fused_computation | loop fusion | flops 14336 | bytes 16400 | tf_op jit(solution)/shard_map/reduce_max | solution.py:240
  7.1 1.0 %copy-done = bf16[512,512]{1,0:T(8,128)(2,1)S(1)} copy-done((bf16[512,512]{1,0:T(8,128)(2,1)S(1)}, bf16[512,512]{1,0:T(8,128)(2,1)}, u32[]{:S(2)}) %copy-start) | copy-done | bytes 524312
  8.1 1.0 %copy-done.2 = bf16[512,512]{1,0:T(8,128)(2,1)S(1)} copy-done((bf16[512,512]{1,0:T(8,128)(2,1)S(1)}, bf16[512,512]{1,0:T(8,128)(2,1)}, u32[]{:S(2)}) %copy-start.2) | copy-done | bytes 524312
  9.1 1.0 %copy-done.6 = bf16[512,512]{1,0:T(8,128)(2,1)S(1)} copy-done((bf16[512,512]{1,0:T(8,128)(2,1)S(1)}, bf16[512,512]{1,0:T(8,128)(2,1)}, u32[]{:S(2)}) %copy-start.6) | copy-done | bytes 524312
  10.2 1.1 %gather_first.1 = (s32[1024,4]{1,0:T(8,128)S(1)}, f32[512,256]{1,0:T(8,128)S(1)}, f32[1024,512]{1,0:T(8,128)S(1)}, bf16[512,256]{1,0:T(8,128)(2,1)S(1)}) custom-call(s32[8,512]{1,0:T(8,128)S(1)} %concatenate.3.links0_ref, s32[8,512]{1,0:T(8,128)S(1)} %collective-permute-done.links1_ref, bf16[512,512]{1,0:T(8,128)(2,1)S(1)} %copy-done.6, ...), custom_call_target="tpu_custom_call" | custom-call | tf_op jit(solution)/shard_map/gather_first/pallas_call | solution.py:249
  11.3 4.5 %collective-permute-done.1.refs_1_ = bf16[512,512]{1,0:T(8,128)(2,1)S(1)} collective-permute-done((bf16[512,512]{1,0:T(8,128)(2,1)}, bf16[512,512]{1,0:T(8,128)(2,1)S(1)}, u32[]{:S(2)}, u32[]{:S(2)}) %collective-permute-start.1) | collective-permute-done | bytes 524320 | tf_op jit(solution)/shard_map/ppermute | solution.py:20
  15.8 1.4 %gather_more.1 = (f32[512,256]{1,0:T(8,128)S(1)}, f32[1024,512]{1,0:T(8,128)S(1)}) custom-call(s32[1024,4]{1,0:T(8,128)S(1)} %get-tuple-element.54.columns_ref, f32[1024,512]{1,0:T(8,128)S(1)} %get-tuple-element.55.h0_ref, bf16[512,512]{1,0:T(8,128)(2,1)S(1)} %collective-permute-done.2.t_ref.t1_ref, bf16[512,256]{1,0:T(8,128)(2,1)S(1)} %get-tuple-element.56.weight_ref, ...), custom_call_target="tpu_custom_call" | custom-call | tf_op jit(solution)/shard_map/gather_more/pallas_call | solution.py:268
  17.7 1.4 %forward.1 = (bf16[1024,512]{1,0:T(8,128)(2,1)S(1)}, bf16[1024,256]{1,0:T(8,128)(2,1)S(1)}, bf16[512,256]{1,0:T(8,128)(2,1)S(1)}, bf16[512,256]{1,0:T(8,128)(2,1)S(1)}) custom-call(s32[8,512]{1,0:T(8,128)S(1)} %concatenate.3.links0_ref, s32[8,512]{1,0:T(8,128)S(1)} %collective-permute-done.links1_ref, s32[1024,4]{1,0:T(8,128)S(1)} %get-tuple-element.54.columns_ref, ...), custom_call_target="tpu_custom_call" | custom-call | tf_op jit(solution)/shard_map/forward/pallas_call | solution.py:276
  19.1 0.8 %weight_terms.1 = (f32[256,256]{1,0:T(8,128)S(1)}, bf16[256,256]{1,0:T(8,128)(2,1)S(1)}, bf16[256,256]{1,0:T(8,128)(2,1)S(1)}, bf16[256,256]{1,0:T(8,128)(2,1)S(1)}) custom-call(bf16[512,512]{1,0:T(8,128)(2,1)S(1)} %copy-done.1, bf16[512,512]{1,0:T(8,128)(2,1)S(1)} %collective-permute-done.2.t_ref.t1_ref, bf16[1024,512]{1,0:T(8,128)(2,1)S(1)} %get-tuple-element.62.h_ref, ...), custom_call_target="tpu_custom_call" | custom-call | tf_op jit(solution)/shard_map/weight_terms/pallas_call | solution.py:288
  20.5 2.7 %collective-permute-start.7 = (bf16[256,256]{1,0:T(8,128)(2,1)S(1)}, bf16[256,256]{1,0:T(8,128)(2,1)S(1)}, u32[]{:S(2)}, u32[]{:S(2)}) collective-permute-start(bf16[256,256]{1,0:T(8,128)(2,1)S(1)} %get-tuple-element.66), channel_id=1, source_target_pairs={{0,6},{1,7},{2,4},{3,5},{4,2},{5,3},{6,0},{7,1},{8,14},{9,15},{10,... | collective-permute-start | bytes 393224 | tf_op jit(solution)/shard_map/ppermute | solution.py:20
  24.0 1.3 %source_terms.1 = (f32[256,512]{1,0:T(8,128)S(1)}, bf16[256,512]{1,0:T(8,128)(2,1)S(1)}, f32[256,512]{1,0:T(8,128)S(1)}, bf16[256,512]{1,0:T(8,128)(2,1)S(1)}) custom-call(s32[8,512]{1,0:T(8,128)S(1)} %concatenate.3.links0_ref, s32[8,512]{1,0:T(8,128)S(1)} %collective-permute-done.links1_ref, bf16[1024,256]{1,0:T(8,128)(2,1)S(1)} %get-tuple-element.69.grad_ref, ...), custom_call_target="tpu_custom_call" | custom-call | tf_op jit(solution)/shard_map/source_terms/pallas_call | solution.py:307
  25.4 1.8 %collective-permute-start.13 = (bf16[256,512]{1,0:T(8,128)(2,1)S(1)}, bf16[256,512]{1,0:T(8,128)(2,1)S(1)}, u32[]{:S(2)}, u32[]{:S(2)}) collective-permute-start(bf16[256,512]{1,0:T(8,128)(2,1)S(1)} %get-tuple-element.74), channel_id=1, source_target_pairs={{0,4},{1,5},{2,6},{3,7},{4,0},{5,1},{6,2},{7,3},{8,12},{9,13},{10,... | collective-permute-start | bytes 786440 | tf_op jit(solution)/shard_map/ppermute | solution.py:20
  27.1 1.5 %collective-permute-start.11 = (bf16[256,512]{1,0:T(8,128)(2,1)S(1)}, bf16[256,512]{1,0:T(8,128)(2,1)S(1)}, u32[]{:S(2)}, u32[]{:S(2)}) collective-permute-start(bf16[256,512]{1,0:T(8,128)(2,1)S(1)} %get-tuple-element.72), channel_id=1, source_target_pairs={{0,2},{1,3},{2,0},{3,1},{4,6},{5,7},{6,4},{7,5},{8,10},{9,11},{10,... | collective-permute-start | bytes 786440 | tf_op jit(solution)/shard_map/ppermute | solution.py:20
  28.7 1.4 %target_side.1 = (bf16[512,512]{1,0:T(8,128)(2,1)}, bf16[512,512]{1,0:T(8,128)(2,1)}) custom-call(bf16[512,512]{1,0:T(8,128)(2,1)S(1)} %copy-done.3, bf16[512,512]{1,0:T(8,128)(2,1)S(1)} %copy-done.4, bf16[1024,256]{1,0:T(8,128)(2,1)S(1)} %get-tuple-element.69.grad_ref, bf16[1024,256]{1,0:T(8,128)(2,1)S(1)} %collective-permute-done.6.other_ref.grad_received_ref, ...), custom_call_target="tpu_custom_call" | custom-call | tf_op jit(solution)/shard_map/target_side/pallas_call | solution.py:314
  30.1 0.8 %collective-permute-done.8.refs_2_ = bf16[256,256]{1,0:T(8,128)(2,1)S(1)} collective-permute-done((bf16[256,256]{1,0:T(8,128)(2,1)S(1)}, bf16[256,256]{1,0:T(8,128)(2,1)S(1)}, u32[]{:S(2)}, u32[]{:S(2)}) %collective-permute-start.8) | collective-permute-done | bytes 131104 | tf_op jit(solution)/shard_map/ppermute | solution.py:20
  30.9 1.6 %collective-permute-start.18 = (bf16[256,256]{1,0:T(8,128)(2,1)S(1)}, bf16[256,256]{1,0:T(8,128)(2,1)S(1)}, u32[]{:S(2)}, u32[]{:S(2)}) collective-permute-start(bf16[256,256]{1,0:T(8,128)(2,1)S(1)} %weight_sum.3.refs_0_), channel_id=1, source_target_pairs={{0,8},{1,9},{2,10},{3,11},{4,12},{5,13},{6,14},{7,15},{8,0},{9,1},... | collective-permute-start | bytes 393224 | tf_op jit(solution)/shard_map/ppermute | solution.py:20
  32.6 3.2 %collective-permute-done.13.received_ref = bf16[256,512]{1,0:T(8,128)(2,1)S(1)} collective-permute-done((bf16[256,512]{1,0:T(8,128)(2,1)S(1)}, bf16[256,512]{1,0:T(8,128)(2,1)S(1)}, u32[]{:S(2)}, u32[]{:S(2)}) %collective-permute-start.13) | collective-permute-done | bytes 262176 | tf_op jit(solution)/shard_map/ppermute | solution.py:20
  36.2 2.8 %collective-permute-start.19 = (bf16[256,256]{1,0:T(8,128)(2,1)S(1)}, bf16[256,256]{1,0:T(8,128)(2,1)S(1)}, u32[]{:S(2)}, u32[]{:S(2)}) collective-permute-start(bf16[256,256]{1,0:T(8,128)(2,1)S(1)} %weight_sum.4.refs_0_), channel_id=1, source_target_pairs={{0,16},{1,17},{2,18},{3,19},{4,20},{5,21},{6,22},{7,23},{8,24},{9,... | collective-permute-start | bytes 393224 | tf_op jit(solution)/shard_map/ppermute | solution.py:20
  39.1 1.6 %collective-permute-start.12 = (bf16[128,512]{1,0:T(8,128)(2,1)S(1)}, bf16[128,512]{1,0:T(8,128)(2,1)S(1)}, u32[]{:S(2)}, u32[]{:S(2)}) collective-permute-start(bf16[128,512]{1,0:T(8,128)(2,1)S(1)} %get-tuple-element.82), channel_id=1, source_target_pairs={{0,4},{1,5},{2,6},{3,7},{4,0},{5,1},{6,2},{7,3},{8,12},{9,13},{10,... | collective-permute-start | bytes 393224 | tf_op jit(solution)/shard_map/ppermute | solution.py:20
  40.9 1.6 %collective-permute-start.15 = (bf16[128,512]{1,0:T(8,128)(2,1)S(1)}, bf16[128,512]{1,0:T(8,128)(2,1)S(1)}, u32[]{:S(2)}, u32[]{:S(2)}) collective-permute-start(bf16[128,512]{1,0:T(8,128)(2,1)S(1)} %source_sum.9), channel_id=1, source_target_pairs={{0,8},{1,9},{2,10},{3,11},{4,12},{5,13},{6,14},{7,15},{8,0},{9,1},... | collective-permute-start | bytes 393224 | tf_op jit(solution)/shard_map/ppermute | solution.py:20
  42.5 2.1 %collective-permute-done.19.refs_1_ = bf16[256,256]{1,0:T(8,128)(2,1)S(1)} collective-permute-done((bf16[256,256]{1,0:T(8,128)(2,1)S(1)}, bf16[256,256]{1,0:T(8,128)(2,1)S(1)}, u32[]{:S(2)}, u32[]{:S(2)}) %collective-permute-start.19) | collective-permute-done | bytes 131104 | tf_op jit(solution)/shard_map/ppermute | solution.py:20
  44.6 1.7 %collective-permute-start.20 = (bf16[256,256]{1,0:T(8,128)(2,1)S(1)}, bf16[256,256]{1,0:T(8,128)(2,1)S(1)}, u32[]{:S(2)}, u32[]{:S(2)}) collective-permute-start(bf16[256,256]{1,0:T(8,128)(2,1)S(1)} %weight_sum.5.refs_0_), channel_id=1, source_target_pairs={{0,2},{1,3},{2,0},{3,1},{4,6},{5,7},{6,4},{7,5},{8,10},{9,11},{10,... | collective-permute-start | bytes 393224 | tf_op jit(solution)/shard_map/ppermute | solution.py:20
  46.3 1.5 %collective-permute-start.21 = (bf16[256,256]{1,0:T(8,128)(2,1)S(1)}, bf16[256,256]{1,0:T(8,128)(2,1)S(1)}, u32[]{:S(2)}, u32[]{:S(2)}) collective-permute-start(bf16[256,256]{1,0:T(8,128)(2,1)S(1)} %weight_sum.5.refs_0_), channel_id=1, source_target_pairs={{0,4},{1,5},{2,6},{3,7},{4,0},{5,1},{6,2},{7,3},{8,12},{9,13},{10,... | collective-permute-start | bytes 393224 | tf_op jit(solution)/shard_map/ppermute | solution.py:20
  48.3 1.2 %collective-permute-start.16 = (bf16[64,512]{1,0:T(8,128)(2,1)S(1)}, bf16[64,512]{1,0:T(8,128)(2,1)S(1)}, u32[]{:S(2)}, u32[]{:S(2)}) collective-permute-start(bf16[64,512]{1,0:T(8,128)(2,1)S(1)} %get-tuple-element.86), channel_id=1, source_target_pairs={{0,16},{1,17},{2,18},{3,19},{4,20},{5,21},{6,22},{7,23},{8,24},{9,... | collective-permute-start | bytes 196616 | tf_op jit(solution)/shard_map/ppermute | solution.py:20
  49.5 1.2 %collective-permute-done.20.refs_1_ = bf16[256,256]{1,0:T(8,128)(2,1)S(1)} collective-permute-done((bf16[256,256]{1,0:T(8,128)(2,1)S(1)}, bf16[256,256]{1,0:T(8,128)(2,1)S(1)}, u32[]{:S(2)}, u32[]{:S(2)}) %collective-permute-start.20) | collective-permute-done | bytes 131104 | tf_op jit(solution)/shard_map/ppermute | solution.py:20
  50.7 0.8 %collective-permute-done.21.refs_2_ = bf16[256,256]{1,0:T(8,128)(2,1)S(1)} collective-permute-done((bf16[256,256]{1,0:T(8,128)(2,1)S(1)}, bf16[256,256]{1,0:T(8,128)(2,1)S(1)}, u32[]{:S(2)}, u32[]{:S(2)}) %collective-permute-start.21) | collective-permute-done | bytes 131104 | tf_op jit(solution)/shard_map/ppermute | solution.py:20
  51.5 2.2 %collective-permute-done.22.refs_3_ = bf16[256,256]{1,0:T(8,128)(2,1)S(1)} collective-permute-done((bf16[256,256]{1,0:T(8,128)(2,1)S(1)}, bf16[256,256]{1,0:T(8,128)(2,1)S(1)}, u32[]{:S(2)}, u32[]{:S(2)}) %collective-permute-start.22) | collective-permute-done | bytes 131104 | tf_op jit(solution)/shard_map/ppermute | solution.py:20
  53.8 0.6 %collective-permute-start.17 = (bf16[64,512]{1,0:T(8,128)(2,1)S(1)}, bf16[64,512]{1,0:T(8,128)(2,1)S(1)}, u32[]{:S(2)}, u32[]{:S(2)}) collective-permute-start(bf16[64,512]{1,0:T(8,128)(2,1)S(1)} %source_sum.11), channel_id=1, source_target_pairs={{0,1},{1,0},{2,3},{3,2},{4,5},{5,4},{6,7},{7,6},{8,9},{9,8},{10,11... | collective-permute-start | bytes 196616 | tf_op jit(solution)/shard_map/ppermute | solution.py:20
  54.3 0.9 %collective-permute-done.17.total_ref = bf16[64,512]{1,0:T(8,128)(2,1)S(1)} collective-permute-done((bf16[64,512]{1,0:T(8,128)(2,1)S(1)}, bf16[64,512]{1,0:T(8,128)(2,1)S(1)}, u32[]{:S(2)}, u32[]{:S(2)}) %collective-permute-start.17) | collective-permute-done | bytes 65568 | tf_op jit(solution)/shard_map/ppermute | solution.py:20
  55.6 1.4 %finish.1 = (f32[512,512]{1,0:T(8,128)}, f32[512,512]{1,0:T(8,128)}, bf16[64,512]{1,0:T(8,128)(2,1)}) custom-call(bf16[64,512]{1,0:T(8,128)(2,1)S(1)} %project_back.1.rows_ref, bf16[256,256]{1,0:T(8,128)(2,1)S(1)} %weight_sum.5.refs_0_, bf16[256,256]{1,0:T(8,128)(2,1)S(1)} %collective-permute-done.20.refs_1_, ...), custom_call_target="tpu_custom_call" | custom-call | tf_op jit(solution)/shard_map/finish/pallas_call | solution.py:367
  (57 shorter events, 4.6 us)
Async XLA Ops:
  0.6 15.2 %collective-permute-start.1 = (bf16[512,512]{1,0:T(8,128)(2,1)}, bf16[512,512]{1,0:T(8,128)(2,1)S(1)}, u32[]{:S(2)}, u32[]{:S(2)}) collective-permute-start(bf16[512,512]{1,0:T(8,128)(2,1)} %s_ref.1), channel_id=1, source_target_pairs={{0,2},{1,3},{2,0},{3,1},{4,6},{5,7},{6,4},{7,5},{8,10},{9,11},{10,... | collective-permute-start | bytes 1572872 | tf_op jit(solution)/shard_map/ppermute | solution.py:20
  5.8 1.2 %collective-permute-start = (s32[8,512]{1,0:T(8,128)S(1)}, s32[8,512]{1,0:T(8,128)S(1)}, u32[]{:S(2)}, u32[]{:S(2)}) collective-permute-start(s32[8,512]{1,0:T(8,128)S(1)} %concatenate.3.links0_ref), channel_id=1, source_target_pairs={{0,1},{1,0},{2,3},{3,2},{4,5},{5,4},{6,7},{7,6},{8,9},{9,8},{10,11... | collective-permute-start | bytes 49160 | tf_op jit(solution)/shard_map/ppermute | solution.py:20
  5.9 9.9 %collective-permute-start.3 = (bf16[512,512]{1,0:T(8,128)(2,1)}, bf16[512,512]{1,0:T(8,128)(2,1)S(1)}, u32[]{:S(2)}, u32[]{:S(2)}) collective-permute-start(bf16[512,512]{1,0:T(8,128)(2,1)} %s_ref.1), channel_id=1, source_target_pairs={{0,1},{1,0},{2,3},{3,2},{4,5},{5,4},{6,7},{7,6},{8,9},{9,8},{10,11... | collective-permute-start | bytes 1572872 | tf_op jit(solution)/shard_map/ppermute | solution.py:20
  6.4 9.4 %collective-permute-start.2 = (bf16[512,512]{1,0:T(8,128)(2,1)}, bf16[512,512]{1,0:T(8,128)(2,1)S(1)}, u32[]{:S(2)}, u32[]{:S(2)}) collective-permute-start(bf16[512,512]{1,0:T(8,128)(2,1)} %t0_ref.3), channel_id=1, source_target_pairs={{0,1},{1,0},{2,3},{3,2},{4,5},{5,4},{6,7},{7,6},{8,9},{9,8},{10,11... | collective-permute-start | bytes 1572872 | tf_op jit(solution)/shard_map/ppermute | solution.py:20
  6.5 10.8 %collective-permute-start.4 = (bf16[512,512]{1,0:T(8,128)(2,1)}, bf16[512,512]{1,0:T(8,128)(2,1)S(1)}, u32[]{:S(2)}, u32[]{:S(2)}) collective-permute-start(bf16[512,512]{1,0:T(8,128)(2,1)} %cot_ref.1), channel_id=1, source_target_pairs={{0,1},{1,0},{2,3},{3,2},{4,5},{5,4},{6,7},{7,6},{8,9},{9,8},{10,11... | collective-permute-start | bytes 1572872 | tf_op jit(solution)/shard_map/ppermute | solution.py:20
  7.1 1.0 %copy-start = (bf16[512,512]{1,0:T(8,128)(2,1)S(1)}, bf16[512,512]{1,0:T(8,128)(2,1)}, u32[]{:S(2)}) copy-start(bf16[512,512]{1,0:T(8,128)(2,1)} %t0_ref.3) | copy-start | bytes 1572868
  15.8 1.9 %copy-start.1 = (bf16[512,512]{1,0:T(8,128)(2,1)S(1)}, bf16[512,512]{1,0:T(8,128)(2,1)}, u32[]{:S(2)}) copy-start(bf16[512,512]{1,0:T(8,128)(2,1)} %t0_ref.3) | copy-start | bytes 1572868
  15.8 1.9 %copy-start.4 = (bf16[512,512]{1,0:T(8,128)(2,1)S(1)}, bf16[512,512]{1,0:T(8,128)(2,1)}, u32[]{:S(2)}) copy-start(bf16[512,512]{1,0:T(8,128)(2,1)} %cot_ref.1) | copy-start | bytes 1572868
  15.8 1.9 %copy-start.5 = (bf16[512,512]{1,0:T(8,128)(2,1)S(1)}, bf16[512,512]{1,0:T(8,128)(2,1)}, u32[]{:S(2)}) copy-start(bf16[512,512]{1,0:T(8,128)(2,1)} %wm_ref.3) | copy-start | bytes 1572868
  15.8 1.9 %collective-permute-start.5 = (bf16[512,512]{1,0:T(8,128)(2,1)S(1)}, bf16[512,512]{1,0:T(8,128)(2,1)S(1)}, u32[]{:S(2)}, u32[]{:S(2)}) collective-permute-start(bf16[512,512]{1,0:T(8,128)(2,1)S(1)} %collective-permute-done.1.refs_1_), channel_id=1, source_target_pairs={{0,1},{1,0},{2,3},{3,2},{4,5},{5,4},{6,7},{7,6},{8,9},{9,8},{10,11... | collective-permute-start | bytes 1572872 | tf_op jit(solution)/shard_map/ppermute | solution.py:20
  19.1 9.5 %copy-start.3 = (bf16[512,512]{1,0:T(8,128)(2,1)S(1)}, bf16[512,512]{1,0:T(8,128)(2,1)}, u32[]{:S(2)}) copy-start(bf16[512,512]{1,0:T(8,128)(2,1)} %ws_ref.3) | copy-start | bytes 1572868
  19.9 4.1 %collective-permute-start.6 = (bf16[1024,256]{1,0:T(8,128)(2,1)S(1)}, bf16[1024,256]{1,0:T(8,128)(2,1)S(1)}, u32[]{:S(2)}, u32[]{:S(2)}) collective-permute-start(bf16[1024,256]{1,0:T(8,128)(2,1)S(1)} %get-tuple-element.69.grad_ref), channel_id=1, source_target_pairs={{0,1},{1,0},{2,3},{3,2},{4,5},{5,4},{6,7},{7,6},{8,9},{9,8},{10,11... | collective-permute-start | bytes 1572872 | tf_op jit(solution)/shard_map/ppermute | solution.py:20
  20.2 6.9 %collective-permute-start.10 = (bf16[512,256]{1,0:T(8,128)(2,1)S(1)}, bf16[512,256]{1,0:T(8,128)(2,1)S(1)}, u32[]{:S(2)}, u32[]{:S(2)}) collective-permute-start(bf16[512,256]{1,0:T(8,128)(2,1)S(1)} %get-tuple-element.76), channel_id=1, source_target_pairs={{0,1},{1,0},{2,3},{3,2},{4,5},{5,4},{6,7},{7,6},{8,9},{9,8},{10,11... | collective-permute-start | bytes 786440 | tf_op jit(solution)/shard_map/ppermute | solution.py:20
  20.5 9.5 %collective-permute-start.7 = (bf16[256,256]{1,0:T(8,128)(2,1)S(1)}, bf16[256,256]{1,0:T(8,128)(2,1)S(1)}, u32[]{:S(2)}, u32[]{:S(2)}) collective-permute-start(bf16[256,256]{1,0:T(8,128)(2,1)S(1)} %get-tuple-element.66), channel_id=1, source_target_pairs={{0,6},{1,7},{2,4},{3,5},{4,2},{5,3},{6,0},{7,1},{8,14},{9,15},{10,... | collective-permute-start | bytes 393224 | tf_op jit(solution)/shard_map/ppermute | solution.py:20
  23.2 7.7 %collective-permute-start.8 = (bf16[256,256]{1,0:T(8,128)(2,1)S(1)}, bf16[256,256]{1,0:T(8,128)(2,1)S(1)}, u32[]{:S(2)}, u32[]{:S(2)}) collective-permute-start(bf16[256,256]{1,0:T(8,128)(2,1)S(1)} %get-tuple-element.65), channel_id=1, source_target_pairs={{0,4},{1,5},{2,6},{3,7},{4,0},{5,1},{6,2},{7,3},{8,12},{9,13},{10,... | collective-permute-start | bytes 393224 | tf_op jit(solution)/shard_map/ppermute | solution.py:20
  23.7 7.2 %collective-permute-start.9 = (bf16[256,256]{1,0:T(8,128)(2,1)S(1)}, bf16[256,256]{1,0:T(8,128)(2,1)S(1)}, u32[]{:S(2)}, u32[]{:S(2)}) collective-permute-start(bf16[256,256]{1,0:T(8,128)(2,1)S(1)} %get-tuple-element.64), channel_id=1, source_target_pairs={{0,2},{1,3},{2,0},{3,1},{4,6},{5,7},{6,4},{7,5},{8,10},{9,11},{10,... | collective-permute-start | bytes 393224 | tf_op jit(solution)/shard_map/ppermute | solution.py:20
  25.4 10.4 %collective-permute-start.13 = (bf16[256,512]{1,0:T(8,128)(2,1)S(1)}, bf16[256,512]{1,0:T(8,128)(2,1)S(1)}, u32[]{:S(2)}, u32[]{:S(2)}) collective-permute-start(bf16[256,512]{1,0:T(8,128)(2,1)S(1)} %get-tuple-element.74), channel_id=1, source_target_pairs={{0,4},{1,5},{2,6},{3,7},{4,0},{5,1},{6,2},{7,3},{8,12},{9,13},{10,... | collective-permute-start | bytes 786440 | tf_op jit(solution)/shard_map/ppermute | solution.py:20
  27.1 11.9 %collective-permute-start.11 = (bf16[256,512]{1,0:T(8,128)(2,1)S(1)}, bf16[256,512]{1,0:T(8,128)(2,1)S(1)}, u32[]{:S(2)}, u32[]{:S(2)}) collective-permute-start(bf16[256,512]{1,0:T(8,128)(2,1)S(1)} %get-tuple-element.72), channel_id=1, source_target_pairs={{0,2},{1,3},{2,0},{3,1},{4,6},{5,7},{6,4},{7,5},{8,10},{9,11},{10,... | collective-permute-start | bytes 786440 | tf_op jit(solution)/shard_map/ppermute | solution.py:20
  30.9 5.2 %collective-permute-start.18 = (bf16[256,256]{1,0:T(8,128)(2,1)S(1)}, bf16[256,256]{1,0:T(8,128)(2,1)S(1)}, u32[]{:S(2)}, u32[]{:S(2)}) collective-permute-start(bf16[256,256]{1,0:T(8,128)(2,1)S(1)} %weight_sum.3.refs_0_), channel_id=1, source_target_pairs={{0,8},{1,9},{2,10},{3,11},{4,12},{5,13},{6,14},{7,15},{8,0},{9,1},... | collective-permute-start | bytes 393224 | tf_op jit(solution)/shard_map/ppermute | solution.py:20
  35.8 5.0 %collective-permute-start.14 = (bf16[128,512]{1,0:T(8,128)(2,1)S(1)}, bf16[128,512]{1,0:T(8,128)(2,1)S(1)}, u32[]{:S(2)}, u32[]{:S(2)}) collective-permute-start(bf16[128,512]{1,0:T(8,128)(2,1)S(1)} %get-tuple-element.84), channel_id=1, source_target_pairs={{0,2},{1,3},{2,0},{3,1},{4,6},{5,7},{6,4},{7,5},{8,10},{9,11},{10,... | collective-permute-start | bytes 393224 | tf_op jit(solution)/shard_map/ppermute | solution.py:20
  36.2 8.4 %collective-permute-start.19 = (bf16[256,256]{1,0:T(8,128)(2,1)S(1)}, bf16[256,256]{1,0:T(8,128)(2,1)S(1)}, u32[]{:S(2)}, u32[]{:S(2)}) collective-permute-start(bf16[256,256]{1,0:T(8,128)(2,1)S(1)} %weight_sum.4.refs_0_), channel_id=1, source_target_pairs={{0,16},{1,17},{2,18},{3,19},{4,20},{5,21},{6,22},{7,23},{8,24},{9,... | collective-permute-start | bytes 393224 | tf_op jit(solution)/shard_map/ppermute | solution.py:20
  39.1 9.1 %collective-permute-start.12 = (bf16[128,512]{1,0:T(8,128)(2,1)S(1)}, bf16[128,512]{1,0:T(8,128)(2,1)S(1)}, u32[]{:S(2)}, u32[]{:S(2)}) collective-permute-start(bf16[128,512]{1,0:T(8,128)(2,1)S(1)} %get-tuple-element.82), channel_id=1, source_target_pairs={{0,4},{1,5},{2,6},{3,7},{4,0},{5,1},{6,2},{7,3},{8,12},{9,13},{10,... | collective-permute-start | bytes 393224 | tf_op jit(solution)/shard_map/ppermute | solution.py:20
  40.9 7.4 %collective-permute-start.15 = (bf16[128,512]{1,0:T(8,128)(2,1)S(1)}, bf16[128,512]{1,0:T(8,128)(2,1)S(1)}, u32[]{:S(2)}, u32[]{:S(2)}) collective-permute-start(bf16[128,512]{1,0:T(8,128)(2,1)S(1)} %source_sum.9), channel_id=1, source_target_pairs={{0,8},{1,9},{2,10},{3,11},{4,12},{5,13},{6,14},{7,15},{8,0},{9,1},... | collective-permute-start | bytes 393224 | tf_op jit(solution)/shard_map/ppermute | solution.py:20
  44.6 6.1 %collective-permute-start.20 = (bf16[256,256]{1,0:T(8,128)(2,1)S(1)}, bf16[256,256]{1,0:T(8,128)(2,1)S(1)}, u32[]{:S(2)}, u32[]{:S(2)}) collective-permute-start(bf16[256,256]{1,0:T(8,128)(2,1)S(1)} %weight_sum.5.refs_0_), channel_id=1, source_target_pairs={{0,2},{1,3},{2,0},{3,1},{4,6},{5,7},{6,4},{7,5},{8,10},{9,11},{10,... | collective-permute-start | bytes 393224 | tf_op jit(solution)/shard_map/ppermute | solution.py:20
  46.3 5.2 %collective-permute-start.21 = (bf16[256,256]{1,0:T(8,128)(2,1)S(1)}, bf16[256,256]{1,0:T(8,128)(2,1)S(1)}, u32[]{:S(2)}, u32[]{:S(2)}) collective-permute-start(bf16[256,256]{1,0:T(8,128)(2,1)S(1)} %weight_sum.5.refs_0_), channel_id=1, source_target_pairs={{0,4},{1,5},{2,6},{3,7},{4,0},{5,1},{6,2},{7,3},{8,12},{9,13},{10,... | collective-permute-start | bytes 393224 | tf_op jit(solution)/shard_map/ppermute | solution.py:20
  47.9 5.9 %collective-permute-start.22 = (bf16[256,256]{1,0:T(8,128)(2,1)S(1)}, bf16[256,256]{1,0:T(8,128)(2,1)S(1)}, u32[]{:S(2)}, u32[]{:S(2)}) collective-permute-start(bf16[256,256]{1,0:T(8,128)(2,1)S(1)} %weight_sum.5.refs_0_), channel_id=1, source_target_pairs={{0,6},{1,7},{2,4},{3,5},{4,2},{5,3},{6,0},{7,1},{8,14},{9,15},{10,... | collective-permute-start | bytes 393224 | tf_op jit(solution)/shard_map/ppermute | solution.py:20
  48.3 5.5 %collective-permute-start.16 = (bf16[64,512]{1,0:T(8,128)(2,1)S(1)}, bf16[64,512]{1,0:T(8,128)(2,1)S(1)}, u32[]{:S(2)}, u32[]{:S(2)}) collective-permute-start(bf16[64,512]{1,0:T(8,128)(2,1)S(1)} %get-tuple-element.86), channel_id=1, source_target_pairs={{0,16},{1,17},{2,18},{3,19},{4,20},{5,21},{6,22},{7,23},{8,24},{9,... | collective-permute-start | bytes 196616 | tf_op jit(solution)/shard_map/ppermute | solution.py:20
  49.5 6.1 %collective-permute-start.23 = (bf16[256,256]{1,0:T(8,128)(2,1)S(1)}, bf16[256,256]{1,0:T(8,128)(2,1)S(1)}, u32[]{:S(2)}, u32[]{:S(2)}) collective-permute-start(bf16[256,256]{1,0:T(8,128)(2,1)S(1)} %weight_sum.5.refs_0_), channel_id=1, source_target_pairs={{0,1},{1,0},{2,3},{3,2},{4,5},{5,4},{6,7},{7,6},{8,9},{9,8},{10,11... | collective-permute-start | bytes 393224 | tf_op jit(solution)/shard_map/ppermute | solution.py:20
  50.7 4.8 %collective-permute-start.24 = (bf16[256,256]{1,0:T(8,128)(2,1)S(1)}, bf16[256,256]{1,0:T(8,128)(2,1)S(1)}, u32[]{:S(2)}, u32[]{:S(2)}) collective-permute-start(bf16[256,256]{1,0:T(8,128)(2,1)S(1)} %collective-permute-done.20.refs_1_), channel_id=1, source_target_pairs={{0,1},{1,0},{2,3},{3,2},{4,5},{5,4},{6,7},{7,6},{8,9},{9,8},{10,11... | collective-permute-start | bytes 393224 | tf_op jit(solution)/shard_map/ppermute | solution.py:20
  51.5 4.0 %collective-permute-start.25 = (bf16[256,256]{1,0:T(8,128)(2,1)S(1)}, bf16[256,256]{1,0:T(8,128)(2,1)S(1)}, u32[]{:S(2)}, u32[]{:S(2)}) collective-permute-start(bf16[256,256]{1,0:T(8,128)(2,1)S(1)} %collective-permute-done.21.refs_2_), channel_id=1, source_target_pairs={{0,1},{1,0},{2,3},{3,2},{4,5},{5,4},{6,7},{7,6},{8,9},{9,8},{10,11... | collective-permute-start | bytes 393224 | tf_op jit(solution)/shard_map/ppermute | solution.py:20
  53.7 1.8 %collective-permute-start.26 = (bf16[256,256]{1,0:T(8,128)(2,1)S(1)}, bf16[256,256]{1,0:T(8,128)(2,1)S(1)}, u32[]{:S(2)}, u32[]{:S(2)}) collective-permute-start(bf16[256,256]{1,0:T(8,128)(2,1)S(1)} %collective-permute-done.22.refs_3_), channel_id=1, source_target_pairs={{0,1},{1,0},{2,3},{3,2},{4,5},{5,4},{6,7},{7,6},{8,9},{9,8},{10,11... | collective-permute-start | bytes 393224 | tf_op jit(solution)/shard_map/ppermute | solution.py:20
  53.8 1.5 %collective-permute-start.17 = (bf16[64,512]{1,0:T(8,128)(2,1)S(1)}, bf16[64,512]{1,0:T(8,128)(2,1)S(1)}, u32[]{:S(2)}, u32[]{:S(2)}) collective-permute-start(bf16[64,512]{1,0:T(8,128)(2,1)S(1)} %source_sum.11), channel_id=1, source_target_pairs={{0,1},{1,0},{2,3},{3,2},{4,5},{5,4},{6,7},{7,6},{8,9},{9,8},{10,11... | collective-permute-start | bytes 196616 | tf_op jit(solution)/shard_map/ppermute | solution.py:20
  (2 other events, 2.1 us)

commit v5 on v4

--- a/solution.py
+++ b/solution.py
@@ -92,7 +92,7 @@
 
 
 def forward(order, links0_ref, links1_ref, columns_ref, h0_ref, own0_ref, own1_ref, wm_ref, t0_ref, t1_ref, c0_ref, c1_ref, *refs):
-    s_refs, (h_ref, grad_ref, *updated_refs) = refs[:-4], refs[-4:]
+    s_refs, (h_ref, grad_ref, updated_ref) = refs[:-3], refs[-3:]
     core = here()[0]
     rows, width = t0_ref.shape
     weight = part(wm_ref, core)
@@ -106,7 +106,11 @@
         h_ref[span, :] = gathered
         preact = own_ref[...] + mm(gathered, weight)
         sig = jax.nn.sigmoid(preact)
-        updated_refs[i][...] = (part(t_ref, core).astype(F32) + preact * sig).astype(BF16)
+        updated = (part(t_ref, core).astype(F32) + preact * sig).astype(BF16)
+        if i == 0:
+            updated_ref[...] = updated
+        else:
+            grad_ref[2 * rows :, :] = updated
         upstream = part(c_ref, core).astype(F32)
         grad_ref[span, :] = (upstream * sig * (1.0 + preact * (1.0 - sig))).astype(BF16)
 
@@ -116,8 +120,8 @@
     quad = here()[1]
     rows, width = t0_ref.shape
     piece = own_ref.shape[0]
-    total_ref[0:width, :] = mm(t0_ref[...], grad_ref[0:rows, :], ROWS) + mm(t1_ref[...], grad_ref[rows:, :], ROWS)
-    total_ref[width:, :] = mm(h_ref[...], grad_ref[...], ROWS)
+    total_ref[0:width, :] = mm(t0_ref[...], grad_ref[0:rows, :], ROWS) + mm(t1_ref[...], grad_ref[rows : 2 * rows, :], ROWS)
+    total_ref[width:, :] = mm(h_ref[...], grad_ref[0 : 2 * rows, :], ROWS)
     for m, ref in enumerate((own_ref, *sent_refs)):
         at = pl.multiple_of((quad ^ m) * piece, piece)
         ref[...] = total_ref[pl.ds(at, piece), :].astype(ref.dtype)
@@ -173,17 +177,17 @@
     refs[-1][...] = total.astype(BF16)
 
 
-def target_side(ws_ref, cot_ref, grad_ref, grad_received_ref, held_ref, held_received_ref, out_ref, updated_ref):
+def target_side(ws_ref, cot_ref, grad_ref, grad_received_ref, held_ref, out_ref, updated_ref):
     core = here()[0]
     rows = cot_ref.shape[0]
     out_ref[...] = (
         cot_ref[...].astype(F32)
         + mm(grad_ref[0:rows, :], part(ws_ref, core), LANES)
-        + mm(grad_received_ref[rows:, :], part(ws_ref, 1 - core), LANES)
+        + mm(grad_received_ref[rows : 2 * rows, :], part(ws_ref, 1 - core), LANES)
     ).astype(BF16)
     half = held_ref.shape[1]
     updated_ref[:, pl.ds(pl.multiple_of(core * half, half), half)] = held_ref[...]
-    updated_ref[:, pl.ds(pl.multiple_of((1 - core) * half, half), half)] = held_received_ref[...]
+    updated_ref[:, pl.ds(pl.multiple_of((1 - core) * half, half), half)] = grad_received_ref[2 * rows :, :]
 
 
 def project_back(total_ref, wm_ref, out_ref):
@@ -273,10 +277,10 @@
         flops=2 * square,
     )(columns, gathered, table1, weight, *[held[m] for m in order])
     order = [m + 1 for m in direct]
-    gathered, grad, updated, updated_there = call(
+    gathered, grad, updated = call(
         functools.partial(forward, order),
         "forward",
-        (shaped((2 * targets, width), BF16), shaped((2 * targets, half), BF16)) + (shaped((targets, half), BF16),) * 2,
+        (shaped((2 * targets, width), BF16), shaped((3 * targets, half), BF16), shaped((targets, half), BF16)),
         inputs=11 + len(order),
         flops=2 * sides * square,
     )(
@@ -295,9 +299,8 @@
     )(table0, table1, gathered, grad)
     received = [swap(terms[m], 2 * m, devices) for m in reversed(range(1, quads))]
 
-    terms, grad_sent, updated_there = lax.optimization_barrier((terms, grad, updated_there))
+    terms, grad_sent = lax.optimization_barrier((terms, grad))
     grad_received = swap(grad_sent, 1, devices)
-    updated_received = swap(updated_there, 1, devices)
     masks = [1 << i for i in range(quads.bit_length() - 1)]
     routes = (masks, masks[::-1])
     orders = [[sum(mask * ((j >> (len(masks) - 1 - i)) & 1) for i, mask in enumerate(route)) for j in range(quads)] for route in routes]
@@ -312,8 +315,8 @@
         flops=4 * square,
     )(links, their_links, grad, grad_received)
     target_gradient, updated = call(
-        target_side, "target_side", (shaped((targets, width), BF16),) * 2, inputs=6
-    )(self_weight, cot0, grad, grad_received, updated, updated_received)
+        target_side, "target_side", (shaped((targets, width), BF16),) * 2, inputs=5
+    )(self_weight, cot0, grad, grad_received, updated)
     _, received, target_gradient, updated = lax.optimization_barrier((sources, received, target_gradient, updated))
 
     state = [[sources[0], sources[1]], [sources[2], sources[3]]]

time: 57.3 us -> 57.3 us (level)
    ppermute x27 -> x26, starting transfers between devices: 24.8 us -> 24.3 us  [swap(): return lax.ppermute(value, AXES, [(i, i ^ mask) for i in range(devices)])]
    ppermute x27 -> x26, waiting for transfers between devices: 16.6 us -> 17.1 us  [swap(): return lax.ppermute(value, AXES, [(i, i ^ mask) for i in range(devices)])]
  transfers between devices with their start and end apart: 27 -> 26, of which waited for: 11 -> 11; matrix products, arithmetic and copies ran while one was open for 3% -> 3% of each run, Pallas kernels for 10% -> 10%
where the time goes in v5:
time: 57.3 us; the launch traced here: 57 us
  starting transfers between devices  24.3 us (42%)
  waiting for transfers between devices  17.1 us (30%)
  Pallas kernels  9.44 us (16%)
  local copies, waits for them, and re-layouts  3.15 us (5%)
  between operations  1.49 us (3%)
  other arithmetic  1.47 us (3%)
    ppermute x26, starting transfers between devices, swap(): return lax.ppermute(value, AXES, [(i, i ^ mask) for i in range(devices)])  24.3 us
    ppermute x26, waiting for transfers between devices, swap(): return lax.ppermute(value, AXES, [(i, i ^ mask) for i in range(devices)])  17.1 us
    unnamed x14, local copies, waits for them, and re-layouts  3.14 us
    pallas_call x1, Pallas kernels, local(): call(functools.partial(finish, quads, scales), 'finish', (shaped((width,...  1.43 us
    pallas_call x1, Pallas kernels, local(): call(target_side, 'target_side', (shaped((targets, width), BF16),) * 2, i...  1.39 us
    pallas_call x1, Pallas kernels, local(): call(functools.partial(gather_more, order), 'gather_more', (shaped((targe...  1.39 us
    pallas_call x1, Pallas kernels, local(): call(functools.partial(forward, order), 'forward', (shaped((2 * targets,...  1.38 us
    pallas_call x1, Pallas kernels, local(): call(functools.partial(source_terms, share, sides, orders), 'source_terms...  1.34 us
  transfers between devices with their start and end apart: 26, of which 11 were waited for; matrix products, arithmetic and copies ran while one was open for 3% of the time, Pallas kernels for 10%

profile of v5, /device:TPU:0, one launch (start us, length us, event | category | flops | bytes accessed | tf_op | source)
XLA Modules:
  0.0 57.0 jit_solution(4369464133638416835)
XLA Ops:
  0.6 3.0 %collective-permute-start.1 = (bf16[512,512]{1,0:T(8,128)(2,1)}, bf16[512,512]{1,0:T(8,128)(2,1)S(1)}, u32[]{:S(2)}, u32[]{:S(2)}) collective-permute-start(bf16[512,512]{1,0:T(8,128)(2,1)} %s_ref.1), channel_id=1, source_target_pairs={{0,2},{1,3},{2,0},{3,1},{4,6},{5,7},{6,4},{7,5},{8,10},{9,11},{10,... | collective-permute-start | bytes 1572872 | tf_op jit(solution)/shard_map/ppermute | solution.py:20
  4.3 0.7 %fusion = pred[4,4]{1,0:T(4,128)(4,1)S(1)} fusion(s32[4]{0:T(128)} %bitcast.6, pred[4]{0:T(512)(128)(4,1)S(1)} %iota_compare_fusion.1), kind=kLoop, calls=%fused_computation.2 | loop fusion | flops 32 | bytes 36 | tf_op jit(solution)/shard_map/and | solution.py:243
  5.0 0.8 %select_reduce_fusion = s32[4,512]{1,0:T(4,128)S(1)} fusion(s32[4,512]{1,0:T(4,128)} %bitcast.5, pred[4,4]{1,0:T(4,128)(4,1)S(1)} %fusion), kind=kLoop, calls=%fused_computation | loop fusion | flops 14336 | bytes 16400 | tf_op jit(solution)/shard_map/reduce_max | solution.py:244
  7.1 1.0 %copy-done = bf16[512,512]{1,0:T(8,128)(2,1)S(1)} copy-done((bf16[512,512]{1,0:T(8,128)(2,1)S(1)}, bf16[512,512]{1,0:T(8,128)(2,1)}, u32[]{:S(2)}) %copy-start) | copy-done | bytes 524312
  8.1 1.0 %copy-done.2 = bf16[512,512]{1,0:T(8,128)(2,1)S(1)} copy-done((bf16[512,512]{1,0:T(8,128)(2,1)S(1)}, bf16[512,512]{1,0:T(8,128)(2,1)}, u32[]{:S(2)}) %copy-start.2) | copy-done | bytes 524312
  9.1 1.0 %copy-done.6 = bf16[512,512]{1,0:T(8,128)(2,1)S(1)} copy-done((bf16[512,512]{1,0:T(8,128)(2,1)S(1)}, bf16[512,512]{1,0:T(8,128)(2,1)}, u32[]{:S(2)}) %copy-start.6) | copy-done | bytes 524312
  10.2 1.1 %gather_first.1 = (s32[1024,4]{1,0:T(8,128)S(1)}, f32[512,256]{1,0:T(8,128)S(1)}, f32[1024,512]{1,0:T(8,128)S(1)}, bf16[512,256]{1,0:T(8,128)(2,1)S(1)}) custom-call(s32[8,512]{1,0:T(8,128)S(1)} %concatenate.3.links0_ref, s32[8,512]{1,0:T(8,128)S(1)} %collective-permute-done.links1_ref, bf16[512,512]{1,0:T(8,128)(2,1)S(1)} %copy-done.6, ...), custom_call_target="tpu_custom_call" | custom-call | tf_op jit(solution)/shard_map/gather_first/pallas_call | solution.py:253
  11.3 4.5 %collective-permute-done.1.refs_1_ = bf16[512,512]{1,0:T(8,128)(2,1)S(1)} collective-permute-done((bf16[512,512]{1,0:T(8,128)(2,1)}, bf16[512,512]{1,0:T(8,128)(2,1)S(1)}, u32[]{:S(2)}, u32[]{:S(2)}) %collective-permute-start.1) | collective-permute-done | bytes 524320 | tf_op jit(solution)/shard_map/ppermute | solution.py:20
  15.8 1.4 %gather_more.1 = (f32[512,256]{1,0:T(8,128)S(1)}, f32[1024,512]{1,0:T(8,128)S(1)}) custom-call(s32[1024,4]{1,0:T(8,128)S(1)} %get-tuple-element.52.columns_ref, f32[1024,512]{1,0:T(8,128)S(1)} %get-tuple-element.53.h0_ref, bf16[512,512]{1,0:T(8,128)(2,1)S(1)} %collective-permute-done.2.t_ref.t1_ref, bf16[512,256]{1,0:T(8,128)(2,1)S(1)} %get-tuple-element.54.weight_ref, ...), custom_call_target="tpu_custom_call" | custom-call | tf_op jit(solution)/shard_map/gather_more/pallas_call | solution.py:272
  17.7 1.4 %forward.1 = (bf16[1024,512]{1,0:T(8,128)(2,1)S(1)}, bf16[1536,256]{1,0:T(8,128)(2,1)S(1)}, bf16[512,256]{1,0:T(8,128)(2,1)S(1)}) custom-call(s32[8,512]{1,0:T(8,128)S(1)} %concatenate.3.links0_ref, s32[8,512]{1,0:T(8,128)S(1)} %collective-permute-done.links1_ref, s32[1024,4]{1,0:T(8,128)S(1)} %get-tuple-element.52.columns_ref, ...), custom_call_target="tpu_custom_call" | custom-call | tf_op jit(solution)/shard_map/forward/pallas_call | solution.py:280
  19.1 0.8 %weight_terms.1 = (f32[256,256]{1,0:T(8,128)S(1)}, bf16[256,256]{1,0:T(8,128)(2,1)S(1)}, bf16[256,256]{1,0:T(8,128)(2,1)S(1)}, bf16[256,256]{1,0:T(8,128)(2,1)S(1)}) custom-call(bf16[512,512]{1,0:T(8,128)(2,1)S(1)} %copy-done.1, bf16[512,512]{1,0:T(8,128)(2,1)S(1)} %collective-permute-done.2.t_ref.t1_ref, bf16[1024,512]{1,0:T(8,128)(2,1)S(1)} %get-tuple-element.60.h_ref, ...), custom_call_target="tpu_custom_call" | custom-call | tf_op jit(solution)/shard_map/weight_terms/pallas_call | solution.py:292
  20.2 2.7 %collective-permute-start.7 = (bf16[256,256]{1,0:T(8,128)(2,1)S(1)}, bf16[256,256]{1,0:T(8,128)(2,1)S(1)}, u32[]{:S(2)}, u32[]{:S(2)}) collective-permute-start(bf16[256,256]{1,0:T(8,128)(2,1)S(1)} %get-tuple-element.64), channel_id=1, source_target_pairs={{0,6},{1,7},{2,4},{3,5},{4,2},{5,3},{6,0},{7,1},{8,14},{9,15},{10,... | collective-permute-start | bytes 393224 | tf_op jit(solution)/shard_map/ppermute | solution.py:20
  23.7 1.3 %source_terms.1 = (f32[256,512]{1,0:T(8,128)S(1)}, bf16[256,512]{1,0:T(8,128)(2,1)S(1)}, f32[256,512]{1,0:T(8,128)S(1)}, bf16[256,512]{1,0:T(8,128)(2,1)S(1)}) custom-call(s32[8,512]{1,0:T(8,128)S(1)} %concatenate.3.links0_ref, s32[8,512]{1,0:T(8,128)S(1)} %collective-permute-done.links1_ref, bf16[1536,256]{1,0:T(8,128)(2,1)S(1)} %get-tuple-element.66.grad_ref, ...), custom_call_target="tpu_custom_call" | custom-call | tf_op jit(solution)/shard_map/source_terms/pallas_call | solution.py:310
  25.0 1.8 %collective-permute-start.12 = (bf16[256,512]{1,0:T(8,128)(2,1)S(1)}, bf16[256,512]{1,0:T(8,128)(2,1)S(1)}, u32[]{:S(2)}, u32[]{:S(2)}) collective-permute-start(bf16[256,512]{1,0:T(8,128)(2,1)S(1)} %get-tuple-element.71), channel_id=1, source_target_pairs={{0,4},{1,5},{2,6},{3,7},{4,0},{5,1},{6,2},{7,3},{8,12},{9,13},{10,... | collective-permute-start | bytes 786440 | tf_op jit(solution)/shard_map/ppermute | solution.py:20
  26.8 1.4 %target_side.1 = (bf16[512,512]{1,0:T(8,128)(2,1)}, bf16[512,512]{1,0:T(8,128)(2,1)}) custom-call(bf16[512,512]{1,0:T(8,128)(2,1)S(1)} %copy-done.3, bf16[512,512]{1,0:T(8,128)(2,1)S(1)} %copy-done.5, bf16[1536,256]{1,0:T(8,128)(2,1)S(1)} %get-tuple-element.66.grad_ref, bf16[1536,256]{1,0:T(8,128)(2,1)S(1)} %collective-permute-done.6.other_ref.grad_received_ref, ...), custom_call_target="tpu_custom_call" | custom-call | tf_op jit(solution)/shard_map/target_side/pallas_call | solution.py:317
  28.2 1.5 %collective-permute-start.10 = (bf16[256,512]{1,0:T(8,128)(2,1)S(1)}, bf16[256,512]{1,0:T(8,128)(2,1)S(1)}, u32[]{:S(2)}, u32[]{:S(2)}) collective-permute-start(bf16[256,512]{1,0:T(8,128)(2,1)S(1)} %get-tuple-element.69), channel_id=1, source_target_pairs={{0,2},{1,3},{2,0},{3,1},{4,6},{5,7},{6,4},{7,5},{8,10},{9,11},{10,... | collective-permute-start | bytes 786440 | tf_op jit(solution)/shard_map/ppermute | solution.py:20
  29.7 0.8 %collective-permute-done.8.refs_2_ = bf16[256,256]{1,0:T(8,128)(2,1)S(1)} collective-permute-done((bf16[256,256]{1,0:T(8,128)(2,1)S(1)}, bf16[256,256]{1,0:T(8,128)(2,1)S(1)}, u32[]{:S(2)}, u32[]{:S(2)}) %collective-permute-start.8) | collective-permute-done | bytes 131104 | tf_op jit(solution)/shard_map/ppermute | solution.py:20
  30.6 1.6 %collective-permute-start.17 = (bf16[256,256]{1,0:T(8,128)(2,1)S(1)}, bf16[256,256]{1,0:T(8,128)(2,1)S(1)}, u32[]{:S(2)}, u32[]{:S(2)}) collective-permute-start(bf16[256,256]{1,0:T(8,128)(2,1)S(1)} %weight_sum.3.refs_0_), channel_id=1, source_target_pairs={{0,8},{1,9},{2,10},{3,11},{4,12},{5,13},{6,14},{7,15},{8,0},{9,1},... | collective-permute-start | bytes 393224 | tf_op jit(solution)/shard_map/ppermute | solution.py:20
  32.2 3.3 %collective-permute-done.12.received_ref = bf16[256,512]{1,0:T(8,128)(2,1)S(1)} collective-permute-done((bf16[256,512]{1,0:T(8,128)(2,1)S(1)}, bf16[256,512]{1,0:T(8,128)(2,1)S(1)}, u32[]{:S(2)}, u32[]{:S(2)}) %collective-permute-start.12) | collective-permute-done | bytes 262176 | tf_op jit(solution)/shard_map/ppermute | solution.py:20
  36.0 2.8 %collective-permute-start.18 = (bf16[256,256]{1,0:T(8,128)(2,1)S(1)}, bf16[256,256]{1,0:T(8,128)(2,1)S(1)}, u32[]{:S(2)}, u32[]{:S(2)}) collective-permute-start(bf16[256,256]{1,0:T(8,128)(2,1)S(1)} %weight_sum.4.refs_0_), channel_id=1, source_target_pairs={{0,16},{1,17},{2,18},{3,19},{4,20},{5,21},{6,22},{7,23},{8,24},{9,... | collective-permute-start | bytes 393224 | tf_op jit(solution)/shard_map/ppermute | solution.py:20
  38.9 1.6 %collective-permute-start.11 = (bf16[128,512]{1,0:T(8,128)(2,1)S(1)}, bf16[128,512]{1,0:T(8,128)(2,1)S(1)}, u32[]{:S(2)}, u32[]{:S(2)}) collective-permute-start(bf16[128,512]{1,0:T(8,128)(2,1)S(1)} %get-tuple-element.78), channel_id=1, source_target_pairs={{0,4},{1,5},{2,6},{3,7},{4,0},{5,1},{6,2},{7,3},{8,12},{9,13},{10,... | collective-permute-start | bytes 393224 | tf_op jit(solution)/shard_map/ppermute | solution.py:20
  40.7 1.6 %collective-permute-start.14 = (bf16[128,512]{1,0:T(8,128)(2,1)S(1)}, bf16[128,512]{1,0:T(8,128)(2,1)S(1)}, u32[]{:S(2)}, u32[]{:S(2)}) collective-permute-start(bf16[128,512]{1,0:T(8,128)(2,1)S(1)} %source_sum.9), channel_id=1, source_target_pairs={{0,8},{1,9},{2,10},{3,11},{4,12},{5,13},{6,14},{7,15},{8,0},{9,1},... | collective-permute-start | bytes 393224 | tf_op jit(solution)/shard_map/ppermute | solution.py:20
  42.3 2.3 %collective-permute-done.18.refs_1_ = bf16[256,256]{1,0:T(8,128)(2,1)S(1)} collective-permute-done((bf16[256,256]{1,0:T(8,128)(2,1)S(1)}, bf16[256,256]{1,0:T(8,128)(2,1)S(1)}, u32[]{:S(2)}, u32[]{:S(2)}) %collective-permute-start.18) | collective-permute-done | bytes 131104 | tf_op jit(solution)/shard_map/ppermute | solution.py:20
  44.7 1.6 %collective-permute-start.19 = (bf16[256,256]{1,0:T(8,128)(2,1)S(1)}, bf16[256,256]{1,0:T(8,128)(2,1)S(1)}, u32[]{:S(2)}, u32[]{:S(2)}) collective-permute-start(bf16[256,256]{1,0:T(8,128)(2,1)S(1)} %weight_sum.5.refs_0_), channel_id=1, source_target_pairs={{0,2},{1,3},{2,0},{3,1},{4,6},{5,7},{6,4},{7,5},{8,10},{9,11},{10,... | collective-permute-start | bytes 393224 | tf_op jit(solution)/shard_map/ppermute | solution.py:20
  46.3 1.5 %collective-permute-start.20 = (bf16[256,256]{1,0:T(8,128)(2,1)S(1)}, bf16[256,256]{1,0:T(8,128)(2,1)S(1)}, u32[]{:S(2)}, u32[]{:S(2)}) collective-permute-start(bf16[256,256]{1,0:T(8,128)(2,1)S(1)} %weight_sum.5.refs_0_), channel_id=1, source_target_pairs={{0,4},{1,5},{2,6},{3,7},{4,0},{5,1},{6,2},{7,3},{8,12},{9,13},{10,... | collective-permute-start | bytes 393224 | tf_op jit(solution)/shard_map/ppermute | solution.py:20
  48.3 1.0 %collective-permute-start.15 = (bf16[64,512]{1,0:T(8,128)(2,1)S(1)}, bf16[64,512]{1,0:T(8,128)(2,1)S(1)}, u32[]{:S(2)}, u32[]{:S(2)}) collective-permute-start(bf16[64,512]{1,0:T(8,128)(2,1)S(1)} %get-tuple-element.82), channel_id=1, source_target_pairs={{0,16},{1,17},{2,18},{3,19},{4,20},{5,21},{6,22},{7,23},{8,24},{9,... | collective-permute-start | bytes 196616 | tf_op jit(solution)/shard_map/ppermute | solution.py:20
  49.4 0.9 %collective-permute-done.19.refs_1_ = bf16[256,256]{1,0:T(8,128)(2,1)S(1)} collective-permute-done((bf16[256,256]{1,0:T(8,128)(2,1)S(1)}, bf16[256,256]{1,0:T(8,128)(2,1)S(1)}, u32[]{:S(2)}, u32[]{:S(2)}) %collective-permute-start.19) | collective-permute-done | bytes 131104 | tf_op jit(solution)/shard_map/ppermute | solution.py:20
  50.3 1.3 %collective-permute-done.20.refs_2_ = bf16[256,256]{1,0:T(8,128)(2,1)S(1)} collective-permute-done((bf16[256,256]{1,0:T(8,128)(2,1)S(1)}, bf16[256,256]{1,0:T(8,128)(2,1)S(1)}, u32[]{:S(2)}, u32[]{:S(2)}) %collective-permute-start.20) | collective-permute-done | bytes 131104 | tf_op jit(solution)/shard_map/ppermute | solution.py:20
  51.6 2.1 %collective-permute-done.21.refs_3_ = bf16[256,256]{1,0:T(8,128)(2,1)S(1)} collective-permute-done((bf16[256,256]{1,0:T(8,128)(2,1)S(1)}, bf16[256,256]{1,0:T(8,128)(2,1)S(1)}, u32[]{:S(2)}, u32[]{:S(2)}) %collective-permute-start.21) | collective-permute-done | bytes 131104 | tf_op jit(solution)/shard_map/ppermute | solution.py:20
  53.7 0.6 %collective-permute-start.16 = (bf16[64,512]{1,0:T(8,128)(2,1)S(1)}, bf16[64,512]{1,0:T(8,128)(2,1)S(1)}, u32[]{:S(2)}, u32[]{:S(2)}) collective-permute-start(bf16[64,512]{1,0:T(8,128)(2,1)S(1)} %source_sum.11), channel_id=1, source_target_pairs={{0,1},{1,0},{2,3},{3,2},{4,5},{5,4},{6,7},{7,6},{8,9},{9,8},{10,11... | collective-permute-start | bytes 196616 | tf_op jit(solution)/shard_map/ppermute | solution.py:20
  54.3 0.9 %collective-permute-done.16.total_ref = bf16[64,512]{1,0:T(8,128)(2,1)S(1)} collective-permute-done((bf16[64,512]{1,0:T(8,128)(2,1)S(1)}, bf16[64,512]{1,0:T(8,128)(2,1)S(1)}, u32[]{:S(2)}, u32[]{:S(2)}) %collective-permute-start.16) | collective-permute-done | bytes 65568 | tf_op jit(solution)/shard_map/ppermute | solution.py:20
  55.5 1.4 %finish.1 = (f32[512,512]{1,0:T(8,128)}, f32[512,512]{1,0:T(8,128)}, bf16[64,512]{1,0:T(8,128)(2,1)}) custom-call(bf16[64,512]{1,0:T(8,128)(2,1)S(1)} %project_back.1.rows_ref, bf16[256,256]{1,0:T(8,128)(2,1)S(1)} %weight_sum.5.refs_0_, bf16[256,256]{1,0:T(8,128)(2,1)S(1)} %collective-permute-done.19.refs_1_, ...), custom_call_target="tpu_custom_call" | custom-call | tf_op jit(solution)/shard_map/finish/pallas_call | solution.py:370
  (55 shorter events, 4.4 us)
Async XLA Ops:
  0.6 15.2 %collective-permute-start.1 = (bf16[512,512]{1,0:T(8,128)(2,1)}, bf16[512,512]{1,0:T(8,128)(2,1)S(1)}, u32[]{:S(2)}, u32[]{:S(2)}) collective-permute-start(bf16[512,512]{1,0:T(8,128)(2,1)} %s_ref.1), channel_id=1, source_target_pairs={{0,2},{1,3},{2,0},{3,1},{4,6},{5,7},{6,4},{7,5},{8,10},{9,11},{10,... | collective-permute-start | bytes 1572872 | tf_op jit(solution)/shard_map/ppermute | solution.py:20
  5.8 1.2 %collective-permute-start = (s32[8,512]{1,0:T(8,128)S(1)}, s32[8,512]{1,0:T(8,128)S(1)}, u32[]{:S(2)}, u32[]{:S(2)}) collective-permute-start(s32[8,512]{1,0:T(8,128)S(1)} %concatenate.3.links0_ref), channel_id=1, source_target_pairs={{0,1},{1,0},{2,3},{3,2},{4,5},{5,4},{6,7},{7,6},{8,9},{9,8},{10,11... | collective-permute-start | bytes 49160 | tf_op jit(solution)/shard_map/ppermute | solution.py:20
  5.9 9.9 %collective-permute-start.3 = (bf16[512,512]{1,0:T(8,128)(2,1)}, bf16[512,512]{1,0:T(8,128)(2,1)S(1)}, u32[]{:S(2)}, u32[]{:S(2)}) collective-permute-start(bf16[512,512]{1,0:T(8,128)(2,1)} %s_ref.1), channel_id=1, source_target_pairs={{0,1},{1,0},{2,3},{3,2},{4,5},{5,4},{6,7},{7,6},{8,9},{9,8},{10,11... | collective-permute-start | bytes 1572872 | tf_op jit(solution)/shard_map/ppermute | solution.py:20
  6.4 9.4 %collective-permute-start.2 = (bf16[512,512]{1,0:T(8,128)(2,1)}, bf16[512,512]{1,0:T(8,128)(2,1)S(1)}, u32[]{:S(2)}, u32[]{:S(2)}) collective-permute-start(bf16[512,512]{1,0:T(8,128)(2,1)} %t0_ref.3), channel_id=1, source_target_pairs={{0,1},{1,0},{2,3},{3,2},{4,5},{5,4},{6,7},{7,6},{8,9},{9,8},{10,11... | collective-permute-start | bytes 1572872 | tf_op jit(solution)/shard_map/ppermute | solution.py:20
  6.5 10.8 %collective-permute-start.4 = (bf16[512,512]{1,0:T(8,128)(2,1)}, bf16[512,512]{1,0:T(8,128)(2,1)S(1)}, u32[]{:S(2)}, u32[]{:S(2)}) collective-permute-start(bf16[512,512]{1,0:T(8,128)(2,1)} %cot_ref.1), channel_id=1, source_target_pairs={{0,1},{1,0},{2,3},{3,2},{4,5},{5,4},{6,7},{7,6},{8,9},{9,8},{10,11... | collective-permute-start | bytes 1572872 | tf_op jit(solution)/shard_map/ppermute | solution.py:20
  7.1 1.0 %copy-start = (bf16[512,512]{1,0:T(8,128)(2,1)S(1)}, bf16[512,512]{1,0:T(8,128)(2,1)}, u32[]{:S(2)}) copy-start(bf16[512,512]{1,0:T(8,128)(2,1)} %t0_ref.3) | copy-start | bytes 1572868
  8.1 1.0 %copy-start.2 = (bf16[512,512]{1,0:T(8,128)(2,1)S(1)}, bf16[512,512]{1,0:T(8,128)(2,1)}, u32[]{:S(2)}) copy-start(bf16[512,512]{1,0:T(8,128)(2,1)} %ws_ref.3) | copy-start | bytes 1572868
  15.8 1.9 %copy-start.1 = (bf16[512,512]{1,0:T(8,128)(2,1)S(1)}, bf16[512,512]{1,0:T(8,128)(2,1)}, u32[]{:S(2)}) copy-start(bf16[512,512]{1,0:T(8,128)(2,1)} %t0_ref.3) | copy-start | bytes 1572868
  15.8 1.9 %copy-start.4 = (bf16[512,512]{1,0:T(8,128)(2,1)S(1)}, bf16[512,512]{1,0:T(8,128)(2,1)}, u32[]{:S(2)}) copy-start(bf16[512,512]{1,0:T(8,128)(2,1)} %wm_ref.3) | copy-start | bytes 1572868
  15.8 1.9 %copy-start.5 = (bf16[512,512]{1,0:T(8,128)(2,1)S(1)}, bf16[512,512]{1,0:T(8,128)(2,1)}, u32[]{:S(2)}) copy-start(bf16[512,512]{1,0:T(8,128)(2,1)} %cot_ref.1) | copy-start | bytes 1572868
  15.8 1.9 %collective-permute-start.5 = (bf16[512,512]{1,0:T(8,128)(2,1)S(1)}, bf16[512,512]{1,0:T(8,128)(2,1)S(1)}, u32[]{:S(2)}, u32[]{:S(2)}) collective-permute-start(bf16[512,512]{1,0:T(8,128)(2,1)S(1)} %collective-permute-done.1.refs_1_), channel_id=1, source_target_pairs={{0,1},{1,0},{2,3},{3,2},{4,5},{5,4},{6,7},{7,6},{8,9},{9,8},{10,11... | collective-permute-start | bytes 1572872 | tf_op jit(solution)/shard_map/ppermute | solution.py:20
  19.1 7.7 %copy-start.3 = (bf16[512,512]{1,0:T(8,128)(2,1)S(1)}, bf16[512,512]{1,0:T(8,128)(2,1)}, u32[]{:S(2)}) copy-start(bf16[512,512]{1,0:T(8,128)(2,1)} %ws_ref.3) | copy-start | bytes 1572868
  19.9 3.7 %collective-permute-start.6 = (bf16[1536,256]{1,0:T(8,128)(2,1)S(1)}, bf16[1536,256]{1,0:T(8,128)(2,1)S(1)}, u32[]{:S(2)}, u32[]{:S(2)}) collective-permute-start(bf16[1536,256]{1,0:T(8,128)(2,1)S(1)} %get-tuple-element.66.grad_ref), channel_id=1, source_target_pairs={{0,1},{1,0},{2,3},{3,2},{4,5},{5,4},{6,7},{7,6},{8,9},{9,8},{10,11... | collective-permute-start | bytes 2359304 | tf_op jit(solution)/shard_map/ppermute | solution.py:20
  20.2 9.5 %collective-permute-start.7 = (bf16[256,256]{1,0:T(8,128)(2,1)S(1)}, bf16[256,256]{1,0:T(8,128)(2,1)S(1)}, u32[]{:S(2)}, u32[]{:S(2)}) collective-permute-start(bf16[256,256]{1,0:T(8,128)(2,1)S(1)} %get-tuple-element.64), channel_id=1, source_target_pairs={{0,6},{1,7},{2,4},{3,5},{4,2},{5,3},{6,0},{7,1},{8,14},{9,15},{10,... | collective-permute-start | bytes 393224 | tf_op jit(solution)/shard_map/ppermute | solution.py:20
  22.9 7.7 %collective-permute-start.8 = (bf16[256,256]{1,0:T(8,128)(2,1)S(1)}, bf16[256,256]{1,0:T(8,128)(2,1)S(1)}, u32[]{:S(2)}, u32[]{:S(2)}) collective-permute-start(bf16[256,256]{1,0:T(8,128)(2,1)S(1)} %get-tuple-element.63), channel_id=1, source_target_pairs={{0,4},{1,5},{2,6},{3,7},{4,0},{5,1},{6,2},{7,3},{8,12},{9,13},{10,... | collective-permute-start | bytes 393224 | tf_op jit(solution)/shard_map/ppermute | solution.py:20
  23.4 7.1 %collective-permute-start.9 = (bf16[256,256]{1,0:T(8,128)(2,1)S(1)}, bf16[256,256]{1,0:T(8,128)(2,1)S(1)}, u32[]{:S(2)}, u32[]{:S(2)}) collective-permute-start(bf16[256,256]{1,0:T(8,128)(2,1)S(1)} %get-tuple-element.62), channel_id=1, source_target_pairs={{0,2},{1,3},{2,0},{3,1},{4,6},{5,7},{6,4},{7,5},{8,10},{9,11},{10,... | collective-permute-start | bytes 393224 | tf_op jit(solution)/shard_map/ppermute | solution.py:20
  25.0 10.5 %collective-permute-start.12 = (bf16[256,512]{1,0:T(8,128)(2,1)S(1)}, bf16[256,512]{1,0:T(8,128)(2,1)S(1)}, u32[]{:S(2)}, u32[]{:S(2)}) collective-permute-start(bf16[256,512]{1,0:T(8,128)(2,1)S(1)} %get-tuple-element.71), channel_id=1, source_target_pairs={{0,4},{1,5},{2,6},{3,7},{4,0},{5,1},{6,2},{7,3},{8,12},{9,13},{10,... | collective-permute-start | bytes 786440 | tf_op jit(solution)/shard_map/ppermute | solution.py:20
  28.2 10.6 %collective-permute-start.10 = (bf16[256,512]{1,0:T(8,128)(2,1)S(1)}, bf16[256,512]{1,0:T(8,128)(2,1)S(1)}, u32[]{:S(2)}, u32[]{:S(2)}) collective-permute-start(bf16[256,512]{1,0:T(8,128)(2,1)S(1)} %get-tuple-element.69), channel_id=1, source_target_pairs={{0,2},{1,3},{2,0},{3,1},{4,6},{5,7},{6,4},{7,5},{8,10},{9,11},{10,... | collective-permute-start | bytes 786440 | tf_op jit(solution)/shard_map/ppermute | solution.py:20
  30.6 5.3 %collective-permute-start.17 = (bf16[256,256]{1,0:T(8,128)(2,1)S(1)}, bf16[256,256]{1,0:T(8,128)(2,1)S(1)}, u32[]{:S(2)}, u32[]{:S(2)}) collective-permute-start(bf16[256,256]{1,0:T(8,128)(2,1)S(1)} %weight_sum.3.refs_0_), channel_id=1, source_target_pairs={{0,8},{1,9},{2,10},{3,11},{4,12},{5,13},{6,14},{7,15},{8,0},{9,1},... | collective-permute-start | bytes 393224 | tf_op jit(solution)/shard_map/ppermute | solution.py:20
  35.6 5.0 %collective-permute-start.13 = (bf16[128,512]{1,0:T(8,128)(2,1)S(1)}, bf16[128,512]{1,0:T(8,128)(2,1)S(1)}, u32[]{:S(2)}, u32[]{:S(2)}) collective-permute-start(bf16[128,512]{1,0:T(8,128)(2,1)S(1)} %get-tuple-element.80), channel_id=1, source_target_pairs={{0,2},{1,3},{2,0},{3,1},{4,6},{5,7},{6,4},{7,5},{8,10},{9,11},{10,... | collective-permute-start | bytes 393224 | tf_op jit(solution)/shard_map/ppermute | solution.py:20
  36.0 8.7 %collective-permute-start.18 = (bf16[256,256]{1,0:T(8,128)(2,1)S(1)}, bf16[256,256]{1,0:T(8,128)(2,1)S(1)}, u32[]{:S(2)}, u32[]{:S(2)}) collective-permute-start(bf16[256,256]{1,0:T(8,128)(2,1)S(1)} %weight_sum.4.refs_0_), channel_id=1, source_target_pairs={{0,16},{1,17},{2,18},{3,19},{4,20},{5,21},{6,22},{7,23},{8,24},{9,... | collective-permute-start | bytes 393224 | tf_op jit(solution)/shard_map/ppermute | solution.py:20
  38.9 9.3 %collective-permute-start.11 = (bf16[128,512]{1,0:T(8,128)(2,1)S(1)}, bf16[128,512]{1,0:T(8,128)(2,1)S(1)}, u32[]{:S(2)}, u32[]{:S(2)}) collective-permute-start(bf16[128,512]{1,0:T(8,128)(2,1)S(1)} %get-tuple-element.78), channel_id=1, source_target_pairs={{0,4},{1,5},{2,6},{3,7},{4,0},{5,1},{6,2},{7,3},{8,12},{9,13},{10,... | collective-permute-start | bytes 393224 | tf_op jit(solution)/shard_map/ppermute | solution.py:20
  40.7 7.6 %collective-permute-start.14 = (bf16[128,512]{1,0:T(8,128)(2,1)S(1)}, bf16[128,512]{1,0:T(8,128)(2,1)S(1)}, u32[]{:S(2)}, u32[]{:S(2)}) collective-permute-start(bf16[128,512]{1,0:T(8,128)(2,1)S(1)} %source_sum.9), channel_id=1, source_target_pairs={{0,8},{1,9},{2,10},{3,11},{4,12},{5,13},{6,14},{7,15},{8,0},{9,1},... | collective-permute-start | bytes 393224 | tf_op jit(solution)/shard_map/ppermute | solution.py:20
  44.7 5.6 %collective-permute-start.19 = (bf16[256,256]{1,0:T(8,128)(2,1)S(1)}, bf16[256,256]{1,0:T(8,128)(2,1)S(1)}, u32[]{:S(2)}, u32[]{:S(2)}) collective-permute-start(bf16[256,256]{1,0:T(8,128)(2,1)S(1)} %weight_sum.5.refs_0_), channel_id=1, source_target_pairs={{0,2},{1,3},{2,0},{3,1},{4,6},{5,7},{6,4},{7,5},{8,10},{9,11},{10,... | collective-permute-start | bytes 393224 | tf_op jit(solution)/shard_map/ppermute | solution.py:20
  46.3 5.3 %collective-permute-start.20 = (bf16[256,256]{1,0:T(8,128)(2,1)S(1)}, bf16[256,256]{1,0:T(8,128)(2,1)S(1)}, u32[]{:S(2)}, u32[]{:S(2)}) collective-permute-start(bf16[256,256]{1,0:T(8,128)(2,1)S(1)} %weight_sum.5.refs_0_), channel_id=1, source_target_pairs={{0,4},{1,5},{2,6},{3,7},{4,0},{5,1},{6,2},{7,3},{8,12},{9,13},{10,... | collective-permute-start | bytes 393224 | tf_op jit(solution)/shard_map/ppermute | solution.py:20
  47.8 5.9 %collective-permute-start.21 = (bf16[256,256]{1,0:T(8,128)(2,1)S(1)}, bf16[256,256]{1,0:T(8,128)(2,1)S(1)}, u32[]{:S(2)}, u32[]{:S(2)}) collective-permute-start(bf16[256,256]{1,0:T(8,128)(2,1)S(1)} %weight_sum.5.refs_0_), channel_id=1, source_target_pairs={{0,6},{1,7},{2,4},{3,5},{4,2},{5,3},{6,0},{7,1},{8,14},{9,15},{10,... | collective-permute-start | bytes 393224 | tf_op jit(solution)/shard_map/ppermute | solution.py:20
  48.3 5.4 %collective-permute-start.15 = (bf16[64,512]{1,0:T(8,128)(2,1)S(1)}, bf16[64,512]{1,0:T(8,128)(2,1)S(1)}, u32[]{:S(2)}, u32[]{:S(2)}) collective-permute-start(bf16[64,512]{1,0:T(8,128)(2,1)S(1)} %get-tuple-element.82), channel_id=1, source_target_pairs={{0,16},{1,17},{2,18},{3,19},{4,20},{5,21},{6,22},{7,23},{8,24},{9,... | collective-permute-start | bytes 196616 | tf_op jit(solution)/shard_map/ppermute | solution.py:20
  49.4 6.1 %collective-permute-start.22 = (bf16[256,256]{1,0:T(8,128)(2,1)S(1)}, bf16[256,256]{1,0:T(8,128)(2,1)S(1)}, u32[]{:S(2)}, u32[]{:S(2)}) collective-permute-start(bf16[256,256]{1,0:T(8,128)(2,1)S(1)} %weight_sum.5.refs_0_), channel_id=1, source_target_pairs={{0,1},{1,0},{2,3},{3,2},{4,5},{5,4},{6,7},{7,6},{8,9},{9,8},{10,11... | collective-permute-start | bytes 393224 | tf_op jit(solution)/shard_map/ppermute | solution.py:20
  50.3 5.2 %collective-permute-start.23 = (bf16[256,256]{1,0:T(8,128)(2,1)S(1)}, bf16[256,256]{1,0:T(8,128)(2,1)S(1)}, u32[]{:S(2)}, u32[]{:S(2)}) collective-permute-start(bf16[256,256]{1,0:T(8,128)(2,1)S(1)} %collective-permute-done.19.refs_1_), channel_id=1, source_target_pairs={{0,1},{1,0},{2,3},{3,2},{4,5},{5,4},{6,7},{7,6},{8,9},{9,8},{10,11... | collective-permute-start | bytes 393224 | tf_op jit(solution)/shard_map/ppermute | solution.py:20
  51.6 3.9 %collective-permute-start.24 = (bf16[256,256]{1,0:T(8,128)(2,1)S(1)}, bf16[256,256]{1,0:T(8,128)(2,1)S(1)}, u32[]{:S(2)}, u32[]{:S(2)}) collective-permute-start(bf16[256,256]{1,0:T(8,128)(2,1)S(1)} %collective-permute-done.20.refs_2_), channel_id=1, source_target_pairs={{0,1},{1,0},{2,3},{3,2},{4,5},{5,4},{6,7},{7,6},{8,9},{9,8},{10,11... | collective-permute-start | bytes 393224 | tf_op jit(solution)/shard_map/ppermute | solution.py:20
  53.7 1.8 %collective-permute-start.25 = (bf16[256,256]{1,0:T(8,128)(2,1)S(1)}, bf16[256,256]{1,0:T(8,128)(2,1)S(1)}, u32[]{:S(2)}, u32[]{:S(2)}) collective-permute-start(bf16[256,256]{1,0:T(8,128)(2,1)S(1)} %collective-permute-done.21.refs_3_), channel_id=1, source_target_pairs={{0,1},{1,0},{2,3},{3,2},{4,5},{5,4},{6,7},{7,6},{8,9},{9,8},{10,11... | collective-permute-start | bytes 393224 | tf_op jit(solution)/shard_map/ppermute | solution.py:20
  53.7 1.5 %collective-permute-start.16 = (bf16[64,512]{1,0:T(8,128)(2,1)S(1)}, bf16[64,512]{1,0:T(8,128)(2,1)S(1)}, u32[]{:S(2)}, u32[]{:S(2)}) collective-permute-start(bf16[64,512]{1,0:T(8,128)(2,1)S(1)} %source_sum.11), channel_id=1, source_target_pairs={{0,1},{1,0},{2,3},{3,2},{4,5},{5,4},{6,7},{7,6},{8,9},{9,8},{10,11... | collective-permute-start | bytes 196616 | tf_op jit(solution)/shard_map/ppermute | solution.py:20
  (1 other events, 1.0 us)

commit v6 on v4

--- a/solution.py
+++ b/solution.py
@@ -24,7 +24,7 @@
     return pl.pallas_call(
         body,
         name=name,
-        in_specs=[VMEM] * inputs,
+        in_specs=more.pop("in_specs", [VMEM] * inputs),
         out_shape=out_shape,
         compiler_params=pltpu.CompilerParams(vmem_limit_bytes=20 << 20),
         cost_estimate=pl.CostEstimate(flops=0, bytes_accessed=0, transcendentals=0),
@@ -190,33 +190,42 @@
     out_ref[...] = mm(total_ref[...], wm_ref[...], LANES).astype(BF16)
 
 
-def finish(quads, scales, rows_ref, *refs):
-    refs, outs, (buffer, sems) = refs[: 2 * quads], refs[2 * quads : 2 * quads + 3], refs[2 * quads + 3 :]
+def write_columns(quads, scales, side, refs, outs, buffer, sems, extra=()):
     core, quad, _, _ = here()
     count = quads // 2
     rows, half = refs[0].shape
+    column = pl.multiple_of((core if side == 0 else 1 - core) * half, half)
 
     def copies(n):
-        slot = quad ^ (n % quads)
-        column = pl.multiple_of((core if n < quads else 1 - core) * half, half)
+        slot = quad ^ n
         row = pl.multiple_of((slot % count) * rows, rows)
         return slot // count, [
-            pltpu.make_async_copy(buffer.at[n], out.at[pl.ds(row, rows), pl.ds(column, half)], sems.at[n])
-            for out in outs[:2]
+            pltpu.make_async_copy(buffer.at[n], out.at[pl.ds(row, rows), pl.ds(column, half)], sems.at[n]) for out in outs
         ]
 
-    last = pltpu.make_async_copy(rows_ref, outs[2], sems.at[2 * quads])
-    last.start()
+    for copy in extra:
+        copy.start()
     for n, ref in enumerate(refs):
         which, pair = copies(n)
         buffer[n] = ref[...].astype(F32) * jnp.where(which == 0, scales[0], scales[1])
         for k in range(2):
             pl.when(which == k)(pair[k].start)
-    for n in range(2 * quads):
+    for n in range(quads):
         which, pair = copies(n)
         for k in range(2):
             pl.when(which == k)(pair[k].wait)
-    last.wait()
+    for copy in extra:
+        copy.wait()
+
+
+def write_own(quads, scales, *refs):
+    write_columns(quads, scales, 0, refs[:quads], refs[quads : quads + 2], *refs[quads + 2 :])
+
+
+def finish(quads, scales, rows_ref, *refs):
+    pieces, outs, (buffer, sems) = refs[:quads], refs[quads + 2 : quads + 5], refs[quads + 5 :]
+    last = pltpu.make_async_copy(rows_ref, outs[2], sems.at[quads])
+    write_columns(quads, scales, 1, pieces, outs[:2], buffer, sems, (last,))
 
 
 def local(row_devices, blk_devices, source_table, target_table, message_weight, self_weight, tile_lists, key_offsets, list_lengths, cotangent):
@@ -364,17 +373,23 @@
 
     their_pieces = {m: swap(value, 1, devices) for m, value in pieces.items()}
     scales = ((targets * devices) ** (-0.5), (block_rows * blk_devices) ** (-0.5))
+    written = call(
+        functools.partial(write_own, quads, scales),
+        "write_own",
+        (shaped((width, width), F32),) * 2,
+        inputs=quads,
+        out_specs=(HBM, HBM),
+        scratch_shapes=[pltpu.VMEM((quads, piece, half), F32), pltpu.SemaphoreType.DMA((quads,))],
+    )(*[pieces[m] for m in range(quads)])
     self_gradient, message_gradient, source_gradient = call(
         functools.partial(finish, quads, scales),
         "finish",
         (shaped((width, width), F32),) * 2 + (shaped((share, width), BF16),),
-        inputs=1 + 2 * quads,
+        in_specs=[VMEM] * (1 + quads) + [HBM] * 2,
         out_specs=(HBM, HBM, HBM),
-        scratch_shapes=[
-            pltpu.VMEM((2 * quads, piece, half), F32),
-            pltpu.SemaphoreType.DMA((2 * quads + 1,)),
-        ],
-    )(source_rows, *[values[m] for values in (pieces, their_pieces) for m in range(quads)])
+        input_output_aliases={1 + quads: 0, 2 + quads: 1},
+        scratch_shapes=[pltpu.VMEM((quads, piece, half), F32), pltpu.SemaphoreType.DMA((quads + 1,))],
+    )(source_rows, *[their_pieces[m] for m in range(quads)], *written)
     return (updated, target_gradient, source_gradient, self_gradient, message_gradient)
 
 

time: 57.3 us -> 57.1 us (level)
  waiting for transfers between devices: 16.6 us -> 15.7 us
  Pallas kernels: 9.44 us -> 10.1 us
    pallas_call x0 -> x1, Pallas kernels: none -> 1.03 us  [local(): call(functools.partial(write_own, quads, scales), 'write_own', (shaped((w...]
    ppermute x27, waiting for transfers between devices: 16.6 us -> 15.7 us  [swap(): return lax.ppermute(value, AXES, [(i, i ^ mask) for i in range(devices)])]
  transfers between devices with their start and end apart: 27 -> 27, of which waited for: 11 -> 10; matrix products, arithmetic and copies ran while one was open for 3% -> 3% of each run, Pallas kernels for 10% -> 12%
where the time goes in v6:
time: 57.1 us; the launch traced here: 56.8 us
  starting transfers between devices  24.8 us (43%)
  waiting for transfers between devices  15.7 us (27%)
  Pallas kernels  10.1 us (18%)
  local copies, waits for them, and re-layouts  3.15 us (6%)
  between operations  1.5 us (3%)
  other arithmetic  1.47 us (3%)
    ppermute x27, starting transfers between devices, swap(): return lax.ppermute(value, AXES, [(i, i ^ mask) for i in range(devices)])  24.8 us
    ppermute x27, waiting for transfers between devices, swap(): return lax.ppermute(value, AXES, [(i, i ^ mask) for i in range(devices)])  15.7 us
    unnamed x14, local copies, waits for them, and re-layouts  3.14 us
    pallas_call x1, Pallas kernels, local(): call(target_side, 'target_side', (shaped((targets, width), BF16),) * 2, i...  1.4 us
    pallas_call x1, Pallas kernels, local(): call(functools.partial(gather_more, order), 'gather_more', (shaped((targe...  1.39 us
    pallas_call x1, Pallas kernels, local(): call(functools.partial(forward, order), 'forward', (shaped((2 * targets,...  1.38 us
    pallas_call x1, Pallas kernels, local(): call(functools.partial(source_terms, share, sides, orders), 'source_terms...  1.34 us
  transfers between devices with their start and end apart: 27, of which 10 were waited for; matrix products, arithmetic and copies ran while one was open for 3% of the time, Pallas kernels for 12%

profile of v6, /device:TPU:0, one launch (start us, length us, event | category | flops | bytes accessed | tf_op | source)
XLA Modules:
  0.0 56.8 jit_solution(5240713170365764213)
XLA Ops:
  0.6 3.0 %collective-permute-start.1 = (bf16[512,512]{1,0:T(8,128)(2,1)}, bf16[512,512]{1,0:T(8,128)(2,1)S(1)}, u32[]{:S(2)}, u32[]{:S(2)}) collective-permute-start(bf16[512,512]{1,0:T(8,128)(2,1)} %s_ref.1), channel_id=1, source_target_pairs={{0,2},{1,3},{2,0},{3,1},{4,6},{5,7},{6,4},{7,5},{8,10},{9,11},{10,... | collective-permute-start | bytes 1572872 | tf_op jit(solution)/shard_map/ppermute | solution.py:20
  4.3 0.7 %fusion = pred[4,4]{1,0:T(4,128)(4,1)S(1)} fusion(s32[4]{0:T(128)} %bitcast.6, pred[4]{0:T(512)(128)(4,1)S(1)} %iota_compare_fusion.1), kind=kLoop, calls=%fused_computation.2 | loop fusion | flops 32 | bytes 36 | tf_op jit(solution)/shard_map/and | solution.py:248
  5.0 0.8 %select_reduce_fusion = s32[4,512]{1,0:T(4,128)S(1)} fusion(s32[4,512]{1,0:T(4,128)} %bitcast.5, pred[4,4]{1,0:T(4,128)(4,1)S(1)} %fusion), kind=kLoop, calls=%fused_computation | loop fusion | flops 14336 | bytes 16400 | tf_op jit(solution)/shard_map/reduce_max | solution.py:249
  7.1 1.0 %copy-done = bf16[512,512]{1,0:T(8,128)(2,1)S(1)} copy-done((bf16[512,512]{1,0:T(8,128)(2,1)S(1)}, bf16[512,512]{1,0:T(8,128)(2,1)}, u32[]{:S(2)}) %copy-start) | copy-done | bytes 524312
  8.1 1.0 %copy-done.2 = bf16[512,512]{1,0:T(8,128)(2,1)S(1)} copy-done((bf16[512,512]{1,0:T(8,128)(2,1)S(1)}, bf16[512,512]{1,0:T(8,128)(2,1)}, u32[]{:S(2)}) %copy-start.2) | copy-done | bytes 524312
  9.1 1.0 %copy-done.6 = bf16[512,512]{1,0:T(8,128)(2,1)S(1)} copy-done((bf16[512,512]{1,0:T(8,128)(2,1)S(1)}, bf16[512,512]{1,0:T(8,128)(2,1)}, u32[]{:S(2)}) %copy-start.6) | copy-done | bytes 524312
  10.2 1.1 %gather_first.1 = (s32[1024,4]{1,0:T(8,128)S(1)}, f32[512,256]{1,0:T(8,128)S(1)}, f32[1024,512]{1,0:T(8,128)S(1)}, bf16[512,256]{1,0:T(8,128)(2,1)S(1)}) custom-call(s32[8,512]{1,0:T(8,128)S(1)} %concatenate.3.links0_ref, s32[8,512]{1,0:T(8,128)S(1)} %collective-permute-done.links1_ref, bf16[512,512]{1,0:T(8,128)(2,1)S(1)} %copy-done.6, ...), custom_call_target="tpu_custom_call" | custom-call | tf_op jit(solution)/shard_map/gather_first/pallas_call | solution.py:258
  11.3 4.5 %collective-permute-done.1.refs_1_ = bf16[512,512]{1,0:T(8,128)(2,1)S(1)} collective-permute-done((bf16[512,512]{1,0:T(8,128)(2,1)}, bf16[512,512]{1,0:T(8,128)(2,1)S(1)}, u32[]{:S(2)}, u32[]{:S(2)}) %collective-permute-start.1) | collective-permute-done | bytes 524320 | tf_op jit(solution)/shard_map/ppermute | solution.py:20
  15.8 1.4 %gather_more.1 = (f32[512,256]{1,0:T(8,128)S(1)}, f32[1024,512]{1,0:T(8,128)S(1)}) custom-call(s32[1024,4]{1,0:T(8,128)S(1)} %get-tuple-element.56.columns_ref, f32[1024,512]{1,0:T(8,128)S(1)} %get-tuple-element.57.h0_ref, bf16[512,512]{1,0:T(8,128)(2,1)S(1)} %collective-permute-done.2.t_ref.t1_ref, bf16[512,256]{1,0:T(8,128)(2,1)S(1)} %get-tuple-element.58.weight_ref, ...), custom_call_target="tpu_custom_call" | custom-call | tf_op jit(solution)/shard_map/gather_more/pallas_call | solution.py:277
  17.7 1.4 %forward.1 = (bf16[1024,512]{1,0:T(8,128)(2,1)S(1)}, bf16[1024,256]{1,0:T(8,128)(2,1)S(1)}, bf16[512,256]{1,0:T(8,128)(2,1)S(1)}, bf16[512,256]{1,0:T(8,128)(2,1)S(1)}) custom-call(s32[8,512]{1,0:T(8,128)S(1)} %concatenate.3.links0_ref, s32[8,512]{1,0:T(8,128)S(1)} %collective-permute-done.links1_ref, s32[1024,4]{1,0:T(8,128)S(1)} %get-tuple-element.56.columns_ref, ...), custom_call_target="tpu_custom_call" | custom-call | tf_op jit(solution)/shard_map/forward/pallas_call | solution.py:285
  19.1 0.8 %weight_terms.1 = (f32[256,256]{1,0:T(8,128)S(1)}, bf16[256,256]{1,0:T(8,128)(2,1)S(1)}, bf16[256,256]{1,0:T(8,128)(2,1)S(1)}, bf16[256,256]{1,0:T(8,128)(2,1)S(1)}) custom-call(bf16[512,512]{1,0:T(8,128)(2,1)S(1)} %copy-done.1, bf16[512,512]{1,0:T(8,128)(2,1)S(1)} %collective-permute-done.2.t_ref.t1_ref, bf16[1024,512]{1,0:T(8,128)(2,1)S(1)} %get-tuple-element.64.h_ref, ...), custom_call_target="tpu_custom_call" | custom-call | tf_op jit(solution)/shard_map/weight_terms/pallas_call | solution.py:297
  20.5 2.7 %collective-permute-start.7 = (bf16[256,256]{1,0:T(8,128)(2,1)S(1)}, bf16[256,256]{1,0:T(8,128)(2,1)S(1)}, u32[]{:S(2)}, u32[]{:S(2)}) collective-permute-start(bf16[256,256]{1,0:T(8,128)(2,1)S(1)} %get-tuple-element.68), channel_id=1, source_target_pairs={{0,6},{1,7},{2,4},{3,5},{4,2},{5,3},{6,0},{7,1},{8,14},{9,15},{10,... | collective-permute-start | bytes 393224 | tf_op jit(solution)/shard_map/ppermute | solution.py:20
  24.0 1.3 %source_terms.1 = (f32[256,512]{1,0:T(8,128)S(1)}, bf16[256,512]{1,0:T(8,128)(2,1)S(1)}, f32[256,512]{1,0:T(8,128)S(1)}, bf16[256,512]{1,0:T(8,128)(2,1)S(1)}) custom-call(s32[8,512]{1,0:T(8,128)S(1)} %concatenate.3.links0_ref, s32[8,512]{1,0:T(8,128)S(1)} %collective-permute-done.links1_ref, bf16[1024,256]{1,0:T(8,128)(2,1)S(1)} %get-tuple-element.71.grad_ref, ...), custom_call_target="tpu_custom_call" | custom-call | tf_op jit(solution)/shard_map/source_terms/pallas_call | solution.py:316
  25.4 1.8 %collective-permute-start.13 = (bf16[256,512]{1,0:T(8,128)(2,1)S(1)}, bf16[256,512]{1,0:T(8,128)(2,1)S(1)}, u32[]{:S(2)}, u32[]{:S(2)}) collective-permute-start(bf16[256,512]{1,0:T(8,128)(2,1)S(1)} %get-tuple-element.76), channel_id=1, source_target_pairs={{0,4},{1,5},{2,6},{3,7},{4,0},{5,1},{6,2},{7,3},{8,12},{9,13},{10,... | collective-permute-start | bytes 786440 | tf_op jit(solution)/shard_map/ppermute | solution.py:20
  27.1 1.5 %collective-permute-start.11 = (bf16[256,512]{1,0:T(8,128)(2,1)S(1)}, bf16[256,512]{1,0:T(8,128)(2,1)S(1)}, u32[]{:S(2)}, u32[]{:S(2)}) collective-permute-start(bf16[256,512]{1,0:T(8,128)(2,1)S(1)} %get-tuple-element.74), channel_id=1, source_target_pairs={{0,2},{1,3},{2,0},{3,1},{4,6},{5,7},{6,4},{7,5},{8,10},{9,11},{10,... | collective-permute-start | bytes 786440 | tf_op jit(solution)/shard_map/ppermute | solution.py:20
  28.7 1.4 %target_side.1 = (bf16[512,512]{1,0:T(8,128)(2,1)}, bf16[512,512]{1,0:T(8,128)(2,1)}) custom-call(bf16[512,512]{1,0:T(8,128)(2,1)S(1)} %copy-done.3, bf16[512,512]{1,0:T(8,128)(2,1)S(1)} %copy-done.4, bf16[1024,256]{1,0:T(8,128)(2,1)S(1)} %get-tuple-element.71.grad_ref, bf16[1024,256]{1,0:T(8,128)(2,1)S(1)} %collective-permute-done.6.other_ref.grad_received_ref, ...), custom_call_target="tpu_custom_call" | custom-call | tf_op jit(solution)/shard_map/target_side/pallas_call | solution.py:323
  30.1 0.8 %collective-permute-done.8.refs_2_ = bf16[256,256]{1,0:T(8,128)(2,1)S(1)} collective-permute-done((bf16[256,256]{1,0:T(8,128)(2,1)S(1)}, bf16[256,256]{1,0:T(8,128)(2,1)S(1)}, u32[]{:S(2)}, u32[]{:S(2)}) %collective-permute-start.8) | collective-permute-done | bytes 131104 | tf_op jit(solution)/shard_map/ppermute | solution.py:20
  30.9 1.6 %collective-permute-start.18 = (bf16[256,256]{1,0:T(8,128)(2,1)S(1)}, bf16[256,256]{1,0:T(8,128)(2,1)S(1)}, u32[]{:S(2)}, u32[]{:S(2)}) collective-permute-start(bf16[256,256]{1,0:T(8,128)(2,1)S(1)} %weight_sum.3.refs_0_), channel_id=1, source_target_pairs={{0,8},{1,9},{2,10},{3,11},{4,12},{5,13},{6,14},{7,15},{8,0},{9,1},... | collective-permute-start | bytes 393224 | tf_op jit(solution)/shard_map/ppermute | solution.py:20
  32.6 3.2 %collective-permute-done.13.received_ref = bf16[256,512]{1,0:T(8,128)(2,1)S(1)} collective-permute-done((bf16[256,512]{1,0:T(8,128)(2,1)S(1)}, bf16[256,512]{1,0:T(8,128)(2,1)S(1)}, u32[]{:S(2)}, u32[]{:S(2)}) %collective-permute-start.13) | collective-permute-done | bytes 262176 | tf_op jit(solution)/shard_map/ppermute | solution.py:20
  36.2 2.8 %collective-permute-start.19 = (bf16[256,256]{1,0:T(8,128)(2,1)S(1)}, bf16[256,256]{1,0:T(8,128)(2,1)S(1)}, u32[]{:S(2)}, u32[]{:S(2)}) collective-permute-start(bf16[256,256]{1,0:T(8,128)(2,1)S(1)} %weight_sum.4.refs_0_), channel_id=1, source_target_pairs={{0,16},{1,17},{2,18},{3,19},{4,20},{5,21},{6,22},{7,23},{8,24},{9,... | collective-permute-start | bytes 393224 | tf_op jit(solution)/shard_map/ppermute | solution.py:20
  39.1 1.6 %collective-permute-start.12 = (bf16[128,512]{1,0:T(8,128)(2,1)S(1)}, bf16[128,512]{1,0:T(8,128)(2,1)S(1)}, u32[]{:S(2)}, u32[]{:S(2)}) collective-permute-start(bf16[128,512]{1,0:T(8,128)(2,1)S(1)} %get-tuple-element.84), channel_id=1, source_target_pairs={{0,4},{1,5},{2,6},{3,7},{4,0},{5,1},{6,2},{7,3},{8,12},{9,13},{10,... | collective-permute-start | bytes 393224 | tf_op jit(solution)/shard_map/ppermute | solution.py:20
  40.9 1.6 %collective-permute-start.15 = (bf16[128,512]{1,0:T(8,128)(2,1)S(1)}, bf16[128,512]{1,0:T(8,128)(2,1)S(1)}, u32[]{:S(2)}, u32[]{:S(2)}) collective-permute-start(bf16[128,512]{1,0:T(8,128)(2,1)S(1)} %source_sum.9), channel_id=1, source_target_pairs={{0,8},{1,9},{2,10},{3,11},{4,12},{5,13},{6,14},{7,15},{8,0},{9,1},... | collective-permute-start | bytes 393224 | tf_op jit(solution)/shard_map/ppermute | solution.py:20
  42.5 2.1 %collective-permute-done.19.refs_1_ = bf16[256,256]{1,0:T(8,128)(2,1)S(1)} collective-permute-done((bf16[256,256]{1,0:T(8,128)(2,1)S(1)}, bf16[256,256]{1,0:T(8,128)(2,1)S(1)}, u32[]{:S(2)}, u32[]{:S(2)}) %collective-permute-start.19) | collective-permute-done | bytes 131104 | tf_op jit(solution)/shard_map/ppermute | solution.py:20
  44.6 1.7 %collective-permute-start.21 = (bf16[256,256]{1,0:T(8,128)(2,1)S(1)}, bf16[256,256]{1,0:T(8,128)(2,1)S(1)}, u32[]{:S(2)}, u32[]{:S(2)}) collective-permute-start(bf16[256,256]{1,0:T(8,128)(2,1)S(1)} %weight_sum.5.refs_0_), channel_id=1, source_target_pairs={{0,2},{1,3},{2,0},{3,1},{4,6},{5,7},{6,4},{7,5},{8,10},{9,11},{10,... | collective-permute-start | bytes 393224 | tf_op jit(solution)/shard_map/ppermute | solution.py:20
  46.3 1.5 %collective-permute-start.23 = (bf16[256,256]{1,0:T(8,128)(2,1)S(1)}, bf16[256,256]{1,0:T(8,128)(2,1)S(1)}, u32[]{:S(2)}, u32[]{:S(2)}) collective-permute-start(bf16[256,256]{1,0:T(8,128)(2,1)S(1)} %weight_sum.5.refs_0_), channel_id=1, source_target_pairs={{0,4},{1,5},{2,6},{3,7},{4,0},{5,1},{6,2},{7,3},{8,12},{9,13},{10,... | collective-permute-start | bytes 393224 | tf_op jit(solution)/shard_map/ppermute | solution.py:20
  48.3 1.2 %collective-permute-start.16 = (bf16[64,512]{1,0:T(8,128)(2,1)S(1)}, bf16[64,512]{1,0:T(8,128)(2,1)S(1)}, u32[]{:S(2)}, u32[]{:S(2)}) collective-permute-start(bf16[64,512]{1,0:T(8,128)(2,1)S(1)} %get-tuple-element.88), channel_id=1, source_target_pairs={{0,16},{1,17},{2,18},{3,19},{4,20},{5,21},{6,22},{7,23},{8,24},{9,... | collective-permute-start | bytes 196616 | tf_op jit(solution)/shard_map/ppermute | solution.py:20
  49.5 1.2 %collective-permute-done.21.refs_1_ = bf16[256,256]{1,0:T(8,128)(2,1)S(1)} collective-permute-done((bf16[256,256]{1,0:T(8,128)(2,1)S(1)}, bf16[256,256]{1,0:T(8,128)(2,1)S(1)}, u32[]{:S(2)}, u32[]{:S(2)}) %collective-permute-start.21) | collective-permute-done | bytes 131104 | tf_op jit(solution)/shard_map/ppermute | solution.py:20
  50.7 0.8 %collective-permute-done.23.refs_2_ = bf16[256,256]{1,0:T(8,128)(2,1)S(1)} collective-permute-done((bf16[256,256]{1,0:T(8,128)(2,1)S(1)}, bf16[256,256]{1,0:T(8,128)(2,1)S(1)}, u32[]{:S(2)}, u32[]{:S(2)}) %collective-permute-start.23) | collective-permute-done | bytes 131104 | tf_op jit(solution)/shard_map/ppermute | solution.py:20
  51.5 2.2 %collective-permute-done.25.refs_3_ = bf16[256,256]{1,0:T(8,128)(2,1)S(1)} collective-permute-done((bf16[256,256]{1,0:T(8,128)(2,1)S(1)}, bf16[256,256]{1,0:T(8,128)(2,1)S(1)}, u32[]{:S(2)}, u32[]{:S(2)}) %collective-permute-start.25) | collective-permute-done | bytes 131104 | tf_op jit(solution)/shard_map/ppermute | solution.py:20
  53.8 0.6 %collective-permute-start.17 = (bf16[64,512]{1,0:T(8,128)(2,1)S(1)}, bf16[64,512]{1,0:T(8,128)(2,1)S(1)}, u32[]{:S(2)}, u32[]{:S(2)}) collective-permute-start(bf16[64,512]{1,0:T(8,128)(2,1)S(1)} %source_sum.11), channel_id=1, source_target_pairs={{0,1},{1,0},{2,3},{3,2},{4,5},{5,4},{6,7},{7,6},{8,9},{9,8},{10,11... | collective-permute-start | bytes 196616 | tf_op jit(solution)/shard_map/ppermute | solution.py:20
  54.3 1.0 %write_own.1 = (f32[512,512]{1,0:T(8,128)}, f32[512,512]{1,0:T(8,128)}) custom-call(bf16[256,256]{1,0:T(8,128)(2,1)S(1)} %weight_sum.5.refs_0_, bf16[256,256]{1,0:T(8,128)(2,1)S(1)} %collective-permute-done.21.refs_1_, bf16[256,256]{1,0:T(8,128)(2,1)S(1)} %collective-permute-done.23.refs_2_, bf16[256,256]{1,0:T(8,128)(2,1)S(1)} %collective-permute-done.25.refs_3_), custom_call_target="tpu_custom_call" | custom-call | tf_op jit(solution)/shard_map/write_own/pallas_call | solution.py:376
  55.7 1.1 %finish.1 = (f32[512,512]{1,0:T(8,128)}, f32[512,512]{1,0:T(8,128)}, bf16[64,512]{1,0:T(8,128)(2,1)}) custom-call(bf16[64,512]{1,0:T(8,128)(2,1)S(1)} %project_back.1.rows_ref, bf16[256,256]{1,0:T(8,128)(2,1)S(1)} %collective-permute-done.20.refs_0_, ...), custom_call_target="tpu_custom_call", output_to_operand_aliasing={{0}: (5, {}), {1}: (6, {})} | custom-call | tf_op jit(solution)/shard_map/finish/pallas_call | solution.py:384
  (58 shorter events, 4.6 us)
Async XLA Ops:
  0.6 15.2 %collective-permute-start.1 = (bf16[512,512]{1,0:T(8,128)(2,1)}, bf16[512,512]{1,0:T(8,128)(2,1)S(1)}, u32[]{:S(2)}, u32[]{:S(2)}) collective-permute-start(bf16[512,512]{1,0:T(8,128)(2,1)} %s_ref.1), channel_id=1, source_target_pairs={{0,2},{1,3},{2,0},{3,1},{4,6},{5,7},{6,4},{7,5},{8,10},{9,11},{10,... | collective-permute-start | bytes 1572872 | tf_op jit(solution)/shard_map/ppermute | solution.py:20
  5.8 1.2 %collective-permute-start = (s32[8,512]{1,0:T(8,128)S(1)}, s32[8,512]{1,0:T(8,128)S(1)}, u32[]{:S(2)}, u32[]{:S(2)}) collective-permute-start(s32[8,512]{1,0:T(8,128)S(1)} %concatenate.3.links0_ref), channel_id=1, source_target_pairs={{0,1},{1,0},{2,3},{3,2},{4,5},{5,4},{6,7},{7,6},{8,9},{9,8},{10,11... | collective-permute-start | bytes 49160 | tf_op jit(solution)/shard_map/ppermute | solution.py:20
  5.9 9.9 %collective-permute-start.3 = (bf16[512,512]{1,0:T(8,128)(2,1)}, bf16[512,512]{1,0:T(8,128)(2,1)S(1)}, u32[]{:S(2)}, u32[]{:S(2)}) collective-permute-start(bf16[512,512]{1,0:T(8,128)(2,1)} %s_ref.1), channel_id=1, source_target_pairs={{0,1},{1,0},{2,3},{3,2},{4,5},{5,4},{6,7},{7,6},{8,9},{9,8},{10,11... | collective-permute-start | bytes 1572872 | tf_op jit(solution)/shard_map/ppermute | solution.py:20
  6.4 9.4 %collective-permute-start.2 = (bf16[512,512]{1,0:T(8,128)(2,1)}, bf16[512,512]{1,0:T(8,128)(2,1)S(1)}, u32[]{:S(2)}, u32[]{:S(2)}) collective-permute-start(bf16[512,512]{1,0:T(8,128)(2,1)} %t0_ref.3), channel_id=1, source_target_pairs={{0,1},{1,0},{2,3},{3,2},{4,5},{5,4},{6,7},{7,6},{8,9},{9,8},{10,11... | collective-permute-start | bytes 1572872 | tf_op jit(solution)/shard_map/ppermute | solution.py:20
  6.5 10.8 %collective-permute-start.4 = (bf16[512,512]{1,0:T(8,128)(2,1)}, bf16[512,512]{1,0:T(8,128)(2,1)S(1)}, u32[]{:S(2)}, u32[]{:S(2)}) collective-permute-start(bf16[512,512]{1,0:T(8,128)(2,1)} %cot_ref.1), channel_id=1, source_target_pairs={{0,1},{1,0},{2,3},{3,2},{4,5},{5,4},{6,7},{7,6},{8,9},{9,8},{10,11... | collective-permute-start | bytes 1572872 | tf_op jit(solution)/shard_map/ppermute | solution.py:20
  7.1 1.0 %copy-start = (bf16[512,512]{1,0:T(8,128)(2,1)S(1)}, bf16[512,512]{1,0:T(8,128)(2,1)}, u32[]{:S(2)}) copy-start(bf16[512,512]{1,0:T(8,128)(2,1)} %t0_ref.3) | copy-start | bytes 1572868
  15.8 1.9 %copy-start.1 = (bf16[512,512]{1,0:T(8,128)(2,1)S(1)}, bf16[512,512]{1,0:T(8,128)(2,1)}, u32[]{:S(2)}) copy-start(bf16[512,512]{1,0:T(8,128)(2,1)} %t0_ref.3) | copy-start | bytes 1572868
  15.8 1.9 %copy-start.4 = (bf16[512,512]{1,0:T(8,128)(2,1)S(1)}, bf16[512,512]{1,0:T(8,128)(2,1)}, u32[]{:S(2)}) copy-start(bf16[512,512]{1,0:T(8,128)(2,1)} %cot_ref.1) | copy-start | bytes 1572868
  15.8 1.9 %copy-start.5 = (bf16[512,512]{1,0:T(8,128)(2,1)S(1)}, bf16[512,512]{1,0:T(8,128)(2,1)}, u32[]{:S(2)}) copy-start(bf16[512,512]{1,0:T(8,128)(2,1)} %wm_ref.3) | copy-start | bytes 1572868
  15.8 1.9 %collective-permute-start.5 = (bf16[512,512]{1,0:T(8,128)(2,1)S(1)}, bf16[512,512]{1,0:T(8,128)(2,1)S(1)}, u32[]{:S(2)}, u32[]{:S(2)}) collective-permute-start(bf16[512,512]{1,0:T(8,128)(2,1)S(1)} %collective-permute-done.1.refs_1_), channel_id=1, source_target_pairs={{0,1},{1,0},{2,3},{3,2},{4,5},{5,4},{6,7},{7,6},{8,9},{9,8},{10,11... | collective-permute-start | bytes 1572872 | tf_op jit(solution)/shard_map/ppermute | solution.py:20
  19.1 9.5 %copy-start.3 = (bf16[512,512]{1,0:T(8,128)(2,1)S(1)}, bf16[512,512]{1,0:T(8,128)(2,1)}, u32[]{:S(2)}) copy-start(bf16[512,512]{1,0:T(8,128)(2,1)} %ws_ref.3) | copy-start | bytes 1572868
  19.9 4.1 %collective-permute-start.6 = (bf16[1024,256]{1,0:T(8,128)(2,1)S(1)}, bf16[1024,256]{1,0:T(8,128)(2,1)S(1)}, u32[]{:S(2)}, u32[]{:S(2)}) collective-permute-start(bf16[1024,256]{1,0:T(8,128)(2,1)S(1)} %get-tuple-element.71.grad_ref), channel_id=1, source_target_pairs={{0,1},{1,0},{2,3},{3,2},{4,5},{5,4},{6,7},{7,6},{8,9},{9,8},{10,11... | collective-permute-start | bytes 1572872 | tf_op jit(solution)/shard_map/ppermute | solution.py:20
  20.2 6.9 %collective-permute-start.10 = (bf16[512,256]{1,0:T(8,128)(2,1)S(1)}, bf16[512,256]{1,0:T(8,128)(2,1)S(1)}, u32[]{:S(2)}, u32[]{:S(2)}) collective-permute-start(bf16[512,256]{1,0:T(8,128)(2,1)S(1)} %get-tuple-element.78), channel_id=1, source_target_pairs={{0,1},{1,0},{2,3},{3,2},{4,5},{5,4},{6,7},{7,6},{8,9},{9,8},{10,11... | collective-permute-start | bytes 786440 | tf_op jit(solution)/shard_map/ppermute | solution.py:20
  20.5 9.5 %collective-permute-start.7 = (bf16[256,256]{1,0:T(8,128)(2,1)S(1)}, bf16[256,256]{1,0:T(8,128)(2,1)S(1)}, u32[]{:S(2)}, u32[]{:S(2)}) collective-permute-start(bf16[256,256]{1,0:T(8,128)(2,1)S(1)} %get-tuple-element.68), channel_id=1, source_target_pairs={{0,6},{1,7},{2,4},{3,5},{4,2},{5,3},{6,0},{7,1},{8,14},{9,15},{10,... | collective-permute-start | bytes 393224 | tf_op jit(solution)/shard_map/ppermute | solution.py:20
  23.2 7.7 %collective-permute-start.8 = (bf16[256,256]{1,0:T(8,128)(2,1)S(1)}, bf16[256,256]{1,0:T(8,128)(2,1)S(1)}, u32[]{:S(2)}, u32[]{:S(2)}) collective-permute-start(bf16[256,256]{1,0:T(8,128)(2,1)S(1)} %get-tuple-element.67), channel_id=1, source_target_pairs={{0,4},{1,5},{2,6},{3,7},{4,0},{5,1},{6,2},{7,3},{8,12},{9,13},{10,... | collective-permute-start | bytes 393224 | tf_op jit(solution)/shard_map/ppermute | solution.py:20
  23.7 7.2 %collective-permute-start.9 = (bf16[256,256]{1,0:T(8,128)(2,1)S(1)}, bf16[256,256]{1,0:T(8,128)(2,1)S(1)}, u32[]{:S(2)}, u32[]{:S(2)}) collective-permute-start(bf16[256,256]{1,0:T(8,128)(2,1)S(1)} %get-tuple-element.66), channel_id=1, source_target_pairs={{0,2},{1,3},{2,0},{3,1},{4,6},{5,7},{6,4},{7,5},{8,10},{9,11},{10,... | collective-permute-start | bytes 393224 | tf_op jit(solution)/shard_map/ppermute | solution.py:20
  25.4 10.4 %collective-permute-start.13 = (bf16[256,512]{1,0:T(8,128)(2,1)S(1)}, bf16[256,512]{1,0:T(8,128)(2,1)S(1)}, u32[]{:S(2)}, u32[]{:S(2)}) collective-permute-start(bf16[256,512]{1,0:T(8,128)(2,1)S(1)} %get-tuple-element.76), channel_id=1, source_target_pairs={{0,4},{1,5},{2,6},{3,7},{4,0},{5,1},{6,2},{7,3},{8,12},{9,13},{10,... | collective-permute-start | bytes 786440 | tf_op jit(solution)/shard_map/ppermute | solution.py:20
  27.1 11.9 %collective-permute-start.11 = (bf16[256,512]{1,0:T(8,128)(2,1)S(1)}, bf16[256,512]{1,0:T(8,128)(2,1)S(1)}, u32[]{:S(2)}, u32[]{:S(2)}) collective-permute-start(bf16[256,512]{1,0:T(8,128)(2,1)S(1)} %get-tuple-element.74), channel_id=1, source_target_pairs={{0,2},{1,3},{2,0},{3,1},{4,6},{5,7},{6,4},{7,5},{8,10},{9,11},{10,... | collective-permute-start | bytes 786440 | tf_op jit(solution)/shard_map/ppermute | solution.py:20
  30.9 5.2 %collective-permute-start.18 = (bf16[256,256]{1,0:T(8,128)(2,1)S(1)}, bf16[256,256]{1,0:T(8,128)(2,1)S(1)}, u32[]{:S(2)}, u32[]{:S(2)}) collective-permute-start(bf16[256,256]{1,0:T(8,128)(2,1)S(1)} %weight_sum.3.refs_0_), channel_id=1, source_target_pairs={{0,8},{1,9},{2,10},{3,11},{4,12},{5,13},{6,14},{7,15},{8,0},{9,1},... | collective-permute-start | bytes 393224 | tf_op jit(solution)/shard_map/ppermute | solution.py:20
  35.8 5.0 %collective-permute-start.14 = (bf16[128,512]{1,0:T(8,128)(2,1)S(1)}, bf16[128,512]{1,0:T(8,128)(2,1)S(1)}, u32[]{:S(2)}, u32[]{:S(2)}) collective-permute-start(bf16[128,512]{1,0:T(8,128)(2,1)S(1)} %get-tuple-element.86), channel_id=1, source_target_pairs={{0,2},{1,3},{2,0},{3,1},{4,6},{5,7},{6,4},{7,5},{8,10},{9,11},{10,... | collective-permute-start | bytes 393224 | tf_op jit(solution)/shard_map/ppermute | solution.py:20
  36.2 8.4 %collective-permute-start.19 = (bf16[256,256]{1,0:T(8,128)(2,1)S(1)}, bf16[256,256]{1,0:T(8,128)(2,1)S(1)}, u32[]{:S(2)}, u32[]{:S(2)}) collective-permute-start(bf16[256,256]{1,0:T(8,128)(2,1)S(1)} %weight_sum.4.refs_0_), channel_id=1, source_target_pairs={{0,16},{1,17},{2,18},{3,19},{4,20},{5,21},{6,22},{7,23},{8,24},{9,... | collective-permute-start | bytes 393224 | tf_op jit(solution)/shard_map/ppermute | solution.py:20
  39.1 9.1 %collective-permute-start.12 = (bf16[128,512]{1,0:T(8,128)(2,1)S(1)}, bf16[128,512]{1,0:T(8,128)(2,1)S(1)}, u32[]{:S(2)}, u32[]{:S(2)}) collective-permute-start(bf16[128,512]{1,0:T(8,128)(2,1)S(1)} %get-tuple-element.84), channel_id=1, source_target_pairs={{0,4},{1,5},{2,6},{3,7},{4,0},{5,1},{6,2},{7,3},{8,12},{9,13},{10,... | collective-permute-start | bytes 393224 | tf_op jit(solution)/shard_map/ppermute | solution.py:20
  40.9 7.4 %collective-permute-start.15 = (bf16[128,512]{1,0:T(8,128)(2,1)S(1)}, bf16[128,512]{1,0:T(8,128)(2,1)S(1)}, u32[]{:S(2)}, u32[]{:S(2)}) collective-permute-start(bf16[128,512]{1,0:T(8,128)(2,1)S(1)} %source_sum.9), channel_id=1, source_target_pairs={{0,8},{1,9},{2,10},{3,11},{4,12},{5,13},{6,14},{7,15},{8,0},{9,1},... | collective-permute-start | bytes 393224 | tf_op jit(solution)/shard_map/ppermute | solution.py:20
  44.6 6.1 %collective-permute-start.21 = (bf16[256,256]{1,0:T(8,128)(2,1)S(1)}, bf16[256,256]{1,0:T(8,128)(2,1)S(1)}, u32[]{:S(2)}, u32[]{:S(2)}) collective-permute-start(bf16[256,256]{1,0:T(8,128)(2,1)S(1)} %weight_sum.5.refs_0_), channel_id=1, source_target_pairs={{0,2},{1,3},{2,0},{3,1},{4,6},{5,7},{6,4},{7,5},{8,10},{9,11},{10,... | collective-permute-start | bytes 393224 | tf_op jit(solution)/shard_map/ppermute | solution.py:20
  46.3 5.2 %collective-permute-start.23 = (bf16[256,256]{1,0:T(8,128)(2,1)S(1)}, bf16[256,256]{1,0:T(8,128)(2,1)S(1)}, u32[]{:S(2)}, u32[]{:S(2)}) collective-permute-start(bf16[256,256]{1,0:T(8,128)(2,1)S(1)} %weight_sum.5.refs_0_), channel_id=1, source_target_pairs={{0,4},{1,5},{2,6},{3,7},{4,0},{5,1},{6,2},{7,3},{8,12},{9,13},{10,... | collective-permute-start | bytes 393224 | tf_op jit(solution)/shard_map/ppermute | solution.py:20
  47.9 5.9 %collective-permute-start.25 = (bf16[256,256]{1,0:T(8,128)(2,1)S(1)}, bf16[256,256]{1,0:T(8,128)(2,1)S(1)}, u32[]{:S(2)}, u32[]{:S(2)}) collective-permute-start(bf16[256,256]{1,0:T(8,128)(2,1)S(1)} %weight_sum.5.refs_0_), channel_id=1, source_target_pairs={{0,6},{1,7},{2,4},{3,5},{4,2},{5,3},{6,0},{7,1},{8,14},{9,15},{10,... | collective-permute-start | bytes 393224 | tf_op jit(solution)/shard_map/ppermute | solution.py:20
  48.3 5.5 %collective-permute-start.16 = (bf16[64,512]{1,0:T(8,128)(2,1)S(1)}, bf16[64,512]{1,0:T(8,128)(2,1)S(1)}, u32[]{:S(2)}, u32[]{:S(2)}) collective-permute-start(bf16[64,512]{1,0:T(8,128)(2,1)S(1)} %get-tuple-element.88), channel_id=1, source_target_pairs={{0,16},{1,17},{2,18},{3,19},{4,20},{5,21},{6,22},{7,23},{8,24},{9,... | collective-permute-start | bytes 196616 | tf_op jit(solution)/shard_map/ppermute | solution.py:20
  49.5 6.2 %collective-permute-start.20 = (bf16[256,256]{1,0:T(8,128)(2,1)S(1)}, bf16[256,256]{1,0:T(8,128)(2,1)S(1)}, u32[]{:S(2)}, u32[]{:S(2)}) collective-permute-start(bf16[256,256]{1,0:T(8,128)(2,1)S(1)} %weight_sum.5.refs_0_), channel_id=1, source_target_pairs={{0,1},{1,0},{2,3},{3,2},{4,5},{5,4},{6,7},{7,6},{8,9},{9,8},{10,11... | collective-permute-start | bytes 393224 | tf_op jit(solution)/shard_map/ppermute | solution.py:20
  50.7 5.0 %collective-permute-start.22 = (bf16[256,256]{1,0:T(8,128)(2,1)S(1)}, bf16[256,256]{1,0:T(8,128)(2,1)S(1)}, u32[]{:S(2)}, u32[]{:S(2)}) collective-permute-start(bf16[256,256]{1,0:T(8,128)(2,1)S(1)} %collective-permute-done.21.refs_1_), channel_id=1, source_target_pairs={{0,1},{1,0},{2,3},{3,2},{4,5},{5,4},{6,7},{7,6},{8,9},{9,8},{10,11... | collective-permute-start | bytes 393224 | tf_op jit(solution)/shard_map/ppermute | solution.py:20
  51.5 4.2 %collective-permute-start.24 = (bf16[256,256]{1,0:T(8,128)(2,1)S(1)}, bf16[256,256]{1,0:T(8,128)(2,1)S(1)}, u32[]{:S(2)}, u32[]{:S(2)}) collective-permute-start(bf16[256,256]{1,0:T(8,128)(2,1)S(1)} %collective-permute-done.23.refs_2_), channel_id=1, source_target_pairs={{0,1},{1,0},{2,3},{3,2},{4,5},{5,4},{6,7},{7,6},{8,9},{9,8},{10,11... | collective-permute-start | bytes 393224 | tf_op jit(solution)/shard_map/ppermute | solution.py:20
  53.7 2.0 %collective-permute-start.26 = (bf16[256,256]{1,0:T(8,128)(2,1)S(1)}, bf16[256,256]{1,0:T(8,128)(2,1)S(1)}, u32[]{:S(2)}, u32[]{:S(2)}) collective-permute-start(bf16[256,256]{1,0:T(8,128)(2,1)S(1)} %collective-permute-done.25.refs_3_), channel_id=1, source_target_pairs={{0,1},{1,0},{2,3},{3,2},{4,5},{5,4},{6,7},{7,6},{8,9},{9,8},{10,11... | collective-permute-start | bytes 393224 | tf_op jit(solution)/shard_map/ppermute | solution.py:20
  53.8 1.6 %collective-permute-start.17 = (bf16[64,512]{1,0:T(8,128)(2,1)S(1)}, bf16[64,512]{1,0:T(8,128)(2,1)S(1)}, u32[]{:S(2)}, u32[]{:S(2)}) collective-permute-start(bf16[64,512]{1,0:T(8,128)(2,1)S(1)} %source_sum.11), channel_id=1, source_target_pairs={{0,1},{1,0},{2,3},{3,2},{4,5},{5,4},{6,7},{7,6},{8,9},{9,8},{10,11... | collective-permute-start | bytes 196616 | tf_op jit(solution)/shard_map/ppermute | solution.py:20
  (2 other events, 2.1 us)
